TPU v7x, 128 devices: a whole 4x4x4 slice. The times are simulated.
128 devices in a mesh: ctx: 32 (over y_lo, x, z), fsdp: 4 (over y_hi, core).
Axes of the slice: x: 4, y: 4 (y_hi: 2, y_lo: 2; y = y_hi * 2 + y_lo), z: 4, core: 2. Of those that a mesh axis runs over, the one named last changes fastest.
Arguments:
- query_rows: bfloat16 [16384, 4096], P('ctx', 'fsdp'), may hold values from -9 to 9
- key_rows: bfloat16 [16384, 4096], P('ctx', 'fsdp'), may hold values from -6 to 6
- value_rows: bfloat16 [16384, 4096], P('ctx', 'fsdp'), may hold values from -9 to 9
- gate_input: bfloat16 [16384, 4096], P('ctx', 'fsdp'), may hold values from -6 to 6
- norm_gain: float32 [4096], P('fsdp'), may hold values from 0.5 to 1.5
- w_out: bfloat16 [4096, 3072], P(None, 'fsdp'), may hold values from -0.09375 to 0.09375
- mixed_grad: bfloat16 [16384, 3072], P('ctx', 'fsdp'), may hold values from -6 to 6
Outputs:
- mixed: bfloat16 [16384, 3072], P('ctx', 'fsdp')
- w_out_grad: float32 [4096, 3072], P('ctx', 'fsdp')
- query_grad: bfloat16 [16384, 4096], P('ctx', 'fsdp')
- key_grad: bfloat16 [16384, 4096], P('ctx', 'fsdp')
- value_grad: bfloat16 [16384, 4096], P('ctx', 'fsdp')
- gate_grad: bfloat16 [16384, 4096], P('ctx', 'fsdp')
All inputs are finite; a program needn't handle non-finite values.
Results may differ from a plain program's by a relative error of at most 0.005.
Values may be sent and summed in bfloat16 or wider, within the bound.
No kernel may reach another device: no remote copies, remote signals or barrier semaphores. Data moves between devices by JAX's collectives and lax.ppermute only.
A program may use at most 192 MiB of HBM per device.

v0:
```python
import jax
import jax.numpy as jnp
from jax import lax
from jax.sharding import PartitionSpec as P

HD = 128


highest = lax.Precision.HIGHEST


def prefix(part, axis, combine, identity, reverse):
    count = lax.axis_size(axis)
    place = lax.axis_index(axis)
    ahead = count - 1 - place if reverse else place
    gathered = lax.all_gather(part, axis)
    state = jnp.zeros_like(part) + jnp.asarray(identity, part.dtype)

    def one(step, state):
        source = count - 1 - step if reverse else step
        return combine(state, lax.dynamic_index_in_dim(gathered, source, 0, False))

    return lax.fori_loop(0, ahead, one, state)


def causal_mask(length):
    row_index = lax.broadcasted_iota(jnp.int32, (length, length), 0)
    col_index = lax.broadcasted_iota(jnp.int32, (length, length), 1)
    return (col_index <= row_index).astype(jnp.float32)


def add_states(earlier, later):
    return earlier + later


def per_device(query_rows, key_rows, value_rows, gate_input, norm_gain, w_out, mixed_grad):
    length = query_rows.shape[0]
    inner_dev = query_rows.shape[1]
    heads_dev = inner_dev // HD
    queries = query_rows.reshape(length, heads_dev, HD)
    keys_local = key_rows.reshape(length, heads_dev, HD)
    values_local = value_rows.reshape(length, heads_dev, HD)
    query_float = queries.astype(jnp.float32)
    key_float = keys_local.astype(jnp.float32)
    value_float = values_local.astype(jnp.float32)
    local_state = jnp.einsum(
        "shc,shd->hcd", keys_local, values_local, preferred_element_type=jnp.float32
    )
    prev_state = prefix(local_state, "ctx", add_states, jnp.zeros_like(local_state), False)
    mask = causal_mask(length)
    scores = (
        jnp.einsum("thc,shc->hts", queries, keys_local, preferred_element_type=jnp.float32) * mask
    )
    attn = jnp.einsum("hts,shd->thd", scores, value_float, precision=highest)
    attn = attn + jnp.einsum("thc,hcd->thd", query_float, prev_state, precision=highest)
    inv_rms = lax.rsqrt(jnp.mean(attn * attn, axis=-1, keepdims=True) + 1e-06)
    gain = norm_gain.reshape(heads_dev, HD)
    normed = attn * inv_rms * gain
    sig = jax.nn.sigmoid(gate_input.reshape(length, heads_dev, HD).astype(jnp.float32))
    out = (normed * sig).reshape(length, inner_dev).astype(jnp.bfloat16)
    out_full = lax.all_gather(out, "fsdp", axis=1, tiled=True)
    mixed = jnp.dot(out_full, w_out, preferred_element_type=jnp.float32).astype(jnp.bfloat16)
    w_out_grad = lax.psum_scatter(
        lax.dot_general(
            out_full, mixed_grad, (((0,), (0,)), ((), ())), preferred_element_type=jnp.float32
        ),
        "ctx",
        scatter_dimension=0,
        tiled=True,
    )
    grad_term = lax.dot_general(
        mixed_grad, w_out, (((1,), (1,)), ((), ())), preferred_element_type=jnp.float32
    )
    out_grad = lax.psum_scatter(grad_term, "fsdp", scatter_dimension=1, tiled=True).reshape(
        length, heads_dev, HD
    )
    gate_grad = (
        (out_grad * normed * sig * (1.0 - sig)).reshape(length, inner_dev).astype(jnp.bfloat16)
    )
    scaled = out_grad * sig * gain
    attn_grad = inv_rms * scaled - inv_rms * inv_rms * inv_rms * attn * jnp.mean(
        scaled * attn, axis=-1, keepdims=True
    )
    local_grad_state = jnp.einsum("thc,thd->hcd", query_float, attn_grad, precision=highest)
    later_state = prefix(
        local_grad_state, "ctx", add_states, jnp.zeros_like(local_grad_state), True
    )
    prob_grad = jnp.einsum("thd,shd->hts", attn_grad, value_float, precision=highest) * mask
    query_part = jnp.einsum("hts,shc->thc", prob_grad, key_float, precision=highest)
    query_part = query_part + jnp.einsum("thd,hcd->thc", attn_grad, prev_state, precision=highest)
    key_part = jnp.einsum("hts,thc->shc", prob_grad, query_float, precision=highest)
    key_part = key_part + jnp.einsum("shd,hcd->shc", value_float, later_state, precision=highest)
    value_part = jnp.einsum("hts,thd->shd", scores, attn_grad, precision=highest)
    value_part = value_part + jnp.einsum("shc,hcd->shd", key_float, later_state, precision=highest)
    query_grad = query_part.reshape(length, inner_dev).astype(jnp.bfloat16)
    key_grad = key_part.reshape(length, inner_dev).astype(jnp.bfloat16)
    value_grad = value_part.reshape(length, inner_dev).astype(jnp.bfloat16)
    return (mixed, w_out_grad, query_grad, key_grad, value_grad, gate_grad)


def solution(mesh):
    return jax.shard_map(
        per_device,
        mesh=mesh,
        in_specs=(
            P("ctx", "fsdp"),
            P("ctx", "fsdp"),
            P("ctx", "fsdp"),
            P("ctx", "fsdp"),
            P("fsdp"),
            P(None, "fsdp"),
            P("ctx", "fsdp"),
        ),
        out_specs=(
            P("ctx", "fsdp"),
            P("ctx", "fsdp"),
            P("ctx", "fsdp"),
            P("ctx", "fsdp"),
            P("ctx", "fsdp"),
            P("ctx", "fsdp"),
        ),
        check_vma=False,
    )
```

profile of v0, /device:TPU:0, one launch (start us, length us, event | category | flops | bytes accessed | tf_op | source)
XLA Modules:
  0.0 756.1 jit_solution(1982029530388771729)
XLA Ops:
  8.1 9.8 %fusion.44 = f32[512,4096]{1,0:T(8,128)} fusion(bf16[512,768]{1,0:T(8,128)(2,1)} %param.17, bf16[4096,768]{1,0:T(8,128)(2,1)} %param.16), kind=kOutput, calls=%fused_computation.60 | convolution fusion | flops 3221225472 | bytes 15466496 | tf_op jit(solution)/shard_map/dot_general | solution.py:71
  20.4 2.4 copy.39
  22.8 2.5 fusion.22
  25.3 3.1 add_divide_fusion
  28.4 3.0 copy.43
  32.8 5.0 copy-done.1
  37.8 6.6 fusion.6
  44.4 54.8 %reduce-scatter.5.cloned.1.call-done = f32[512,1024]{1,0:T(8,128)} async-done(((f32[512,4096]{1,0:T(8,128)}), f32[512,1024]{1,0:T(8,128)}) %reduce-scatter.5.cloned.1.call-update) | async-done | bytes 2097168 | tf_op jit(solution)/shard_map/reduce_scatter | solution.py:74
  99.2 2.9 copy.44
  102.1 120.1 %all-gather.8.cloned.1.call-done = f32[256,128,128]{2,1,0:T(8,128)} async-done(((f32[8,128,128]{2,1,0:T(8,128)}), f32[256,128,128]{2,1,0:T(8,128)}) %all-gather.8.cloned.1.call-update) | async-done | bytes 16777232 | tf_op jit(solution)/shard_map/all_gather | solution.py:16
  222.3 11.3 %while.22 = (s32[]{:T(128)}, f32[8,128,128]{2,1,0:T(8,128)S(1)}, s32[]{:T(128)}, f32[32,8,128,128]{3,2,1,0:T(8,128)}, s32[]{:T(128)}, /*index=5*/s32[]{:T(128)}, s32[]{:T(128)}) while((s32[]{:T(128)}, f32[8,128,128]{2,1,0:T(8,128)S(1)}, s32[]{:T(128)}, f32[32,8,128,128]{3,2,1,0:T(8,128)}, s32[]{:T(128)}, /*index=5*/s32[]{:T(128)}, ...), condition=%wide.region_1.2_spmd, body=%wide.region_0.1_spmd.sunk | while | flops 131077 | bytes 1572979 | solution.py:23
  233.7 4.7 multiply_reduce_fusion
  238.4 2.4 multiply_convert_fusion
  242.8 2.1 copy.51
  245.0 107.9 %all-gather.6.cloned.1.call-done = bf16[512,4096]{0,1:T(8,128)(2,1)} async-done(((bf16[512,1024]{0,1:T(8,128)(2,1)}), bf16[512,4096]{0,1:T(8,128)(2,1)}) %all-gather.6.cloned.1.call-update) | async-done | bytes 4194320 | tf_op jit(solution)/shard_map/all_gather | solution.py:61
  352.9 10.3 %fusion.43 = f32[4096,768]{1,0:T(8,128)} fusion(bf16[512,4096]{0,1:T(8,128)(2,1)} %all-gather.6.cloned.1.call-done, bf16[512,768]{1,0:T(8,128)(2,1)} %param.17), kind=kOutput, calls=%fused_computation.59 | convolution fusion | flops 3221225472 | bytes 17563648 | tf_op jit(solution)/shard_map/dot_general | solution.py:64
  363.3 3.0 fusion.45
  366.3 3.6 fusion.20
  370.0 6.3 fusion.13
  376.3 2.3 copy.55
  378.6 2.3 copy.58
  380.8 8.6 %fusion = f32[8,512,128]{1,2,0:T(8,128)} fusion(f32[8,512,512]{2,1,0:T(8,128)} %copy-done.2, f32[512,512]{1,0:T(8,128)} %copy-done.5, bf16[512,1024]{1,0:T(8,128)(2,1)S(1)} %copy-done), kind=kOutput, calls=%fused_computation.2 | convolution fusion | flops 3223322624 | bytes 12582912 | tf_op jit(solution)/shard_map/hts,thc->shc/dot_general | solution.py:91
  389.5 6.6 convolution_convert_fusion
  396.1 268.0 %all-gather.10.cloned.1.call-done = f32[256,128,128]{2,1,0:T(8,128)} async-done(((f32[8,128,128]{2,1,0:T(8,128)}), f32[256,128,128]{2,1,0:T(8,128)}) %all-gather.10.cloned.1.call-update) | async-done | bytes 16777232 | tf_op jit(solution)/shard_map/all_gather | solution.py:16
  664.9 63.4 %while.23 = (s32[]{:T(128)}, f32[8,128,128]{2,1,0:T(8,128)}, s32[]{:T(128)}, f32[32,8,128,128]{3,2,1,0:T(8,128)}, s32[]{:T(128)}, /*index=5*/s32[]{:T(128)}, s32[]{:T(128)}, s32[]{:T(128)}) while((s32[]{:T(128)}, f32[8,128,128]{2,1,0:T(8,128)}, s32[]{:T(128)}, f32[32,8,128,128]{3,2,1,0:T(8,128)}, s32[]{:T(128)}, /*index=5*/s32[]{:T(128)}, ...), condition=%wide.region_7.8_spmd, body=%wide.region_6.7_spmd.sunk | while | flops 131078 | bytes 1572999 | solution.py:23
  664.9 2.1 bitcast_add_fusion.8
  667.0 2.0 bitcast_add_fusion.8
  669.0 2.0 bitcast_add_fusion.8
  671.1 2.0 bitcast_add_fusion.8
  675.2 2.1 bitcast_add_fusion.8
  677.2 2.1 bitcast_add_fusion.8
  679.3 2.0 bitcast_add_fusion.8
  681.3 2.0 bitcast_add_fusion.8
  683.3 2.0 bitcast_add_fusion.8
  687.4 2.0 bitcast_add_fusion.8
  689.4 2.0 bitcast_add_fusion.8
  691.5 2.0 bitcast_add_fusion.8
  693.5 2.0 bitcast_add_fusion.8
  695.5 2.0 bitcast_add_fusion.8
  697.6 2.0 bitcast_add_fusion.8
  701.7 2.0 bitcast_add_fusion.8
  703.7 2.0 bitcast_add_fusion.8
  705.7 2.0 bitcast_add_fusion.8
  728.4 2.5 fusion.24
  730.9 9.4 %add_convert_fusion = bf16[8,128,512]{2,1,0:T(8,128)(2,1)} fusion(f32[8,128,512]{2,1,0:T(8,128)S(1)} %fusion.24, f32[512,8,128]{0,2,1:T(8,128)S(1)} %get-tuple-element.122, f32[8,512,512]{2,1,0:T(8,128)} %copy-done.1, f32[512,512]{1,0:T(8,128)S(1)} %copy-done.7), kind=kOutput, calls=%fused_computation.20 | convolution fusion | flops 3224371200 | bytes 14680064 | tf_op jit(solution)/shard_map/hts,thd->shd/dot_general | solution.py:93
  740.3 2.4 copy.57
  742.7 3.6 fusion.12
  746.3 2.3 copy.56
  (64 shorter events, 33.4 us)
Async XLA Ops:
  8.0 23.5 %copy-start = (bf16[512,1024]{1,0:T(8,128)(2,1)S(1)}, bf16[512,1024]{1,0:T(8,128)(2,1)}, u32[]{:S(2)}) copy-start(bf16[512,1024]{1,0:T(8,128)(2,1)} %param.11) | copy-start | bytes 3145732
  8.0 91.2 %reduce-scatter.5.cloned.1.call-start = ((), (), s32[]{:S(2)}) async-start(), calls=%async_computation.4 | async-start | bytes 10485760 | tf_op jit(solution)/shard_map/reduce_scatter | solution.py:74
  17.9 1.2 copy-start.13
  17.9 204.3 %all-gather.8.cloned.1.call-start = ((), (), s32[]{:S(2)}) async-start(), calls=%async_computation.5 | async-start | bytes 17301504 | tf_op jit(solution)/shard_map/all_gather | solution.py:16
  19.1 3.7 copy-start.10
  25.3 327.7 %all-gather.6.cloned.1.call-start = ((), (), s32[]{:S(2)}) async-start(), calls=%async_computation.2 | async-start | bytes 5242880 | tf_op jit(solution)/shard_map/all_gather | solution.py:61
  31.5 1.3 copy-start.5
  32.8 5.0 copy-start.1
  222.2 11.4 %copy-start.15 = (f32[1024]{0:T(1024)S(1)}, f32[1024]{0:T(1024)}, u32[]{:S(2)}) copy-start(f32[1024]{0:T(1024)} %param.15) | copy-start | bytes 12292
  233.6 4.8 copy-start.4
  233.6 4.8 copy-start.8
  233.6 4.8 copy-start.9
  240.8 423.3 %all-gather.10.cloned.1.call-start = ((), (), s32[]{:S(2)}) async-start(), calls=%async_computation.6 | async-start | bytes 17301504 | tf_op jit(solution)/shard_map/all_gather | solution.py:16
  244.9 503.6 %reduce-scatter.3.cloned.1.call-start = ((), (), s32[]{:S(2)}) async-start(), calls=%async_computation.3 | async-start | bytes 12976128 | tf_op jit(solution)/shard_map/reduce_scatter | solution.py:63
  363.3 3.0 copy-start.11
  366.3 3.7 copy-start.6
  366.3 3.7 copy-start.14
  370.0 6.3 copy-start.2
  380.8 8.6 %copy-start.16 = (bf16[512,4096]{0,1:T(8,128)(2,1)S(1)}, bf16[512,4096]{0,1:T(8,128)(2,1)}, u32[]{:S(2)}) copy-start(bf16[512,4096]{0,1:T(8,128)(2,1)} %all-gather.6.cloned.1.call-done) | copy-start | bytes 12582916
  728.3 2.5 copy-start.7
  740.3 2.4 copy-start.3
  740.3 2.4 copy-start.12
Sparse Core Ops, SparseCore 0:
  18.0 81.1 reduce-scatter.4
  240.9 111.9 all-gather.5
  354.7 309.3 all-gather.9
Sparse Core Ops, SparseCore 1:
  25.4 196.8 all-gather.7
  363.4 314.3 reduce-scatter.2
where the time goes:
time: 761 us; the launch traced here: 756 us
  waiting for transfers between devices  551 us (72%)
  matrix products  80.9 us (11%)
  other arithmetic  68.8 us (9%)
  local copies, waits for them, and re-layouts  27.8 us (4%)
  between operations  15.9 us (2%)
  loops' own time  11.6 us (2%)
    all_gather x2, waiting for transfers between devices, prefix(): gathered = lax.all_gather(part, axis)  388 us
    all_gather x1, waiting for transfers between devices, per_device(): out_full = lax.all_gather(out, 'fsdp', axis=1, tiled=True)  108 us
    add x31, other arithmetic, add_states(): return earlier + later  63.2 us
    reduce_scatter x1, waiting for transfers between devices, per_device(): lax.psum_scatter(grad_term, 'fsdp', scatter_dimension=1, tiled=True)  54.8 us
    unnamed x39, local copies, waits for them, and re-layouts  16.6 us
  transfers between devices with their start and end apart: 5, of which 4 were waited for; matrix products, arithmetic and copies ran while one was open for 20% of the time, Pallas kernels for 0%

commit v1 on v0

v1 whole, which is shorter than its diff:
```python
import functools

import jax
import jax.numpy as jnp
from jax import lax
from jax.experimental import pallas as pl
from jax.experimental.pallas import tpu as pltpu
from jax.sharding import PartitionSpec as P

HD = 128
F32 = jnp.float32
BF16 = jnp.bfloat16
VMEM_LIMIT = 48 * 1024 * 1024

NT = (((1,), (1,)), ((), ()))
TN = (((0,), (0,)), ((), ()))
NN = (((1,), (0,)), ((), ()))


def dot(a, b, dims):
    return lax.dot_general(a, b, dims, preferred_element_type=F32)


def params():
    return pltpu.CompilerParams(vmem_limit_bytes=VMEM_LIMIT)


def cost(flops, nbytes):
    return pl.CostEstimate(flops=flops, bytes_accessed=nbytes, transcendentals=0)


def state_kernel(k_ref, v_ref, s_ref):
    s_ref[0] = dot(k_ref[...], v_ref[...], TN)


def block_states(keys, values):
    length, inner = keys.shape
    heads = inner // HD
    rows = pl.BlockSpec((length, HD), lambda i: (0, i))
    return pl.pallas_call(
        state_kernel,
        grid=(heads,),
        in_specs=[rows, rows],
        out_specs=pl.BlockSpec((1, HD, HD), lambda i: (i, 0, 0)),
        out_shape=jax.ShapeDtypeStruct((heads, HD, HD), F32),
        compiler_params=params(),
        cost_estimate=cost(2 * length * inner * HD, 4 * length * inner),
    )(keys, values)


def running_kernel(reverse, count, use_ref, p_ref, offset_ref, out_ref):
    total = offset_ref[...] * use_ref[0].astype(F32)
    for step in range(count):
        place = count - 1 - step if reverse else step
        out_ref[place] = total.astype(out_ref.dtype)
        if step < count - 1:
            total = total + p_ref[place]


def running_sum(pieces, offset, use, reverse):
    count, rows, lanes = pieces.shape
    return pl.pallas_call(
        functools.partial(running_kernel, reverse, count),
        in_specs=[
            pl.BlockSpec(memory_space=pltpu.SMEM),
            pl.BlockSpec(memory_space=pltpu.VMEM),
            pl.BlockSpec(memory_space=pltpu.VMEM),
        ],
        out_specs=pl.BlockSpec(memory_space=pltpu.VMEM),
        out_shape=jax.ShapeDtypeStruct((count, rows, lanes), BF16),
        compiler_params=params(),
        cost_estimate=cost(count * rows * lanes, 6 * count * rows * lanes),
    )(use, pieces, offset)


def head_grad_kernel(sel_ref, a_ref, b_ref, wa_ref, wb_ref, o_ref):
    total = dot(a_ref[...], wa_ref[...], NT) + dot(b_ref[...], wb_ref[...], NT)
    o_ref[...] = total.astype(o_ref.dtype)


def head_grad(sel, mine, other, w_mine, w_other, dtype):
    length, features = mine.shape
    tile = 512
    tiles = 1024 // tile
    whole = pl.BlockSpec((length, features), lambda j, s: (0, 0))
    return pl.pallas_call(
        head_grad_kernel,
        grid_spec=pltpu.PrefetchScalarGridSpec(
            num_scalar_prefetch=1,
            grid=(tiles,),
            in_specs=[
                whole,
                whole,
                pl.BlockSpec((tile, features), lambda j, s: ((s[0] * 2 + s[1]) * tiles + j, 0)),
                pl.BlockSpec((tile, features), lambda j, s: (s[0] * tiles + j, 0)),
            ],
            out_specs=pl.BlockSpec((length, tile), lambda j, s: (0, j)),
        ),
        out_shape=jax.ShapeDtypeStruct((length, 1024), dtype),
        compiler_params=params(),
        cost_estimate=cost(4 * length * features * 1024, 6 * 1024 * features),
    )(sel, mine, other, w_mine, w_other)


def score_rows(q_ref, k_ref, first, size):
    last = first + size
    scores = dot(q_ref[first:last], k_ref[:last], NT)
    return masked(scores, first)


def masked(scores, first):
    rows = lax.broadcasted_iota(jnp.int32, scores.shape, 0) + first
    cols = lax.broadcasted_iota(jnp.int32, scores.shape, 1)
    return jnp.where(cols <= rows, scores, 0.0).astype(BF16)


def head_kernel(
    part, q_ref, k_ref, v_ref, g_ref, gain_ref, s_ref, own_ref, far_ref,
    out_ref, gate_ref, hi_ref, lo_ref, state_ref,
):
    gain = gain_ref[...]
    length = q_ref.shape[0]
    for first in range(0, length, part):
        last = first + part
        scores = score_rows(q_ref, k_ref, first, part)
        attn = dot(scores, v_ref[:last], NN) + dot(q_ref[first:last], s_ref[0], NN)
        inv = lax.rsqrt(jnp.mean(attn * attn, axis=-1, keepdims=True) + 1e-06)
        normed = attn * inv * gain
        sig = 1.0 / (1.0 + jnp.exp(-g_ref[first:last].astype(F32)))
        out_ref[first:last] = (normed * sig).astype(BF16)
        grad = own_ref[first:last] + far_ref[first:last].astype(F32)
        gate_ref[first:last] = (grad * normed * sig * (1.0 - sig)).astype(BF16)
        scaled = grad * sig * gain
        mean = jnp.mean(scaled * attn, axis=-1, keepdims=True)
        full = inv * scaled - inv * inv * inv * attn * mean
        high = full.astype(BF16)
        hi_ref[first:last] = high
        lo_ref[first:last] = (full - high.astype(F32)).astype(BF16)
    state_ref[0] = dot(q_ref[...], hi_ref[...], TN)


def head_forward(queries, keys, values, gate, gain, state, own, far):
    length, inner = queries.shape
    heads = inner // HD
    rows = pl.BlockSpec((length, HD), lambda i: (0, i))
    square = pl.BlockSpec((1, HD, HD), lambda i: (i, 0, 0))
    wide = jax.ShapeDtypeStruct((length, inner), BF16)
    return pl.pallas_call(
        functools.partial(head_kernel, 256),
        grid=(heads,),
        in_specs=[
            rows, rows, rows, rows, pl.BlockSpec((1, HD), lambda i: (0, i)), square, rows, rows,
        ],
        out_specs=[rows, rows, rows, rows, square],
        out_shape=[wide, wide, wide, wide, jax.ShapeDtypeStruct((heads, HD, HD), F32)],
        compiler_params=params(),
        cost_estimate=cost(6 * length * length * inner, 20 * length * inner),
    )(queries, keys, values, gate, gain, state, own, far)


def grads_kernel(
    part, q_ref, k_ref, v_ref, hi_ref, lo_ref, s_ref, l_ref, dq_ref, dk_ref, dv_ref, dk_sum, dv_sum
):
    length = q_ref.shape[0]
    later = l_ref[0]
    dk_sum[...] = dot(v_ref[...], later, NT)
    dv_sum[...] = dot(k_ref[...], later, NN)
    for first in range(0, length, part):
        last = first + part
        high = hi_ref[first:last]
        scores = score_rows(q_ref, k_ref, first, part)
        prob = dot(high, v_ref[:last], NT) + dot(lo_ref[first:last], v_ref[:last], NT)
        prob = masked(prob, first)
        dq = dot(prob, k_ref[:last], NN) + dot(high, s_ref[0], NT)
        dq_ref[first:last] = dq.astype(BF16)
        dk_sum[:last] += dot(prob, q_ref[first:last], TN)
        dv_sum[:last] += dot(scores, high, TN)
    dk_ref[...] = dk_sum[...].astype(BF16)
    dv_ref[...] = dv_sum[...].astype(BF16)


def head_grads(queries, keys, values, high, low, state, later):
    length, inner = queries.shape
    heads = inner // HD
    rows = pl.BlockSpec((length, HD), lambda i: (0, i))
    square = pl.BlockSpec((1, HD, HD), lambda i: (i, 0, 0))
    wide = jax.ShapeDtypeStruct((length, inner), BF16)
    return pl.pallas_call(
        functools.partial(grads_kernel, 256),
        grid=(heads,),
        in_specs=[rows, rows, rows, rows, rows, square, square],
        out_specs=[rows, rows, rows],
        out_shape=[wide, wide, wide],
        scratch_shapes=[pltpu.VMEM((length, HD), F32), pltpu.VMEM((length, HD), F32)],
        compiler_params=params(),
        cost_estimate=cost(12 * length * length * inner, 16 * length * inner),
    )(queries, keys, values, high, low, state, later)


def mixed_kernel(sel_ref, a_ref, b_ref, c_ref, d_ref, w_ref, o_ref):
    total = None
    for place, block in enumerate((a_ref, b_ref, c_ref, d_ref)):
        first = pl.multiple_of(sel_ref[place] * 1024, 1024)
        term = dot(block[...], w_ref[pl.ds(first, 1024), :], NN)
        total = term if total is None else total + term
    o_ref[...] = total.astype(BF16)


def mix(sel, blocks, w_out):
    length, width = blocks[0].shape
    inner, features = w_out.shape
    tile = 256
    whole = pl.BlockSpec((length, width), lambda j, s: (0, 0))
    return pl.pallas_call(
        mixed_kernel,
        grid_spec=pltpu.PrefetchScalarGridSpec(
            num_scalar_prefetch=1,
            grid=(features // tile,),
            in_specs=[whole] * 4 + [pl.BlockSpec((inner, tile), lambda j, s: (0, j))],
            out_specs=pl.BlockSpec((length, tile), lambda j, s: (0, j)),
        ),
        out_shape=jax.ShapeDtypeStruct((length, features), BF16),
        compiler_params=params(),
        cost_estimate=cost(2 * length * inner * features, 2 * inner * features),
    )(sel, *blocks, w_out)


def weight_kernel(sel_ref, a0_ref, a1_ref, b0_ref, b1_ref, m0_ref, m1_ref, o_ref):
    source = pl.program_id(0)

    @pl.when(source == 0)
    def _():
        total = dot(a0_ref[...], m0_ref[...], TN) + dot(a1_ref[...], m1_ref[...], TN)
        o_ref[...] = total.astype(BF16)

    @pl.when(source == 1)
    def _():
        total = dot(b0_ref[...], m0_ref[...], TN) + dot(b1_ref[...], m1_ref[...], TN)
        o_ref[...] = total.astype(BF16)


def weight_grad(sel, mine, other, grads):
    length, width = mine[0].shape
    features = grads[0].shape[1]
    tile = 256
    tiles = width // tile
    last = tiles - 1
    first_rows = pl.BlockSpec((length, tile), lambda i, j, s: (0, jnp.where(i == 0, j, last)))
    second_rows = pl.BlockSpec((length, tile), lambda i, j, s: (0, jnp.where(i == 0, 0, j)))
    whole = pl.BlockSpec((length, features), lambda i, j, s: (0, 0))
    return pl.pallas_call(
        weight_kernel,
        grid_spec=pltpu.PrefetchScalarGridSpec(
            num_scalar_prefetch=1,
            grid=(2, tiles),
            in_specs=[first_rows, first_rows, second_rows, second_rows, whole, whole],
            out_specs=pl.BlockSpec(
                (tile, features), lambda i, j, s: ((s[0] + i - 2 * s[0] * i) * tiles + j, 0)
            ),
        ),
        out_shape=jax.ShapeDtypeStruct((2 * width, features), BF16),
        compiler_params=params(),
        cost_estimate=cost(8 * length * width * features, 4 * width * features),
    )(sel, mine[0], mine[1], other[0], other[1], *grads)


def per_device(query_rows, key_rows, value_rows, gate_input, norm_gain, w_out, mixed_grad):
    length, inner_dev = query_rows.shape
    heads_dev = inner_dev // HD
    features = w_out.shape[1]
    planes, across = 2, 16
    ctx, fsdp = lax.axis_index("ctx"), lax.axis_index("fsdp")
    y_lo = ctx // across
    y_hi, core = fsdp // 2, fsdp % 2
    groups = [[y * across + i for i in range(across)] for y in range(planes)]
    core_swap = [(0, 1), (1, 0), (2, 3), (3, 2)]
    hi_swap = [(0, 2), (1, 3), (2, 0), (3, 1)]
    lo_swap = [(i, (i + across) % (2 * across)) for i in range(2 * across)]

    def swap_core(array):
        return lax.ppermute(array, "fsdp", core_swap)

    def swap_hi(array):
        return lax.ppermute(array, "fsdp", hi_swap)

    def swap_lo(array):
        return lax.ppermute(array, "ctx", lo_swap)

    def exchange(array):
        return lax.all_to_all(array, "ctx", 0, 0, axis_index_groups=groups)

    def states_before(local, reverse):
        rows = heads_dev * HD // across
        pieces = exchange(local.reshape(across, rows, HD))
        offset = swap_lo(jnp.sum(pieces, axis=0))
        use = (y_lo == (0 if reverse else 1)).astype(jnp.int32).reshape(1)
        sums = running_sum(pieces, offset, use, reverse)
        return exchange(sums).reshape(heads_dev, HD, HD)

    grad_pair = swap_lo(mixed_grad)
    grad_core = swap_core(mixed_grad)
    w_rows = w_out.reshape(2, 2, inner_dev, features)
    w_sent = lax.dynamic_index_in_dim(w_rows, 1 - core, 1, False).reshape(2 * inner_dev, features)
    w_core = swap_core(w_sent)
    select_far = jnp.stack([1 - y_hi, core]).astype(jnp.int32)
    select_own = jnp.stack([y_hi, core]).astype(jnp.int32)
    far_part = head_grad(select_far, mixed_grad, grad_core, w_out, w_core, BF16)
    grad_own = head_grad(select_own, mixed_grad, grad_core, w_out, w_core, F32)

    local_state = block_states(key_rows, value_rows)
    prev_state = states_before(local_state, False)
    grad_far = swap_hi(far_part)

    out, gate_grad, high, low, grad_state = head_forward(
        query_rows, key_rows, value_rows, gate_input, norm_gain.reshape(1, inner_dev),
        prev_state, grad_own, grad_far,
    )

    moves = []
    for turn in range(2):
        pairs = []
        for place in range(2 * across):
            lo, rest = place // across, place % across
            for part in range(4):
                hi, side = part // 2, part % 2
                target = (hi * across + rest) * 4 + (lo ^ turn) * 2 + side
                pairs.append((place * 4 + part, target))
        moves.append(lax.ppermute(out, ("ctx", "fsdp"), pairs))
    moved_core = [swap_core(block) for block in moves]
    near = y_hi == y_lo
    grads = [jnp.where(near, mixed_grad, grad_pair), jnp.where(near, grad_pair, mixed_grad)]
    weight = weight_grad(core.astype(jnp.int32).reshape(1), moves, moved_core, grads)
    parts = exchange(weight.reshape(across, 2 * inner_dev // across, features))
    w_out_grad = jnp.sum(parts.astype(F32), axis=0)

    out_far = swap_hi(out)
    blocks = [out, swap_core(out), out_far, swap_core(out_far)]
    order = jnp.stack(
        [fsdp, fsdp + 1 - 2 * core, (fsdp + 2) % 4, (fsdp + 2) % 4 + 1 - 2 * core]
    ).astype(jnp.int32)
    mixed = mix(order, blocks, w_out)

    later_state = states_before(grad_state, True)
    query_grad, key_grad, value_grad = head_grads(
        query_rows, key_rows, value_rows, high, low, prev_state, later_state
    )
    return (mixed, w_out_grad, query_grad, key_grad, value_grad, gate_grad)


def solution(mesh):
    return jax.shard_map(
        per_device,
        mesh=mesh,
        in_specs=(
            P("ctx", "fsdp"),
            P("ctx", "fsdp"),
            P("ctx", "fsdp"),
            P("ctx", "fsdp"),
            P("fsdp"),
            P(None, "fsdp"),
            P("ctx", "fsdp"),
        ),
        out_specs=(
            P("ctx", "fsdp"),
            P("ctx", "fsdp"),
            P("ctx", "fsdp"),
            P("ctx", "fsdp"),
            P("ctx", "fsdp"),
            P("ctx", "fsdp"),
        ),
        check_vma=False,
    )
```

time: 761 us -> 219 us (0.29)
  waiting for transfers between devices: 551 us -> 70.4 us
  matrix products: 80.9 us -> 0 us
  other arithmetic: 68.8 us -> 5.75 us
  starting transfers between devices: 0.21 us -> 55.5 us
  Pallas kernels: 0 us -> 52.5 us
  blocking collectives: 0 us -> 19.2 us
  local copies, waits for them, and re-layouts: 27.8 us -> 11.9 us
  between operations: 15.9 us -> 0.8 us
  loops' own time: 11.6 us -> 0 us
    all_gather x3 -> x0, waiting for transfers between devices: 496 us -> none  [the longest x2 388 us: prefix(): gathered = lax.all_gather(part, axis)]
    dot_general x15 -> x0, matrix products: 80.9 us -> none  [the longest x1 10.3 us: per_device(): lax.dot_general(out_full, mixed_grad, (((0,), (0,)), ((), ())), preferred...]
    add x31 -> x0, other arithmetic: 63.2 us -> none  [add_states(): return earlier + later]
    ppermute x0 -> x13, waiting for transfers between devices: none -> 55.8 us  [the longest x2 23.6 us: per_device(): moves.append(lax.ppermute(out, ('ctx', 'fsdp'), pairs))]
    reduce_scatter x2 -> x0, waiting for transfers between devices: 54.8 us -> none  [the longest x1 54.8 us: per_device(): lax.psum_scatter(grad_term, 'fsdp', scatter_dimension=1, tiled=True)]
    pallas_call x0 -> x9, Pallas kernels: none -> 52.5 us  [the longest x1 11.4 us: head_grads(): pl.pallas_call(functools.partial(grads_kernel, 256), grid=(heads,), in_sp...]
    ppermute x0 -> x13, starting transfers between devices: none -> 32.9 us  [the longest x3 21.6 us: swap_lo(): return lax.ppermute(array, 'ctx', lo_swap)]
    all_to_all x0 -> x4, starting transfers between devices: none -> 22.6 us  [exchange(): return lax.all_to_all(array, 'ctx', 0, 0, axis_index_groups=groups)]
  transfers between devices with their start and end apart: 5 -> 17, of which waited for: 4 -> 7; matrix products, arithmetic and copies ran while one was open for 20% -> 1% of each run, Pallas kernels for 0% -> 17%
where the time goes in v1:
time: 219 us; the launch traced here: 216 us
  waiting for transfers between devices  70.4 us (32%)
  starting transfers between devices  55.5 us (25%)
  Pallas kernels  52.5 us (24%)
  blocking collectives  19.2 us (9%)
  local copies, waits for them, and re-layouts  11.9 us (5%)
  other arithmetic  5.75 us (3%)
    ppermute x2, waiting for transfers between devices, per_device(): moves.append(lax.ppermute(out, ('ctx', 'fsdp'), pairs))  23.6 us
    all_to_all x4, starting transfers between devices, exchange(): return lax.all_to_all(array, 'ctx', 0, 0, axis_index_groups=groups)  22.6 us
    ppermute x2, waiting for transfers between devices, swap_hi(): return lax.ppermute(array, 'fsdp', hi_swap)  22.6 us
    ppermute x3, starting transfers between devices, swap_lo(): return lax.ppermute(array, 'ctx', lo_swap)  21.6 us
    all_to_all x1, blocking collectives, exchange(): return lax.all_to_all(array, 'ctx', 0, 0, axis_index_groups=groups)  19.2 us
    all_to_all x4, waiting for transfers between devices, exchange(): return lax.all_to_all(array, 'ctx', 0, 0, axis_index_groups=groups)  14.6 us
    pallas_call x1, Pallas kernels, head_grads(): pl.pallas_call(functools.partial(grads_kernel, 256), grid=(heads,), in_sp...  11.4 us
    pallas_call x1, Pallas kernels, head_forward(): pl.pallas_call(functools.partial(head_kernel, 256), grid=(heads,), in_spe...  10.3 us
  transfers between devices with their start and end apart: 17, of which 7 were waited for; matrix products, arithmetic and copies ran while one was open for 1% of the time, Pallas kernels for 17%

profile of v1, /device:TPU:0, one launch (start us, length us, event | category | flops | bytes accessed | tf_op | source)
XLA Modules:
  0.0 216.0 jit_solution(13915120664000451606)
XLA Ops:
  0.6 3.7 %constant_dynamic-slice_fusion = bf16[2,1,1024,768]{3,2,1,0:T(8,128)(2,1)} fusion(bf16[2,2,1024,768]{3,2,1,0:T(8,128)(2,1)} %bitcast.24, s32[]{:T(128)S(6)} %select_n.40), kind=kLoop, calls=%fused_computation.6 | loop fusion | bytes 6291460 | tf_op jit(solution)/shard_map/jit(dynamic_index_in_dim)/dynamic_slice | solution.py:303
  4.4 0.0 collective-permute-start.2
  4.4 0.5 collective-permute-start.1
  4.9 0.1 pad_add_fusion.2.sel_ref
  5.0 6.2 %collective-permute-done.1.b_ref = bf16[512,768]{1,0:T(8,128)(2,1)} collective-permute-done((bf16[512,768]{1,0:T(8,128)(2,1)}, bf16[512,768]{1,0:T(8,128)(2,1)}, u32[]{:S(2)}, u32[]{:S(2)}) %collective-permute-start.1) | collective-permute-done | bytes 786464 | tf_op jit(solution)/shard_map/ppermute | solution.py:281
  11.1 0.2 collective-permute-done.2.wb_ref
  11.4 5.6 %shard_map.121 = bf16[512,1024]{1,0:T(8,128)(2,1)} custom-call(s32[2]{0:T(128)S(1)} %pad_add_fusion.2.sel_ref, bf16[512,768]{1,0:T(8,128)(2,1)} %a_ref.3, bf16[512,768]{1,0:T(8,128)(2,1)} %collective-permute-done.1.b_ref, bf16[4096,768]{1,0:T(8,128)(2,1)} %w_ref.1, bf16[2048,768]{1,0:T(8,128)(2,1)S(1)} %collective-permute-done.2.wb_ref), custom_call_target="tpu_custom_call" | custom-call | flops 1610612736 | bytes 4718592 | tf_op jit(solution)/shard_map/pallas_call | solution.py:86
  16.9 3.3 %collective-permute-start.3 = (bf16[512,1024]{1,0:T(8,128)(2,1)}, bf16[512,1024]{1,0:T(8,128)(2,1)}, u32[]{:S(2)}, u32[]{:S(2)}) collective-permute-start(bf16[512,1024]{1,0:T(8,128)(2,1)} %shard_map.121), channel_id=1, source_target_pairs={{0,2},{1,3},{2,0},{3,1},{4,6},{5,7},{6,4},{7,5},{8,10},{9,11},{10,... | collective-permute-start | bytes 3145736 | tf_op jit(solution)/shard_map/ppermute | solution.py:284
  20.2 2.5 %shard_map.118 = f32[8,128,128]{2,1,0:T(8,128)S(1)} custom-call(bf16[512,1024]{1,0:T(8,128)(2,1)S(1)} %copy-done.2, bf16[512,1024]{1,0:T(8,128)(2,1)S(1)} %copy-done.4), custom_call_target="tpu_custom_call" | custom-call | flops 134217728 | bytes 2097152 | tf_op jit(solution)/shard_map/pallas_call | solution.py:40
  22.7 19.2 %all_to_all.25.p_ref = f32[16,64,128]{2,1,0:T(8,128)S(1)} all-to-all(f32[16,64,128]{2,1,0:T(8,128)S(1)} %bitcast.19), channel_id=1, replica_groups={{0,4,8,12,16,20,24,28,32,36,40,44,48,52,56,60},{64,68,72,76,80,84,88,92..., dimensions={0} | all-to-all | bytes 1048576 | tf_op jit(solution)/shard_map/all_to_all | solution.py:290
  41.9 0.8 collective-permute-start
  42.7 3.2 %collective-permute-done.offset_ref = f32[64,128]{1,0:T(8,128)S(1)} collective-permute-done((f32[64,128]{1,0:T(8,128)S(1)}, f32[64,128]{1,0:T(8,128)S(1)}, u32[]{:S(2)}, u32[]{:S(2)}) %collective-permute-start) | collective-permute-done | bytes 32800 | tf_op jit(solution)/shard_map/ppermute | solution.py:287
  45.9 0.7 shard_map.119
  46.7 6.9 %all-to-all-start.1 = ((bf16[16,64,128]{2,1,0:T(8,128)(2,1)}), bf16[16,64,128]{2,1,0:T(8,128)(2,1)S(1)}, u32[]{:S(2)}, u32[]{:S(2)}) async-start(bf16[16,64,128]{2,1,0:T(8,128)(2,1)} %shard_map.119), calls=%async_computation.1 | async-start | bytes 524288 | tf_op jit(solution)/shard_map/all_to_all | solution.py:290
  53.6 0.1 pad_add_fusion.1.sel_ref
  53.7 4.7 %shard_map.120.own_ref = f32[512,1024]{1,0:T(8,128)S(1)} custom-call(s32[2]{0:T(128)S(1)} %pad_add_fusion.1.sel_ref, bf16[512,768]{1,0:T(8,128)(2,1)} %a_ref.3, bf16[512,768]{1,0:T(8,128)(2,1)} %collective-permute-done.1.b_ref, bf16[4096,768]{1,0:T(8,128)(2,1)} %w_ref.1, bf16[2048,768]{1,0:T(8,128)(2,1)} %copy-done), custom_call_target="tpu_custom_call" | custom-call | flops 1610612736 | bytes 4718592 | tf_op jit(solution)/shard_map/pallas_call | solution.py:86
  58.4 1.3 copy-done.1
  59.7 2.4 %all-to-all-done.1 = bf16[16,64,128]{2,1,0:T(8,128)(2,1)S(1)} async-done(((bf16[16,64,128]{2,1,0:T(8,128)(2,1)}), bf16[16,64,128]{2,1,0:T(8,128)(2,1)S(1)}, u32[]{:S(2)}, u32[]{:S(2)}) %all-to-all-start.1) | async-done | bytes 262176 | tf_op jit(solution)/shard_map/all_to_all | solution.py:290
  62.1 10.3 %shard_map.122 = (bf16[512,1024]{1,0:T(8,128)(2,1)S(1)}, bf16[512,1024]{1,0:T(8,128)(2,1)}, bf16[512,1024]{1,0:T(8,128)(2,1)S(1)}, bf16[512,1024]{1,0:T(8,128)(2,1)S(1)}, f32[8,128,128]{2,1,0:T(8,128)}) custom-call(bf16[512,1024]{1,0:T(8,128)(2,1)S(1)} %copy-done.6, bf16[512,1024]{1,0:T(8,128)(2,1)S(1)} %copy-done.3, bf16[512,1024]{1,0:T(8,128)(2,1)} %v_ref.5, ...), custom_call_target="tpu_custom_call" | custom-call | flops 1610612736 | bytes 10485760 | tf_op jit(solution)/shard_map/pallas_call | solution.py:148
  72.4 1.0 copy-done.12
  73.4 1.0 copy-done.14
  74.4 1.6 collective-permute-start.7
  76.0 3.8 %collective-permute-start.8 = (bf16[512,1024]{1,0:T(8,128)(2,1)S(1)}, bf16[512,1024]{1,0:T(8,128)(2,1)}, u32[]{:S(2)}, u32[]{:S(2)}) collective-permute-start(bf16[512,1024]{1,0:T(8,128)(2,1)S(1)} %get-tuple-element.14.a_ref), channel_id=1, source_target_pairs={{0,2},{1,3},{2,66},{3,67},{4,6},{5,7},{6,70},{7,71},{8,10},{9,11},... | collective-permute-start | bytes 3145736 | tf_op jit(solution)/shard_map/ppermute | solution.py:328
  79.8 0.0 collective-permute-start.11
  79.8 23.6 %collective-permute-done.8.a1_ref = bf16[512,1024]{1,0:T(8,128)(2,1)} collective-permute-done((bf16[512,1024]{1,0:T(8,128)(2,1)S(1)}, bf16[512,1024]{1,0:T(8,128)(2,1)}, u32[]{:S(2)}, u32[]{:S(2)}) %collective-permute-start.8) | collective-permute-done | bytes 1048608 | tf_op jit(solution)/shard_map/ppermute | solution.py:328
  103.4 4.8 %all-to-all-start.3 = ((f32[16,64,128]{2,1,0:T(8,128)}), f32[16,64,128]{2,1,0:T(8,128)S(1)}, u32[]{:S(2)}, u32[]{:S(2)}) async-start(f32[16,64,128]{2,1,0:T(8,128)} %bitcast.15), calls=%async_computation.3 | async-start | bytes 1048576 | tf_op jit(solution)/shard_map/all_to_all | solution.py:290
  108.2 12.2 %all-to-all-done.3.p_ref = f32[16,64,128]{2,1,0:T(8,128)S(1)} async-done(((f32[16,64,128]{2,1,0:T(8,128)}), f32[16,64,128]{2,1,0:T(8,128)S(1)}, u32[]{:S(2)}, u32[]{:S(2)}) %all-to-all-start.3) | async-done | bytes 524320 | tf_op jit(solution)/shard_map/all_to_all | solution.py:290
  120.4 20.8 %collective-permute-start.12 = (f32[64,128]{1,0:T(8,128)S(1)}, f32[64,128]{1,0:T(8,128)S(1)}, u32[]{:S(2)}, u32[]{:S(2)}) collective-permute-start(f32[64,128]{1,0:T(8,128)S(1)} %reduce_sum.29), channel_id=1, source_target_pairs={{0,64},{4,68},{8,72},{12,76},{16,80},{20,84},{24,88},{28,92},{32,9... | collective-permute-start | bytes 98312 | tf_op jit(solution)/shard_map/ppermute | solution.py:287
  141.2 0.0 collective-permute-done.11
  141.2 2.4 %broadcast_select_fusion = (bf16[512,768]{1,0:T(8,128)(2,1)S(1)}, bf16[512,768]{1,0:T(8,128)(2,1)}) fusion(bf16[512,768]{1,0:T(8,128)(2,1)} %collective-permute-done.11, bf16[512,768]{1,0:T(8,128)(2,1)} %a_ref.3, pred[]{:T(512)S(6)} %eq.14), kind=kLoop, calls=%fused_computation.1 | loop fusion | flops 786432 | bytes 3145729 | tf_op jit(solution)/shard_map/jit(_where)/select_n | solution.py:331
  143.6 0.0 collective-permute-done.12.offset_ref
  143.6 0.7 shard_map.125
  144.3 3.5 %all-to-all-start.4 = ((bf16[16,64,128]{2,1,0:T(8,128)(2,1)}), bf16[16,64,128]{2,1,0:T(8,128)(2,1)S(1)}, u32[]{:S(2)}, u32[]{:S(2)}) async-start(bf16[16,64,128]{2,1,0:T(8,128)(2,1)} %shard_map.125), calls=%async_computation.4 | async-start | bytes 524288 | tf_op jit(solution)/shard_map/all_to_all | solution.py:290
  147.9 0.0 collective-permute-done.9.b0_ref
  147.9 0.0 collective-permute-done.10.b1_ref
  147.9 0.0 copy-start.8
  147.9 1.1 copy-done.8
  149.0 8.7 %shard_map.124 = bf16[2048,768]{1,0:T(8,128)(2,1)} custom-call(s32[1]{0:T(128)} %bitcast.9.sel_ref, bf16[512,1024]{1,0:T(8,128)(2,1)} %collective-permute-done.7.a0_ref, bf16[512,1024]{1,0:T(8,128)(2,1)} %collective-permute-done.8.a1_ref, bf16[512,1024]{1,0:T(8,128)(2,1)} %collective-permute-done.9.b0_ref, bf16[512,1024]{1,0:T(8,128)(2,1)} %collective-permute-done.10.b1_ref, ...), custom_call_target="tpu_custom_call" | custom-call | flops 3221225472 | bytes 3145728 | tf_op jit(solution)/shard_map/pallas_call | solution.py:251
  157.7 7.4 %all-to-all-start.2 = ((bf16[16,128,768]{2,1,0:T(8,128)(2,1)}), bf16[16,128,768]{2,1,0:T(8,128)(2,1)}, u32[]{:S(2)}, u32[]{:S(2)}) async-start(bf16[16,128,768]{2,1,0:T(8,128)(2,1)} %bitcast.25), calls=%async_computation.2 | async-start | bytes 6291456 | tf_op jit(solution)/shard_map/all_to_all | solution.py:290
  165.1 2.1 collective-permute-start.5
  167.2 22.6 %collective-permute-done.5.c_ref = bf16[512,1024]{1,0:T(8,128)(2,1)} collective-permute-done((bf16[512,1024]{1,0:T(8,128)(2,1)}, bf16[512,1024]{1,0:T(8,128)(2,1)}, u32[]{:S(2)}, u32[]{:S(2)}) %collective-permute-start.5) | collective-permute-done | bytes 1048608 | tf_op jit(solution)/shard_map/ppermute | solution.py:284
  189.8 0.1 pad_add_fusion.sel_ref
  189.8 1.2 copy-done.7
  191.1 1.2 copy-done.13
  192.3 1.2 copy-done.15
  193.5 11.4 %shard_map.126 = (bf16[512,1024]{1,0:T(8,128)(2,1)}, bf16[512,1024]{1,0:T(8,128)(2,1)}, bf16[512,1024]{1,0:T(8,128)(2,1)}) custom-call(bf16[512,1024]{1,0:T(8,128)(2,1)S(1)} %copy-done.7, bf16[512,1024]{1,0:T(8,128)(2,1)S(1)} %copy-done.3, bf16[512,1024]{1,0:T(8,128)(2,1)S(1)} %copy-done.5, bf16[512,1024]{1,0:T(8,128)(2,1)S(1)} %copy-done.13, ...), custom_call_target="tpu_custom_call" | custom-call | flops 3221225472 | bytes 8388608 | tf_op jit(solution)/shard_map/pallas_call | solution.py:188
  204.9 8.0 %shard_map.123 = bf16[512,768]{1,0:T(8,128)(2,1)} custom-call(s32[4]{0:T(128)S(1)} %pad_add_fusion.sel_ref, bf16[512,1024]{1,0:T(8,128)(2,1)S(1)} %copy-done.11, bf16[512,1024]{1,0:T(8,128)(2,1)} %collective-permute-done.4.b_ref, bf16[512,1024]{1,0:T(8,128)(2,1)} %collective-permute-done.5.c_ref, bf16[512,1024]{1,0:T(8,128)(2,1)} %collective-permute-done.6.d_ref, ...), custom_call_target="tpu_custom_call" | custom-call | flops 3221225472 | bytes 6291456 | tf_op jit(solution)/shard_map/pallas_call | solution.py:214
  212.9 3.1 %convert_reduce_fusion = f32[128,768]{1,0:T(8,128)} fusion(bf16[16,128,768]{2,1,0:T(8,128)(2,1)} %all-to-all-done.2), kind=kLoop, calls=%fused_computation | loop fusion | flops 3047424 | bytes 3538944 | tf_op jit(solution)/shard_map/reduce_sum | solution.py:334
  (36 shorter events, 0.1 us)
Async XLA Ops:
  4.4 7.0 %collective-permute-start.2 = (bf16[2048,768]{1,0:T(8,128)(2,1)}, bf16[2048,768]{1,0:T(8,128)(2,1)S(1)}, u32[]{:S(2)}, u32[]{:S(2)}) collective-permute-start(bf16[2048,768]{1,0:T(8,128)(2,1)} %bitcast.11), channel_id=1, source_target_pairs={{0,1},{1,0},{2,3},{3,2},{4,5},{5,4},{6,7},{7,6},{8,9},{9,8},{10,11... | collective-permute-start | bytes 9437192 | tf_op jit(solution)/shard_map/ppermute | solution.py:281
  4.4 6.8 %collective-permute-start.1 = (bf16[512,768]{1,0:T(8,128)(2,1)}, bf16[512,768]{1,0:T(8,128)(2,1)}, u32[]{:S(2)}, u32[]{:S(2)}) collective-permute-start(bf16[512,768]{1,0:T(8,128)(2,1)} %a_ref.3), channel_id=1, source_target_pairs={{0,1},{1,0},{2,3},{3,2},{4,5},{5,4},{6,7},{7,6},{8,9},{9,8},{10,11... | collective-permute-start | bytes 2359304 | tf_op jit(solution)/shard_map/ppermute | solution.py:281
  5.0 15.3 %copy-start.2 = (bf16[512,1024]{1,0:T(8,128)(2,1)S(1)}, bf16[512,1024]{1,0:T(8,128)(2,1)}, u32[]{:S(2)}) copy-start(bf16[512,1024]{1,0:T(8,128)(2,1)} %k_ref.5) | copy-start | bytes 3145732
  5.0 15.3 %copy-start.4 = (bf16[512,1024]{1,0:T(8,128)(2,1)S(1)}, bf16[512,1024]{1,0:T(8,128)(2,1)}, u32[]{:S(2)}) copy-start(bf16[512,1024]{1,0:T(8,128)(2,1)} %v_ref.5) | copy-start | bytes 3145732
  11.4 5.6 %copy-start = (bf16[2048,768]{1,0:T(8,128)(2,1)}, bf16[2048,768]{1,0:T(8,128)(2,1)S(1)}, u32[]{:S(2)}) copy-start(bf16[2048,768]{1,0:T(8,128)(2,1)S(1)} %collective-permute-done.2.wb_ref) | copy-start | bytes 9437188
  16.9 45.2 %collective-permute-start.3 = (bf16[512,1024]{1,0:T(8,128)(2,1)}, bf16[512,1024]{1,0:T(8,128)(2,1)}, u32[]{:S(2)}, u32[]{:S(2)}) collective-permute-start(bf16[512,1024]{1,0:T(8,128)(2,1)} %shard_map.121), channel_id=1, source_target_pairs={{0,2},{1,3},{2,0},{3,1},{4,6},{5,7},{6,4},{7,5},{8,10},{9,11},{10,... | collective-permute-start | bytes 3145736 | tf_op jit(solution)/shard_map/ppermute | solution.py:284
  41.9 4.0 %collective-permute-start = (f32[64,128]{1,0:T(8,128)S(1)}, f32[64,128]{1,0:T(8,128)S(1)}, u32[]{:S(2)}, u32[]{:S(2)}) collective-permute-start(f32[64,128]{1,0:T(8,128)S(1)} %reduce_sum.27), channel_id=1, source_target_pairs={{0,64},{4,68},{8,72},{12,76},{16,80},{20,84},{24,88},{28,92},{32,9... | collective-permute-start | bytes 98312 | tf_op jit(solution)/shard_map/ppermute | solution.py:287
  46.7 15.5 %all-to-all-start.1 = ((bf16[16,64,128]{2,1,0:T(8,128)(2,1)}), bf16[16,64,128]{2,1,0:T(8,128)(2,1)S(1)}, u32[]{:S(2)}, u32[]{:S(2)}) async-start(bf16[16,64,128]{2,1,0:T(8,128)(2,1)} %shard_map.119), calls=%async_computation.1 | async-start | bytes 524288 | tf_op jit(solution)/shard_map/all_to_all | solution.py:290
  53.7 8.4 %copy-start.3 = (bf16[512,1024]{1,0:T(8,128)(2,1)S(1)}, bf16[512,1024]{1,0:T(8,128)(2,1)}, u32[]{:S(2)}) copy-start(bf16[512,1024]{1,0:T(8,128)(2,1)} %k_ref.5) | copy-start | bytes 3145732
  53.7 8.4 %copy-start.6 = (bf16[512,1024]{1,0:T(8,128)(2,1)S(1)}, bf16[512,1024]{1,0:T(8,128)(2,1)}, u32[]{:S(2)}) copy-start(bf16[512,1024]{1,0:T(8,128)(2,1)} %q_ref.3) | copy-start | bytes 3145732
  53.7 8.4 %copy-start.9 = (f32[1024]{0:T(1024)S(1)}, f32[1024]{0:T(1024)}, u32[]{:S(2)}) copy-start(f32[1024]{0:T(1024)} %param.11) | copy-start | bytes 12292
  58.4 1.3 copy-start.1
  72.4 1.0 copy-start.12
  73.4 1.0 copy-start.14
  74.4 1.6 copy-start.10
  74.4 5.4 %collective-permute-start.7 = (bf16[512,1024]{1,0:T(8,128)(2,1)S(1)}, bf16[512,1024]{1,0:T(8,128)(2,1)}, u32[]{:S(2)}, u32[]{:S(2)}) collective-permute-start(bf16[512,1024]{1,0:T(8,128)(2,1)S(1)} %get-tuple-element.14.a_ref), channel_id=1, source_target_pairs={{0,0},{1,1},{2,64},{3,65},{4,4},{5,5},{6,68},{7,69},{8,8},{9,9},{1... | collective-permute-start | bytes 3145736 | tf_op jit(solution)/shard_map/ppermute | solution.py:328
  76.0 27.4 %collective-permute-start.8 = (bf16[512,1024]{1,0:T(8,128)(2,1)S(1)}, bf16[512,1024]{1,0:T(8,128)(2,1)}, u32[]{:S(2)}, u32[]{:S(2)}) collective-permute-start(bf16[512,1024]{1,0:T(8,128)(2,1)S(1)} %get-tuple-element.14.a_ref), channel_id=1, source_target_pairs={{0,2},{1,3},{2,66},{3,67},{4,6},{5,7},{6,70},{7,71},{8,10},{9,11},... | collective-permute-start | bytes 3145736 | tf_op jit(solution)/shard_map/ppermute | solution.py:328
  79.8 61.4 %collective-permute-start.11 = (bf16[512,768]{1,0:T(8,128)(2,1)}, bf16[512,768]{1,0:T(8,128)(2,1)}, u32[]{:S(2)}, u32[]{:S(2)}) collective-permute-start(bf16[512,768]{1,0:T(8,128)(2,1)} %a_ref.3), channel_id=1, source_target_pairs={{0,64},{4,68},{8,72},{12,76},{16,80},{20,84},{24,88},{28,92},{32,9... | collective-permute-start | bytes 2359304 | tf_op jit(solution)/shard_map/ppermute | solution.py:287
  79.8 68.1 %collective-permute-start.9 = (bf16[512,1024]{1,0:T(8,128)(2,1)}, bf16[512,1024]{1,0:T(8,128)(2,1)}, u32[]{:S(2)}, u32[]{:S(2)}) collective-permute-start(bf16[512,1024]{1,0:T(8,128)(2,1)} %collective-permute-done.7.a0_ref), channel_id=1, source_target_pairs={{0,1},{1,0},{2,3},{3,2},{4,5},{5,4},{6,7},{7,6},{8,9},{9,8},{10,11... | collective-permute-start | bytes 3145736 | tf_op jit(solution)/shard_map/ppermute | solution.py:281
  103.4 44.5 %collective-permute-start.10 = (bf16[512,1024]{1,0:T(8,128)(2,1)}, bf16[512,1024]{1,0:T(8,128)(2,1)}, u32[]{:S(2)}, u32[]{:S(2)}) collective-permute-start(bf16[512,1024]{1,0:T(8,128)(2,1)} %collective-permute-done.8.a1_ref), channel_id=1, source_target_pairs={{0,1},{1,0},{2,3},{3,2},{4,5},{5,4},{6,7},{7,6},{8,9},{9,8},{10,11... | collective-permute-start | bytes 3145736 | tf_op jit(solution)/shard_map/ppermute | solution.py:281
  103.4 17.0 %all-to-all-start.3 = ((f32[16,64,128]{2,1,0:T(8,128)}), f32[16,64,128]{2,1,0:T(8,128)S(1)}, u32[]{:S(2)}, u32[]{:S(2)}) async-start(f32[16,64,128]{2,1,0:T(8,128)} %bitcast.15), calls=%async_computation.3 | async-start | bytes 1048576 | tf_op jit(solution)/shard_map/all_to_all | solution.py:290
  120.4 23.2 %collective-permute-start.12 = (f32[64,128]{1,0:T(8,128)S(1)}, f32[64,128]{1,0:T(8,128)S(1)}, u32[]{:S(2)}, u32[]{:S(2)}) collective-permute-start(f32[64,128]{1,0:T(8,128)S(1)} %reduce_sum.29), channel_id=1, source_target_pairs={{0,64},{4,68},{8,72},{12,76},{16,80},{20,84},{24,88},{28,92},{32,9... | collective-permute-start | bytes 98312 | tf_op jit(solution)/shard_map/ppermute | solution.py:287
  144.3 13.4 %all-to-all-start.4 = ((bf16[16,64,128]{2,1,0:T(8,128)(2,1)}), bf16[16,64,128]{2,1,0:T(8,128)(2,1)S(1)}, u32[]{:S(2)}, u32[]{:S(2)}) async-start(bf16[16,64,128]{2,1,0:T(8,128)(2,1)} %shard_map.125), calls=%async_computation.4 | async-start | bytes 524288 | tf_op jit(solution)/shard_map/all_to_all | solution.py:290
  147.9 1.1 copy-start.8
  157.7 32.1 %copy-start.5 = (bf16[512,1024]{1,0:T(8,128)(2,1)S(1)}, bf16[512,1024]{1,0:T(8,128)(2,1)}, u32[]{:S(2)}) copy-start(bf16[512,1024]{1,0:T(8,128)(2,1)} %v_ref.5) | copy-start | bytes 3145732
  157.7 55.2 %all-to-all-start.2 = ((bf16[16,128,768]{2,1,0:T(8,128)(2,1)}), bf16[16,128,768]{2,1,0:T(8,128)(2,1)}, u32[]{:S(2)}, u32[]{:S(2)}) async-start(bf16[16,128,768]{2,1,0:T(8,128)(2,1)} %bitcast.25), calls=%async_computation.2 | async-start | bytes 6291456 | tf_op jit(solution)/shard_map/all_to_all | solution.py:290
  165.1 24.7 %collective-permute-start.5 = (bf16[512,1024]{1,0:T(8,128)(2,1)}, bf16[512,1024]{1,0:T(8,128)(2,1)}, u32[]{:S(2)}, u32[]{:S(2)}) collective-permute-start(bf16[512,1024]{1,0:T(8,128)(2,1)} %copy-done.10), channel_id=1, source_target_pairs={{0,2},{1,3},{2,0},{3,1},{4,6},{5,7},{6,4},{7,5},{8,10},{9,11},{10,... | collective-permute-start | bytes 3145736 | tf_op jit(solution)/shard_map/ppermute | solution.py:284
  167.2 37.7 %collective-permute-start.4 = (bf16[512,1024]{1,0:T(8,128)(2,1)}, bf16[512,1024]{1,0:T(8,128)(2,1)}, u32[]{:S(2)}, u32[]{:S(2)}) collective-permute-start(bf16[512,1024]{1,0:T(8,128)(2,1)} %copy-done.10), channel_id=1, source_target_pairs={{0,1},{1,0},{2,3},{3,2},{4,5},{5,4},{6,7},{7,6},{8,9},{9,8},{10,11... | collective-permute-start | bytes 3145736 | tf_op jit(solution)/shard_map/ppermute | solution.py:281
  189.8 15.2 %collective-permute-start.6 = (bf16[512,1024]{1,0:T(8,128)(2,1)}, bf16[512,1024]{1,0:T(8,128)(2,1)}, u32[]{:S(2)}, u32[]{:S(2)}) collective-permute-start(bf16[512,1024]{1,0:T(8,128)(2,1)} %collective-permute-done.5.c_ref), channel_id=1, source_target_pairs={{0,1},{1,0},{2,3},{3,2},{4,5},{5,4},{6,7},{7,6},{8,9},{9,8},{10,11... | collective-permute-start | bytes 3145736 | tf_op jit(solution)/shard_map/ppermute | solution.py:281
  189.8 1.2 copy-start.7
  191.1 1.2 copy-start.13
  192.3 1.2 copy-start.15
  193.5 11.4 %copy-start.11 = (bf16[512,1024]{1,0:T(8,128)(2,1)S(1)}, bf16[512,1024]{1,0:T(8,128)(2,1)}, u32[]{:S(2)}) copy-start(bf16[512,1024]{1,0:T(8,128)(2,1)} %copy-done.10) | copy-start | bytes 3145732

commit v2 on v1

v2 whole, which is shorter than its diff:
```python
import functools

import jax
import jax.numpy as jnp
from jax import lax
from jax.experimental import pallas as pl
from jax.experimental.pallas import tpu as pltpu
from jax.sharding import PartitionSpec as P

HD = 128
F32 = jnp.float32
BF16 = jnp.bfloat16
VMEM_LIMIT = 62 * 1024 * 1024

NT = (((1,), (1,)), ((), ()))
TN = (((0,), (0,)), ((), ()))
NN = (((1,), (0,)), ((), ()))


def dot(a, b, dims):
    return lax.dot_general(a, b, dims, preferred_element_type=F32)


def after(array, other):
    return lax.optimization_barrier((array, other))[0]


def params():
    return pltpu.CompilerParams(vmem_limit_bytes=VMEM_LIMIT)


def cost(flops, nbytes):
    return pl.CostEstimate(flops=flops, bytes_accessed=nbytes, transcendentals=0)


def state_kernel(k_ref, v_ref, s_ref):
    for head in range(2):
        cols = slice(head * HD, (head + 1) * HD)
        s_ref[head] = dot(k_ref[:, cols], v_ref[:, cols], TN)


def block_states(keys, values):
    length, inner = keys.shape
    heads = inner // HD
    rows = pl.BlockSpec((length, 2 * HD), lambda i: (0, i))
    return pl.pallas_call(
        state_kernel,
        grid=(heads // 2,),
        in_specs=[rows, rows],
        out_specs=pl.BlockSpec((2, HD, HD), lambda i: (i, 0, 0)),
        out_shape=jax.ShapeDtypeStruct((heads, HD, HD), F32),
        compiler_params=params(),
        cost_estimate=cost(2 * length * inner * HD, 4 * length * inner),
    )(keys, values)


def running_kernel(reverse, count, use_ref, p_ref, offset_ref, *rest):
    out_ref = rest[-1]
    rows, lanes = out_ref.shape[1], p_ref.shape[2]
    groups = p_ref.shape[1] // rows
    if out_ref.shape[2] > groups * lanes:
        out_ref[...] = jnp.zeros(out_ref.shape, out_ref.dtype)
    total = offset_ref[...] * use_ref[0].astype(F32)
    for step in range(count):
        place = count - 1 - step if reverse else step
        piece = total.astype(out_ref.dtype)
        for group in range(groups):
            cols = slice(group * lanes, (group + 1) * lanes)
            out_ref[place, :, cols] = piece[group * rows : (group + 1) * rows]
        if step < count - 1:
            total = total + p_ref[place]


def running_sum(pieces, offset, use, reverse, target=None):
    count, rows, lanes = pieces.shape
    in_specs = [
        pl.BlockSpec(memory_space=pltpu.SMEM),
        pl.BlockSpec(pieces.shape, lambda i: (0, 0, 0)),
        pl.BlockSpec(offset.shape, lambda i: (0, 0)),
    ]
    operands = [use, pieces, offset]
    if target is None:
        aliases = {}
        out_spec = pl.BlockSpec(pieces.shape, lambda i: (0, 0, 0))
        out_shape = jax.ShapeDtypeStruct(pieces.shape, BF16)
    else:
        aliases = {3: 0}
        in_specs.append(pl.BlockSpec(memory_space=pl.ANY))
        operands.append(target)
        last = target.shape[1] // 16 - 1
        out_spec = pl.BlockSpec((count, 16, target.shape[2]), lambda i: (0, last, 0))
        out_shape = jax.ShapeDtypeStruct(target.shape, BF16)
    return pl.pallas_call(
        functools.partial(running_kernel, reverse, count),
        grid=(1,),
        in_specs=in_specs,
        out_specs=out_spec,
        out_shape=out_shape,
        input_output_aliases=aliases,
        compiler_params=params(),
        cost_estimate=cost(count * rows * lanes, 6 * count * rows * lanes),
    )(*operands)


def head_term_kernel(sel_ref, a_ref, w_ref, o_ref):
    o_ref[...] = dot(a_ref[...], w_ref[...], NT).astype(o_ref.dtype)


def head_sum_kernel(sel_ref, a_ref, w_ref, r_ref, o_ref):
    total = dot(a_ref[...], w_ref[...], NT) + r_ref[...].astype(F32)
    o_ref[...] = total.astype(o_ref.dtype)


def head_term(place, grad, w_out, width, dtype, received=None):
    length, features = grad.shape
    tile = 512
    tiles = width // tile
    rows = pl.BlockSpec((length, tile), lambda j, s: (0, j))
    in_specs = [
        pl.BlockSpec((length, features), lambda j, s: (0, 0)),
        pl.BlockSpec((tile, features), lambda j, s: (s[0] * tiles + j, 0)),
    ]
    operands = [place.astype(jnp.int32).reshape(1), grad, w_out]
    if received is not None:
        in_specs.append(rows)
        operands.append(received)
    return pl.pallas_call(
        head_term_kernel if received is None else head_sum_kernel,
        grid_spec=pltpu.PrefetchScalarGridSpec(
            num_scalar_prefetch=1, grid=(tiles,), in_specs=in_specs, out_specs=rows
        ),
        out_shape=jax.ShapeDtypeStruct((length, width), dtype),
        compiler_params=params(),
        cost_estimate=cost(2 * length * features * width, 4 * width * features),
    )(*operands)


def score_rows(q_ref, k_ref, first, size):
    last = first + size
    scores = dot(q_ref[first:last], k_ref[:last], NT)
    return masked(scores, first)


def masked(scores, first):
    rows = lax.broadcasted_iota(jnp.int32, scores.shape, 0) + first
    cols = lax.broadcasted_iota(jnp.int32, scores.shape, 1)
    return jnp.where(cols <= rows, scores, 0.0).astype(BF16)


def sigmoid(gate):
    return 0.5 * jnp.tanh(0.5 * gate.astype(F32)) + 0.5


def head_out_kernel(
    part, half_ref, q_ref, k_ref, v_ref, g_ref, gain_ref, s_ref, mine_ref, other_ref, attn_ref
):
    length = q_ref.shape[0]
    half = HD // 2
    lane = lax.broadcasted_iota(jnp.int32, (part, HD), 1)
    upper = half_ref[0] == 1
    for first in range(0, length, part):
        last = first + part
        outs = []
        for head in range(2):
            cols = slice(head * HD, (head + 1) * HD)
            queries = q_ref[first:last, cols]
            scores = masked(dot(queries, k_ref[:last, cols], NT), first)
            attn = dot(scores, v_ref[:last, cols], NN) + dot(queries, s_ref[head], NN)
            inv = lax.rsqrt(jnp.mean(attn * attn, axis=-1, keepdims=True) + 1e-06)
            outs.append(attn * inv * gain_ref[:, cols] * sigmoid(g_ref[first:last, cols]))
            attn_ref[first:last, cols] = attn
        low = jnp.where(lane < half, outs[0], pltpu.roll(outs[1], half, 1))
        high = jnp.where(lane < half, pltpu.roll(outs[0], half, 1), outs[1])
        mine_ref[first:last] = jnp.where(upper, high, low).astype(BF16)
        other_ref[first:last] = jnp.where(upper, low, high).astype(BF16)


def head_outputs(half, queries, keys, values, gate, gain, state):
    length, inner = queries.shape
    heads = inner // HD
    rows = pl.BlockSpec((length, 2 * HD), lambda i: (0, i))
    packed_rows = pl.BlockSpec((length, HD), lambda i: (0, i))
    square = pl.BlockSpec((2, HD, HD), lambda i: (i, 0, 0))
    packed = jax.ShapeDtypeStruct((length, inner // 2), BF16)
    return pl.pallas_call(
        functools.partial(head_out_kernel, 256),
        grid=(heads // 2,),
        in_specs=[
            pl.BlockSpec(memory_space=pltpu.SMEM),
            rows,
            rows,
            rows,
            rows,
            pl.BlockSpec((1, 2 * HD), lambda i: (0, i)),
            square,
        ],
        out_specs=[packed_rows, packed_rows, rows],
        out_shape=[packed, packed, jax.ShapeDtypeStruct((length, inner), F32)],
        compiler_params=params(),
        cost_estimate=cost(4 * length * length * inner, 14 * length * inner),
    )(half, queries, keys, values, gate, gain, state)


def head_back_kernel(
    q_ref, g_ref, gain_ref, attn_ref, own_ref, far_ref, gate_ref, hi_ref, lo_ref, state_ref
):
    gain = gain_ref[...]
    attn = attn_ref[...]
    inv = lax.rsqrt(jnp.mean(attn * attn, axis=-1, keepdims=True) + 1e-06)
    sig = sigmoid(g_ref[...])
    grad = own_ref[...] + far_ref[...].astype(F32)
    unit = attn * inv
    scaled = grad * sig * gain
    product = scaled * unit
    gate_ref[...] = (product * (1.0 - sig)).astype(BF16)
    full = inv * (scaled - unit * jnp.mean(product, axis=-1, keepdims=True))
    high = full.astype(BF16)
    hi_ref[...] = high
    lo_ref[...] = (full - high.astype(F32)).astype(BF16)
    state_ref[0] = dot(q_ref[...], high, TN)


def head_back(queries, gate, gain, attn, own, far):
    length, inner = queries.shape
    heads = inner // HD
    rows = pl.BlockSpec((length, HD), lambda i: (0, i))
    square = pl.BlockSpec((1, HD, HD), lambda i: (i, 0, 0))
    wide = jax.ShapeDtypeStruct((length, inner), BF16)
    return pl.pallas_call(
        head_back_kernel,
        grid=(heads,),
        in_specs=[rows, rows, pl.BlockSpec((1, HD), lambda i: (0, i)), rows, rows, rows],
        out_specs=[rows, rows, rows, square],
        out_shape=[wide, wide, wide, jax.ShapeDtypeStruct((heads, HD, HD), F32)],
        compiler_params=params(),
        cost_estimate=cost(2 * length * HD * inner, 20 * length * inner),
    )(queries, gate, gain, attn, own, far)


def grads_kernel(
    part, q_ref, k_ref, v_ref, hi_ref, lo_ref, s_ref, dq_ref, dk_ref, dv_ref
):
    length = q_ref.shape[0]
    for first in range(0, length, part):
        last = first + part
        high = hi_ref[first:last]
        scores = score_rows(q_ref, k_ref, first, part)
        prob = dot(high, v_ref[:last], NT) + dot(lo_ref[first:last], v_ref[:last], NT)
        prob = masked(prob, first)
        dq = dot(prob, k_ref[:last], NN) + dot(high, s_ref[0], NT)
        dq_ref[first:last] = dq.astype(BF16)
        dk = dot(prob, q_ref[first:last], TN)
        dv = dot(scores, high, TN)
        if first:
            dk_ref[:first] += dk[:first]
            dv_ref[:first] += dv[:first]
        dk_ref[first:last] = dk[first:]
        dv_ref[first:last] = dv[first:]


def head_grads(queries, keys, values, high, low, state):
    length, inner = queries.shape
    heads = inner // HD
    rows = pl.BlockSpec((length, HD), lambda i: (0, i))
    square = pl.BlockSpec((1, HD, HD), lambda i: (i, 0, 0))
    wide = jax.ShapeDtypeStruct((length, inner), BF16)
    full = jax.ShapeDtypeStruct((length, inner), F32)
    return pl.pallas_call(
        functools.partial(grads_kernel, 256),
        grid=(heads,),
        in_specs=[rows, rows, rows, rows, rows, square],
        out_specs=[rows, rows, rows],
        out_shape=[wide, full, full],
        compiler_params=params(),
        cost_estimate=cost(10 * length * length * inner, 20 * length * inner),
    )(queries, keys, values, high, low, state)


def later_kernel(k_ref, v_ref, dk_ref, dv_ref, l_ref, dk_out, dv_out):
    groups = HD // (2 * l_ref.shape[1])
    for head in range(2):
        cols = slice(head * HD, (head + 1) * HD)
        later = jnp.concatenate(
            [
                l_ref[2 * head + piece, :, group * HD : (group + 1) * HD]
                for piece in range(2)
                for group in range(groups)
            ],
            axis=0,
        )
        dk_out[:, cols] = (dk_ref[:, cols] + dot(v_ref[:, cols], later, NT)).astype(BF16)
        dv_out[:, cols] = (dv_ref[:, cols] + dot(k_ref[:, cols], later, NN)).astype(BF16)


def later_grads(keys, values, key_part, value_part, parts):
    length, inner = keys.shape
    heads = inner // HD
    rows = pl.BlockSpec((length, 2 * HD), lambda i: (0, i))
    wide = jax.ShapeDtypeStruct((length, inner), BF16)
    last = parts.shape[1] // 16 - 1
    return pl.pallas_call(
        later_kernel,
        grid=(heads // 2,),
        in_specs=[
            rows,
            rows,
            rows,
            rows,
            pl.BlockSpec((4, 16, parts.shape[2]), lambda i: (i, last, 0)),
        ],
        out_specs=[rows, rows],
        out_shape=[wide, wide],
        compiler_params=params(),
        cost_estimate=cost(4 * length * HD * inner, 16 * length * inner),
    )(keys, values, key_part, value_part, parts)


def mixed_kernel(sel_ref, *refs):
    blocks, w_ref, o_ref = refs[:-2], refs[-2], refs[-1]
    half = HD // 2
    total = None
    for place, block in enumerate(blocks):
        rows = []
        for head in range(block.shape[1] // half):
            first = sel_ref[2 * place] * 1024 + sel_ref[2 * place + 1] * half + head * HD
            rows.append(w_ref[pl.ds(pl.multiple_of(first, half), half), :])
        term = dot(block[...], jnp.concatenate(rows, axis=0), NN)
        total = term if total is None else total + term
    o_ref[...] = total.astype(BF16)


def mix(sel, blocks, w_out):
    length, width = blocks[0].shape
    inner, features = w_out.shape
    tile = 256
    whole = pl.BlockSpec((length, width), lambda j, s: (0, 0))
    return pl.pallas_call(
        mixed_kernel,
        grid_spec=pltpu.PrefetchScalarGridSpec(
            num_scalar_prefetch=1,
            grid=(features // tile,),
            in_specs=[whole] * len(blocks) + [pl.BlockSpec((inner, tile), lambda j, s: (0, j))],
            out_specs=pl.BlockSpec((length, tile), lambda j, s: (0, j)),
        ),
        out_shape=jax.ShapeDtypeStruct((length, features), BF16),
        compiler_params=params(),
        cost_estimate=cost(2 * length * inner * features, 2 * inner * features),
    )(sel, *blocks, w_out)


def weight_kernel(sel_ref, a0_ref, a1_ref, b0_ref, b1_ref, m0_ref, m1_ref, *rest):
    o_ref = rest[-1]
    count, size = o_ref.shape[:2]
    for source, (first, second) in enumerate(((a0_ref, a1_ref), (b0_ref, b1_ref))):

        @pl.when(pl.program_id(0) == source)
        def _(first=first, second=second):
            total = dot(first[...], m0_ref[...], TN) + dot(second[...], m1_ref[...], TN)
            for piece in range(count):
                o_ref[piece] = total[piece * size : (piece + 1) * size].astype(BF16)


def weight_grad(sel, mine, other, grads, across, index, target=None):
    length, width = mine[0].shape
    features = grads[0].shape[1]
    size = 2 * width // across
    tile = 256
    tiles, count = width // tile, tile // size
    last = tiles - 1

    def place(i, j, s):
        return ((s[0] + i - 2 * s[0] * i) * tiles + j, index, 0)

    first_rows = pl.BlockSpec((length, tile), lambda i, j, s: (0, jnp.where(i == 0, j, last)))
    second_rows = pl.BlockSpec((length, tile), lambda i, j, s: (0, jnp.where(i == 0, 0, j)))
    whole = pl.BlockSpec((length, features), lambda i, j, s: (0, 0))
    in_specs = [first_rows, first_rows, second_rows, second_rows, whole, whole]
    operands = [sel, mine[0], mine[1], other[0], other[1], *grads]
    aliases = {}
    if target is not None:
        in_specs.append(pl.BlockSpec(memory_space=pl.ANY))
        operands.append(target)
        aliases = {len(operands) - 1: 0}
    return pl.pallas_call(
        weight_kernel,
        grid_spec=pltpu.PrefetchScalarGridSpec(
            num_scalar_prefetch=1,
            grid=(2, tiles),
            in_specs=in_specs,
            out_specs=pl.BlockSpec((count, size, features), place),
        ),
        out_shape=jax.ShapeDtypeStruct((across, 2 * size + 16, features), BF16),
        input_output_aliases=aliases,
        compiler_params=params(),
        cost_estimate=cost(8 * length * width * features, 4 * width * features),
    )(*operands)


def per_device(query_rows, key_rows, value_rows, gate_input, norm_gain, w_out, mixed_grad):
    length, inner_dev = query_rows.shape
    heads_dev = inner_dev // HD
    features = w_out.shape[1]
    planes, across = 2, 16
    ctx, fsdp = lax.axis_index("ctx"), lax.axis_index("fsdp")
    y_lo = ctx // across
    y_hi, core = fsdp // 2, fsdp % 2
    groups = [[y * across + i for i in range(across)] for y in range(planes)]
    core_swap = [(0, 1), (1, 0), (2, 3), (3, 2)]
    hi_swap = [(0, 2), (1, 3), (2, 0), (3, 1)]
    lo_swap = [(i, (i + across) % (2 * across)) for i in range(2 * across)]

    def swap_core(array):
        return lax.ppermute(array, "fsdp", core_swap)

    def swap_hi(array):
        return lax.ppermute(array, "fsdp", hi_swap)

    def swap_lo(array):
        return lax.ppermute(array, "ctx", lo_swap)

    def exchange(array):
        return lax.all_to_all(array, "ctx", 0, 0, axis_index_groups=groups)

    def sums_before(pieces, offset, reverse, target=None):
        use = (y_lo == (0 if reverse else 1)).astype(jnp.int32).reshape(1)
        return running_sum(pieces, offset, use, reverse, target)

    def split_states(local):
        return exchange(local.reshape(across, heads_dev * HD // across, HD))

    gain = norm_gain.reshape(1, inner_dev)
    peer, far = fsdp + 1 - 2 * core, (fsdp + 2) % 4
    far_peer = (peer + 2) % 4

    grad_pair = swap_lo(mixed_grad)
    local_state = block_states(key_rows, value_rows)
    pieces = split_states(local_state)
    far_sent = head_term(after(far_peer, local_state), mixed_grad, w_out, inner_dev, BF16)
    far_got = swap_core(far_sent)
    far_part = head_term(far, mixed_grad, w_out, inner_dev, BF16, far_got)
    own_sent = head_term(after(peer, far_got), mixed_grad, w_out, inner_dev, BF16)
    own_got = swap_core(own_sent)
    total = jnp.sum(after(after(pieces, far_part), own_sent), axis=0)
    offset = swap_lo(total)
    grad_far = swap_hi(after(after(far_part, offset), grad_pair))
    sums = sums_before(pieces, offset, False)
    grad_own = head_term(after(fsdp, sums), mixed_grad, w_out, inner_dev, F32, own_got)
    prev_state = exchange(sums).reshape(heads_dev, HD, HD)

    half = y_lo.astype(jnp.int32).reshape(1)
    out, out_other, attn = head_outputs(
        half, after(query_rows, grad_own), key_rows, value_rows, gate_input, gain, prev_state
    )
    gate_grad, high, low, grad_state = head_back(
        query_rows, gate_input, gain, attn, grad_own, grad_far
    )
    later_pieces = split_states(grad_state)
    later_total = jnp.sum(later_pieces, axis=0)

    across_y = []
    for place in range(2 * across):
        for part in range(4):
            target = ((place + across) % (2 * across)) * 4 + (part + 2) % 4
            across_y.append((place * 4 + part, target))
    out_pair = swap_lo(out_other)
    out_far = swap_hi(out)
    out_far_pair = lax.ppermute(out_other, ("ctx", "fsdp"), across_y)
    out_core, out_pair_core = swap_core(out), swap_core(after(out_pair, grad_state))
    select = core.astype(jnp.int32).reshape(1)
    grads = [mixed_grad, grad_pair]
    out_far_core, out_far_pair_core = swap_core(out_far), swap_core(out_far_pair)
    weight = weight_grad(
        after(select, later_total), [out, out_pair], [out_core, out_pair_core], grads, across, 0
    )
    weight = weight_grad(
        select, [out_far, out_far_pair], [out_far_core, out_far_pair_core], grads, across, 1,
        weight,
    )
    later_offset = swap_lo(later_total)
    weight = sums_before(later_pieces, later_offset, True, weight)
    parts = exchange(weight)
    far_other = swap_hi(after(out_other, later_offset))
    query_grad, key_part, value_part = head_grads(
        after(query_rows, weight), key_rows, value_rows, high, low, prev_state
    )

    blocks = [out, out_other, out_core, swap_core(after(out_other, later_offset))]
    blocks += [out_far, far_other, out_far_core, swap_core(far_other)]
    order = []
    for heads in (fsdp, peer, far, far_peer):
        order += [heads, y_lo, heads, 1 - y_lo]
    order = jnp.stack(order).astype(jnp.int32)
    mixed = mix(after(order, query_grad), blocks, w_out)

    parts = after(parts, mixed)
    key_grad, value_grad = later_grads(key_rows, value_rows, key_part, value_part, parts)
    size = 2 * inner_dev // (2 * across)
    near_sum = jnp.sum(parts[:, :size].astype(F32), axis=0)
    far_sum = jnp.sum(parts[:, size : 2 * size].astype(F32), axis=0)
    keeps = y_hi == y_lo
    kept = jnp.where(keeps, near_sum, far_sum)
    received = swap_lo(jnp.where(keeps, far_sum, near_sum))
    w_out_grad = jnp.where(
        y_lo == 0,
        jnp.concatenate([kept, received], axis=0),
        jnp.concatenate([received, kept], axis=0),
    )
    return (mixed, w_out_grad, query_grad, key_grad, value_grad, gate_grad)


def solution(mesh):
    return jax.shard_map(
        per_device,
        mesh=mesh,
        in_specs=(
            P("ctx", "fsdp"),
            P("ctx", "fsdp"),
            P("ctx", "fsdp"),
            P("ctx", "fsdp"),
            P("fsdp"),
            P(None, "fsdp"),
            P("ctx", "fsdp"),
        ),
        out_specs=(
            P("ctx", "fsdp"),
            P("ctx", "fsdp"),
            P("ctx", "fsdp"),
            P("ctx", "fsdp"),
            P("ctx", "fsdp"),
            P("ctx", "fsdp"),
        ),
        check_vma=False,
    )
```

time: 219 us -> 172 us (0.79)
  Pallas kernels: 52.5 us -> 73.3 us
  starting transfers between devices: 55.5 us -> 35.1 us
  blocking collectives: 19.2 us -> 0 us
  waiting for transfers between devices: 70.4 us -> 53.4 us
  local copies, waits for them, and re-layouts: 11.9 us -> 5.35 us
  other arithmetic: 5.75 us -> 3.22 us
    ppermute x2 -> x1, waiting for transfers between devices: 23.6 us -> 2.46 us  [per_device(): out_far_pair = lax.ppermute(out_other, ('ctx', 'fsdp'), across_y)]
    all_to_all x1 -> x0, blocking collectives: 19.2 us -> none  [exchange(): return lax.all_to_all(array, 'ctx', 0, 0, axis_index_groups=groups)]
    pallas_call x6 -> x10, Pallas kernels: 24.5 us -> 42 us  [the longest x4 14.3 us: head_term(): pl.pallas_call(head_term_kernel if received is None else head_sum_kernel,...]
    all_to_all x4, waiting for transfers between devices: 14.6 us -> 30.4 us  [exchange(): return lax.all_to_all(array, 'ctx', 0, 0, axis_index_groups=groups)]
    ppermute x3 -> x5, starting transfers between devices: 21.6 us -> 6.58 us  [swap_lo(): return lax.ppermute(array, 'ctx', lo_swap)]
    ppermute x2 -> x3, waiting for transfers between devices: 22.6 us -> 15.7 us  [swap_hi(): return lax.ppermute(array, 'fsdp', hi_swap)]
    ppermute x6 -> x8, waiting for transfers between devices: 6.41 us -> 1.28 us  [swap_core(): return lax.ppermute(array, 'fsdp', core_swap)]
    dynamic_slice x1 -> x0, local copies, waits for them, and re-layouts: 3.74 us -> none  [per_device(): lax.dynamic_index_in_dim(w_rows, 1 - core, 1, False)]
  transfers between devices with their start and end apart: 17 -> 21, of which waited for: 7 -> 10; matrix products, arithmetic and copies ran while one was open for 1% -> 0% of each run, Pallas kernels for 17% -> 37%
where the time goes in v2:
time: 172 us; the launch traced here: 171 us
  Pallas kernels  73.3 us (43%)
  waiting for transfers between devices  53.4 us (31%)
  starting transfers between devices  35.1 us (20%)
  local copies, waits for them, and re-layouts  5.35 us (3%)
  other arithmetic  3.22 us (2%)
    all_to_all x4, waiting for transfers between devices, exchange(): return lax.all_to_all(array, 'ctx', 0, 0, axis_index_groups=groups)  30.4 us
    all_to_all x4, starting transfers between devices, exchange(): return lax.all_to_all(array, 'ctx', 0, 0, axis_index_groups=groups)  19.8 us
    ppermute x3, waiting for transfers between devices, swap_hi(): return lax.ppermute(array, 'fsdp', hi_swap)  15.7 us
    pallas_call x4, Pallas kernels, head_term(): pl.pallas_call(head_term_kernel if received is None else head_sum_kernel,...  14.3 us
    pallas_call x1, Pallas kernels, head_grads(): pl.pallas_call(functools.partial(grads_kernel, 256), grid=(heads,), in_sp...  11.6 us
    pallas_call x2, Pallas kernels, weight_grad(): pl.pallas_call(weight_kernel, grid_spec=pltpu.PrefetchScalarGridSpec(num_...  11.3 us
    pallas_call x1, Pallas kernels, mix(): pl.pallas_call(mixed_kernel, grid_spec=pltpu.PrefetchScalarGridSpec(num_s...  8.39 us
    pallas_call x1, Pallas kernels, head_back(): pl.pallas_call(head_back_kernel, grid=(heads,), in_specs=[rows, rows, pl....  8.27 us
  transfers between devices with their start and end apart: 21, of which 10 were waited for; matrix products, arithmetic and copies ran while one was open for 0% of the time, Pallas kernels for 37%

profile of v2, /device:TPU:0, one launch (start us, length us, event | category | flops | bytes accessed | tf_op | source)
XLA Modules:
  0.0 171.1 jit_solution(5264578506064316991)
XLA Ops:
  0.7 4.0 %shard_map.118 = f32[8,128,128]{2,1,0:T(8,128)} custom-call(bf16[512,1024]{1,0:T(8,128)(2,1)} %k_ref.7, bf16[512,1024]{1,0:T(8,128)(2,1)} %v_ref.7), custom_call_target="tpu_custom_call" | custom-call | flops 134217728 | bytes 2097152 | tf_op jit(solution)/shard_map/pallas_call | solution.py:46
  4.6 3.5 %shard_map.119 = bf16[512,1024]{1,0:T(8,128)(2,1)} custom-call(s32[1]{0:T(128)} %bitcast.10.sel_ref, bf16[512,768]{1,0:T(8,128)(2,1)} %m0_ref.3, bf16[4096,768]{1,0:T(8,128)(2,1)} %refs_8_.1), custom_call_target="tpu_custom_call" | custom-call | flops 805306368 | bytes 3145728 | tf_op jit(solution)/shard_map/pallas_call | solution.py:127
  8.1 1.7 %collective-permute-start.3 = (bf16[512,768]{1,0:T(8,128)(2,1)S(1)}, bf16[512,768]{1,0:T(8,128)(2,1)}, u32[]{:S(2)}, u32[]{:S(2)}) collective-permute-start(bf16[512,768]{1,0:T(8,128)(2,1)S(1)} %copy-done), channel_id=1, source_target_pairs={{0,64},{4,68},{8,72},{12,76},{16,80},{20,84},{24,88},{28,92},{32,9... | collective-permute-start | bytes 2359304 | tf_op jit(solution)/shard_map/ppermute | solution.py:419
  9.9 1.3 collective-permute-done.r_ref
  11.1 3.4 %shard_map.121 = bf16[512,1024]{1,0:T(8,128)(2,1)} custom-call(s32[1]{0:T(128)} %bitcast.11.sel_ref, bf16[512,768]{1,0:T(8,128)(2,1)} %m0_ref.3, bf16[4096,768]{1,0:T(8,128)(2,1)} %refs_8_.1), custom_call_target="tpu_custom_call" | custom-call | flops 805306368 | bytes 3145728 | tf_op jit(solution)/shard_map/pallas_call | solution.py:127
  14.5 0.1 collective-permute-start.2
  14.7 8.0 %all-to-all-start = ((f32[16,64,128]{2,1,0:T(8,128)}), f32[16,64,128]{2,1,0:T(8,128)S(1)}, u32[]{:S(2)}, u32[]{:S(2)}) async-start(f32[16,64,128]{2,1,0:T(8,128)} %bitcast.9), calls=%async_computation | async-start | bytes 1048576 | tf_op jit(solution)/shard_map/all_to_all | solution.py:422
  22.6 3.6 %shard_map.120 = bf16[512,1024]{1,0:T(8,128)(2,1)} custom-call(s32[1]{0:T(128)} %bitcast.4.sel_ref, bf16[512,768]{1,0:T(8,128)(2,1)} %m0_ref.3, bf16[4096,768]{1,0:T(8,128)(2,1)} %refs_8_.1, bf16[512,1024]{1,0:T(8,128)(2,1)} %collective-permute-done.r_ref), custom_call_target="tpu_custom_call" | custom-call | flops 805306368 | bytes 3145728 | tf_op jit(solution)/shard_map/pallas_call | solution.py:127
  26.2 8.4 %all-to-all-done.p_ref = f32[16,64,128]{2,1,0:T(8,128)S(1)} async-done(((f32[16,64,128]{2,1,0:T(8,128)}), f32[16,64,128]{2,1,0:T(8,128)S(1)}, u32[]{:S(2)}, u32[]{:S(2)}) %all-to-all-start) | async-done | bytes 524320 | tf_op jit(solution)/shard_map/all_to_all | solution.py:422
  34.7 1.7 collective-permute-start.1
  36.3 2.3 %collective-permute-done.1.offset_ref = f32[64,128]{1,0:T(8,128)S(1)} collective-permute-done((f32[64,128]{1,0:T(8,128)S(1)}, f32[64,128]{1,0:T(8,128)S(1)}, u32[]{:S(2)}, u32[]{:S(2)}) %collective-permute-start.1) | collective-permute-done | bytes 32800 | tf_op jit(solution)/shard_map/ppermute | solution.py:419
  38.7 3.2 %collective-permute-start.4 = (bf16[512,1024]{1,0:T(8,128)(2,1)}, bf16[512,1024]{1,0:T(8,128)(2,1)S(1)}, u32[]{:S(2)}, u32[]{:S(2)}) collective-permute-start(bf16[512,1024]{1,0:T(8,128)(2,1)} %shard_map.120), channel_id=1, source_target_pairs={{0,2},{1,3},{2,0},{3,1},{4,6},{5,7},{6,4},{7,5},{8,10},{9,11},{10,... | collective-permute-start | bytes 3145736 | tf_op jit(solution)/shard_map/ppermute | solution.py:416
  41.9 1.8 %shard_map.122 = bf16[16,64,128]{2,1,0:T(8,128)(2,1)} custom-call(s32[1]{0:T(128)} %bitcast.8.use_ref, f32[16,64,128]{2,1,0:T(8,128)} %copy-done.1, f32[64,128]{1,0:T(8,128)} %copy-done.8), custom_call_target="tpu_custom_call" | custom-call | flops 131072 | bytes 786432 | tf_op jit(solution)/shard_map/pallas_call | solution.py:93
  43.7 3.5 %all-to-all-start.1 = ((bf16[16,64,128]{2,1,0:T(8,128)(2,1)}), bf16[16,64,128]{2,1,0:T(8,128)(2,1)S(1)}, u32[]{:S(2)}, u32[]{:S(2)}) async-start(bf16[16,64,128]{2,1,0:T(8,128)(2,1)} %shard_map.122), calls=%async_computation.1 | async-start | bytes 524288 | tf_op jit(solution)/shard_map/all_to_all | solution.py:422
  47.2 3.8 %shard_map.123.own_ref = f32[512,1024]{1,0:T(8,128)} custom-call(s32[1]{0:T(128)} %bitcast.12.sel_ref, bf16[512,768]{1,0:T(8,128)(2,1)} %m0_ref.3, bf16[4096,768]{1,0:T(8,128)(2,1)} %refs_8_.1, bf16[512,1024]{1,0:T(8,128)(2,1)} %collective-permute-done.2.r_ref), custom_call_target="tpu_custom_call" | custom-call | flops 805306368 | bytes 3145728 | tf_op jit(solution)/shard_map/pallas_call | solution.py:127
  51.0 4.6 %all-to-all-done.1 = bf16[16,64,128]{2,1,0:T(8,128)(2,1)S(1)} async-done(((bf16[16,64,128]{2,1,0:T(8,128)(2,1)}), bf16[16,64,128]{2,1,0:T(8,128)(2,1)S(1)}, u32[]{:S(2)}, u32[]{:S(2)}) %all-to-all-start.1) | async-done | bytes 262176 | tf_op jit(solution)/shard_map/all_to_all | solution.py:422
  55.6 0.7 copy-done.4
  56.4 6.8 %shard_map.124 = (bf16[512,512]{1,0:T(8,128)(2,1)}, bf16[512,512]{1,0:T(8,128)(2,1)}, f32[512,1024]{1,0:T(8,128)}) custom-call(s32[1]{0:T(128)} %bitcast.1.half_ref, bf16[512,1024]{1,0:T(8,128)(2,1)} %q_ref.3, bf16[512,1024]{1,0:T(8,128)(2,1)} %k_ref.7, bf16[512,1024]{1,0:T(8,128)(2,1)} %v_ref.7, bf16[512,1024]{1,0:T(8,128)(2,1)} %g_ref.3, ...), custom_call_target="tpu_custom_call" | custom-call | flops 1073741824 | bytes 7340032 | tf_op jit(solution)/shard_map/pallas_call | solution.py:185
  63.2 1.0 collective-permute-start.10
  64.1 1.5 collective-permute-start.6
  65.7 2.2 %collective-permute-start.7 = (bf16[512,512]{1,0:T(8,128)(2,1)}, bf16[512,512]{1,0:T(8,128)(2,1)}, u32[]{:S(2)}, u32[]{:S(2)}) collective-permute-start(bf16[512,512]{1,0:T(8,128)(2,1)} %get-tuple-element.51.refs_1_), channel_id=1, source_target_pairs={{0,66},{1,67},{2,64},{3,65},{4,70},{5,71},{6,68},{7,69},{8,74},{9,... | collective-permute-start | bytes 1572872 | tf_op jit(solution)/shard_map/ppermute | solution.py:467
  67.9 1.0 copy-done.3
  68.8 8.3 %shard_map.125 = (bf16[512,1024]{1,0:T(8,128)(2,1)}, bf16[512,1024]{1,0:T(8,128)(2,1)}, bf16[512,1024]{1,0:T(8,128)(2,1)}, f32[8,128,128]{2,1,0:T(8,128)}) custom-call(bf16[512,1024]{1,0:T(8,128)(2,1)} %q_ref.3, bf16[512,1024]{1,0:T(8,128)(2,1)} %g_ref.3, f32[1,1024]{1,0:T(1,128)} %bitcast.20, f32[512,1024]{1,0:T(8,128)} %get-tuple-element.38.attn_ref, ...), custom_call_target="tpu_custom_call" | custom-call | flops 134217728 | bytes 10485760 | tf_op jit(solution)/shard_map/pallas_call | solution.py:229
  77.1 1.2 collective-permute-done.10.a1_ref
  78.3 3.7 %all-to-all-start.2 = ((f32[16,64,128]{2,1,0:T(8,128)}), f32[16,64,128]{2,1,0:T(8,128)S(1)}, u32[]{:S(2)}, u32[]{:S(2)}) async-start(f32[16,64,128]{2,1,0:T(8,128)} %bitcast.18), calls=%async_computation.2 | async-start | bytes 1048576 | tf_op jit(solution)/shard_map/all_to_all | solution.py:422
  82.0 3.6 %collective-permute-done.6.a0_ref.refs_4_ = bf16[512,512]{1,0:T(8,128)(2,1)} collective-permute-done((bf16[512,512]{1,0:T(8,128)(2,1)}, bf16[512,512]{1,0:T(8,128)(2,1)}, u32[]{:S(2)}, u32[]{:S(2)}) %collective-permute-start.6) | collective-permute-done | bytes 524320 | tf_op jit(solution)/shard_map/ppermute | solution.py:416
  85.6 2.5 %collective-permute-done.7.a1_ref = bf16[512,512]{1,0:T(8,128)(2,1)} collective-permute-done((bf16[512,512]{1,0:T(8,128)(2,1)}, bf16[512,512]{1,0:T(8,128)(2,1)}, u32[]{:S(2)}, u32[]{:S(2)}) %collective-permute-start.7) | collective-permute-done | bytes 524320 | tf_op jit(solution)/shard_map/ppermute | solution.py:467
  88.0 6.3 %all-to-all-done.2.p_ref = f32[16,64,128]{2,1,0:T(8,128)S(1)} async-done(((f32[16,64,128]{2,1,0:T(8,128)}), f32[16,64,128]{2,1,0:T(8,128)S(1)}, u32[]{:S(2)}, u32[]{:S(2)}) %all-to-all-start.2) | async-done | bytes 524320 | tf_op jit(solution)/shard_map/all_to_all | solution.py:422
  94.4 1.1 collective-permute-start.5
  95.4 0.8 copy-done.5
  96.2 0.8 copy-done.6
  97.0 5.6 %shard_map.126.rest_0_ = bf16[16,144,768]{2,1,0:T(8,128)(2,1)} custom-call(s32[1]{0:T(128)} %bitcast.15.sel_ref, bf16[512,512]{1,0:T(8,128)(2,1)} %get-tuple-element.42.a0_ref.refs_0_, bf16[512,512]{1,0:T(8,128)(2,1)} %collective-permute-done.10.a1_ref, bf16[512,512]{1,0:T(8,128)(2,1)} %copy-done.5, bf16[512,512]{1,0:T(8,128)(2,1)} %copy-done.6, ...), custom_call_target="tpu_custom_call" | custom-call | flops 1610612736 | bytes 1572864 | tf_op jit(solution)/shard_map/pallas_call | solution.py:384
  102.7 5.6 %shard_map.127.rest_0_ = bf16[16,144,768]{2,1,0:T(8,128)(2,1)} custom-call(s32[1]{0:T(128)} %bitcast.15.sel_ref, bf16[512,512]{1,0:T(8,128)(2,1)} %collective-permute-done.6.a0_ref.refs_4_, bf16[512,512]{1,0:T(8,128)(2,1)} %collective-permute-done.7.a1_ref, bf16[512,512]{1,0:T(8,128)(2,1)} %collective-permute-done.8.b0_ref.refs_6_, ...), custom_call_target="tpu_custom_call", output_to_operand_aliasing={{}: (7, {})} | custom-call | flops 1610612736 | bytes 1572864 | tf_op jit(solution)/shard_map/pallas_call | solution.py:384
  108.3 0.6 copy-done.7
  108.9 1.8 %shard_map.128 = bf16[16,144,768]{2,1,0:T(8,128)(2,1)} custom-call(s32[1]{0:T(128)} %bitcast.6.use_ref, f32[16,64,128]{2,1,0:T(8,128)} %copy-done.2, f32[64,128]{1,0:T(8,128)} %copy-done.7, bf16[16,144,768]{2,1,0:T(8,128)(2,1)} %shard_map.127.rest_0_), custom_call_target="tpu_custom_call", output_to_operand_aliasing={{}: (3, {})} | custom-call | flops 131072 | bytes 786432 | tf_op jit(solution)/shard_map/pallas_call | solution.py:93
  110.8 4.6 %all-to-all-start.3 = ((bf16[16,144,768]{2,1,0:T(8,128)(2,1)}), bf16[16,144,768]{2,1,0:T(8,128)(2,1)}, u32[]{:S(2)}, u32[]{:S(2)}) async-start(bf16[16,144,768]{2,1,0:T(8,128)(2,1)} %shard_map.128), calls=%async_computation.3 | async-start | bytes 7077888 | tf_op jit(solution)/shard_map/all_to_all | solution.py:422
  115.4 1.6 collective-permute-start.14
  117.0 12.1 %collective-permute-done.14.refs_5_ = bf16[512,512]{1,0:T(8,128)(2,1)S(1)} collective-permute-done((bf16[512,512]{1,0:T(8,128)(2,1)S(1)}, bf16[512,512]{1,0:T(8,128)(2,1)S(1)}, u32[]{:S(2)}, u32[]{:S(2)}) %collective-permute-start.14) | collective-permute-done | bytes 524320 | tf_op jit(solution)/shard_map/ppermute | solution.py:416
  129.2 0.7 stack.37.sel_ref
  129.9 11.6 %shard_map.129 = (bf16[512,1024]{1,0:T(8,128)(2,1)}, f32[512,1024]{1,0:T(8,128)}, f32[512,1024]{1,0:T(8,128)}) custom-call(bf16[512,1024]{1,0:T(8,128)(2,1)} %q_ref.3, bf16[512,1024]{1,0:T(8,128)(2,1)} %k_ref.7, bf16[512,1024]{1,0:T(8,128)(2,1)} %v_ref.7, bf16[512,1024]{1,0:T(8,128)(2,1)} %get-tuple-element.47.hi_ref, ...), custom_call_target="tpu_custom_call" | custom-call | flops 2684354560 | bytes 10485760 | tf_op jit(solution)/shard_map/pallas_call | solution.py:268
  141.5 0.0 copy-start.11
  141.5 0.8 copy-done.11
  142.3 8.4 %shard_map.130 = bf16[512,768]{1,0:T(8,128)(2,1)} custom-call(s32[16]{0:T(128)} %stack.37.sel_ref, bf16[512,512]{1,0:T(8,128)(2,1)} %get-tuple-element.42.a0_ref.refs_0_, bf16[512,512]{1,0:T(8,128)(2,1)} %get-tuple-element.51.refs_1_, bf16[512,512]{1,0:T(8,128)(2,1)} %copy-done.5, bf16[512,512]{1,0:T(8,128)(2,1)} %copy-done.11, ...), custom_call_target="tpu_custom_call" | custom-call | flops 3221225472 | bytes 6291456 | tf_op jit(solution)/shard_map/pallas_call | solution.py:337
  150.7 11.1 %all-to-all-done.3.l_ref = bf16[16,144,768]{2,1,0:T(8,128)(2,1)} async-done(((bf16[16,144,768]{2,1,0:T(8,128)(2,1)}), bf16[16,144,768]{2,1,0:T(8,128)(2,1)}, u32[]{:S(2)}, u32[]{:S(2)}) %all-to-all-start.3) | async-done | bytes 3538976 | tf_op jit(solution)/shard_map/all_to_all | solution.py:422
  161.7 2.3 %convert_reduce_fusion.1 = (f32[64,768]{1,0:T(8,128)S(1)}, f32[64,768]{1,0:T(8,128)S(1)}) fusion(bf16[16,144,768]{2,1,0:T(8,128)(2,1)} %all-to-all-done.3.l_ref), kind=kLoop, calls=%fused_computation.1 | loop fusion | flops 3047424 | bytes 3538944 | tf_op jit(solution)/shard_map/reduce_sum | solution.py:498
  164.1 1.2 collective-permute-start.16
  165.3 5.1 %shard_map.131 = (bf16[512,1024]{1,0:T(8,128)(2,1)}, bf16[512,1024]{1,0:T(8,128)(2,1)}) custom-call(bf16[512,1024]{1,0:T(8,128)(2,1)} %k_ref.7, bf16[512,1024]{1,0:T(8,128)(2,1)} %v_ref.7, f32[512,1024]{1,0:T(8,128)} %get-tuple-element.53.dk_ref, f32[512,1024]{1,0:T(8,128)} %get-tuple-element.54.dv_ref, bf16[16,144,768]{2,1,0:T(8,128)(2,1)} %all-to-all-done.3.l_ref), custom_call_target="tpu_custom_call" | custom-call | flops 268435456 | bytes 8388608 | tf_op jit(solution)/shard_map/pallas_call | solution.py:301
  170.4 0.8 maximum_select_fusion
  (38 shorter events, 0.2 us)
Async XLA Ops:
  4.6 3.5 %copy-start = (bf16[512,768]{1,0:T(8,128)(2,1)S(1)}, bf16[512,768]{1,0:T(8,128)(2,1)}, u32[]{:S(2)}) copy-start(bf16[512,768]{1,0:T(8,128)(2,1)} %m0_ref.3) | copy-start | bytes 2359300
  8.1 3.0 %collective-permute-start = (bf16[512,1024]{1,0:T(8,128)(2,1)}, bf16[512,1024]{1,0:T(8,128)(2,1)}, u32[]{:S(2)}, u32[]{:S(2)}) collective-permute-start(bf16[512,1024]{1,0:T(8,128)(2,1)} %shard_map.119), channel_id=1, source_target_pairs={{0,1},{1,0},{2,3},{3,2},{4,5},{5,4},{6,7},{7,6},{8,9},{9,8},{10,11... | collective-permute-start | bytes 3145736 | tf_op jit(solution)/shard_map/ppermute | solution.py:413
  8.1 30.6 %collective-permute-start.3 = (bf16[512,768]{1,0:T(8,128)(2,1)S(1)}, bf16[512,768]{1,0:T(8,128)(2,1)}, u32[]{:S(2)}, u32[]{:S(2)}) collective-permute-start(bf16[512,768]{1,0:T(8,128)(2,1)S(1)} %copy-done), channel_id=1, source_target_pairs={{0,64},{4,68},{8,72},{12,76},{16,80},{20,84},{24,88},{28,92},{32,9... | collective-permute-start | bytes 2359304 | tf_op jit(solution)/shard_map/ppermute | solution.py:419
  14.5 32.7 %collective-permute-start.2 = (bf16[512,1024]{1,0:T(8,128)(2,1)}, bf16[512,1024]{1,0:T(8,128)(2,1)}, u32[]{:S(2)}, u32[]{:S(2)}) collective-permute-start(bf16[512,1024]{1,0:T(8,128)(2,1)} %shard_map.121), channel_id=1, source_target_pairs={{0,1},{1,0},{2,3},{3,2},{4,5},{5,4},{6,7},{7,6},{8,9},{9,8},{10,11... | collective-permute-start | bytes 3145736 | tf_op jit(solution)/shard_map/ppermute | solution.py:413
  14.7 20.0 %all-to-all-start = ((f32[16,64,128]{2,1,0:T(8,128)}), f32[16,64,128]{2,1,0:T(8,128)S(1)}, u32[]{:S(2)}, u32[]{:S(2)}) async-start(f32[16,64,128]{2,1,0:T(8,128)} %bitcast.9), calls=%async_computation | async-start | bytes 1048576 | tf_op jit(solution)/shard_map/all_to_all | solution.py:422
  34.6 7.2 %copy-start.1 = (f32[16,64,128]{2,1,0:T(8,128)}, f32[16,64,128]{2,1,0:T(8,128)S(1)}, u32[]{:S(2)}) copy-start(f32[16,64,128]{2,1,0:T(8,128)S(1)} %all-to-all-done.p_ref) | copy-start | bytes 1572868
  34.7 4.0 %collective-permute-start.1 = (f32[64,128]{1,0:T(8,128)S(1)}, f32[64,128]{1,0:T(8,128)S(1)}, u32[]{:S(2)}, u32[]{:S(2)}) collective-permute-start(f32[64,128]{1,0:T(8,128)S(1)} %reduce_sum.36), channel_id=1, source_target_pairs={{0,64},{4,68},{8,72},{12,76},{16,80},{20,84},{24,88},{28,92},{32,9... | collective-permute-start | bytes 98312 | tf_op jit(solution)/shard_map/ppermute | solution.py:419
  38.7 3.2 %copy-start.8 = (f32[64,128]{1,0:T(8,128)}, f32[64,128]{1,0:T(8,128)S(1)}, u32[]{:S(2)}) copy-start(f32[64,128]{1,0:T(8,128)S(1)} %collective-permute-done.1.offset_ref) | copy-start | bytes 98308
  38.7 29.2 %collective-permute-start.4 = (bf16[512,1024]{1,0:T(8,128)(2,1)}, bf16[512,1024]{1,0:T(8,128)(2,1)S(1)}, u32[]{:S(2)}, u32[]{:S(2)}) collective-permute-start(bf16[512,1024]{1,0:T(8,128)(2,1)} %shard_map.120), channel_id=1, source_target_pairs={{0,2},{1,3},{2,0},{3,1},{4,6},{5,7},{6,4},{7,5},{8,10},{9,11},{10,... | collective-permute-start | bytes 3145736 | tf_op jit(solution)/shard_map/ppermute | solution.py:416
  43.7 12.0 %all-to-all-start.1 = ((bf16[16,64,128]{2,1,0:T(8,128)(2,1)}), bf16[16,64,128]{2,1,0:T(8,128)(2,1)S(1)}, u32[]{:S(2)}, u32[]{:S(2)}) async-start(bf16[16,64,128]{2,1,0:T(8,128)(2,1)} %shard_map.122), calls=%async_computation.1 | async-start | bytes 524288 | tf_op jit(solution)/shard_map/all_to_all | solution.py:422
  55.6 0.7 copy-start.4
  63.2 15.2 %collective-permute-start.10 = (bf16[512,512]{1,0:T(8,128)(2,1)}, bf16[512,512]{1,0:T(8,128)(2,1)}, u32[]{:S(2)}, u32[]{:S(2)}) collective-permute-start(bf16[512,512]{1,0:T(8,128)(2,1)} %get-tuple-element.51.refs_1_), channel_id=1, source_target_pairs={{0,64},{4,68},{8,72},{12,76},{16,80},{20,84},{24,88},{28,92},{32,9... | collective-permute-start | bytes 1572872 | tf_op jit(solution)/shard_map/ppermute | solution.py:419
  64.1 21.4 %collective-permute-start.6 = (bf16[512,512]{1,0:T(8,128)(2,1)}, bf16[512,512]{1,0:T(8,128)(2,1)}, u32[]{:S(2)}, u32[]{:S(2)}) collective-permute-start(bf16[512,512]{1,0:T(8,128)(2,1)} %get-tuple-element.42.a0_ref.refs_0_), channel_id=1, source_target_pairs={{0,2},{1,3},{2,0},{3,1},{4,6},{5,7},{6,4},{7,5},{8,10},{9,11},{10,... | collective-permute-start | bytes 1572872 | tf_op jit(solution)/shard_map/ppermute | solution.py:416
  65.7 22.4 %collective-permute-start.7 = (bf16[512,512]{1,0:T(8,128)(2,1)}, bf16[512,512]{1,0:T(8,128)(2,1)}, u32[]{:S(2)}, u32[]{:S(2)}) collective-permute-start(bf16[512,512]{1,0:T(8,128)(2,1)} %get-tuple-element.51.refs_1_), channel_id=1, source_target_pairs={{0,66},{1,67},{2,64},{3,65},{4,70},{5,71},{6,68},{7,69},{8,74},{9,... | collective-permute-start | bytes 1572872 | tf_op jit(solution)/shard_map/ppermute | solution.py:467
  67.9 27.6 %collective-permute-start.11 = (bf16[512,512]{1,0:T(8,128)(2,1)}, bf16[512,512]{1,0:T(8,128)(2,1)S(1)}, u32[]{:S(2)}, u32[]{:S(2)}) collective-permute-start(bf16[512,512]{1,0:T(8,128)(2,1)} %get-tuple-element.42.a0_ref.refs_0_), channel_id=1, source_target_pairs={{0,1},{1,0},{2,3},{3,2},{4,5},{5,4},{6,7},{7,6},{8,9},{9,8},{10,11... | collective-permute-start | bytes 1572872 | tf_op jit(solution)/shard_map/ppermute | solution.py:413
  67.9 1.0 copy-start.3
  78.3 17.1 %collective-permute-start.12 = (bf16[512,512]{1,0:T(8,128)(2,1)}, bf16[512,512]{1,0:T(8,128)(2,1)S(1)}, u32[]{:S(2)}, u32[]{:S(2)}) collective-permute-start(bf16[512,512]{1,0:T(8,128)(2,1)} %collective-permute-done.10.a1_ref), channel_id=1, source_target_pairs={{0,1},{1,0},{2,3},{3,2},{4,5},{5,4},{6,7},{7,6},{8,9},{9,8},{10,11... | collective-permute-start | bytes 1572872 | tf_op jit(solution)/shard_map/ppermute | solution.py:413
  78.3 16.0 %all-to-all-start.2 = ((f32[16,64,128]{2,1,0:T(8,128)}), f32[16,64,128]{2,1,0:T(8,128)S(1)}, u32[]{:S(2)}, u32[]{:S(2)}) async-start(f32[16,64,128]{2,1,0:T(8,128)} %bitcast.18), calls=%async_computation.2 | async-start | bytes 1048576 | tf_op jit(solution)/shard_map/all_to_all | solution.py:422
  85.6 17.1 %collective-permute-start.8 = (bf16[512,512]{1,0:T(8,128)(2,1)}, bf16[512,512]{1,0:T(8,128)(2,1)}, u32[]{:S(2)}, u32[]{:S(2)}) collective-permute-start(bf16[512,512]{1,0:T(8,128)(2,1)} %collective-permute-done.6.a0_ref.refs_4_), channel_id=1, source_target_pairs={{0,1},{1,0},{2,3},{3,2},{4,5},{5,4},{6,7},{7,6},{8,9},{9,8},{10,11... | collective-permute-start | bytes 1572872 | tf_op jit(solution)/shard_map/ppermute | solution.py:413
  88.0 14.6 %collective-permute-start.9 = (bf16[512,512]{1,0:T(8,128)(2,1)}, bf16[512,512]{1,0:T(8,128)(2,1)}, u32[]{:S(2)}, u32[]{:S(2)}) collective-permute-start(bf16[512,512]{1,0:T(8,128)(2,1)} %collective-permute-done.7.a1_ref), channel_id=1, source_target_pairs={{0,1},{1,0},{2,3},{3,2},{4,5},{5,4},{6,7},{7,6},{8,9},{9,8},{10,11... | collective-permute-start | bytes 1572872 | tf_op jit(solution)/shard_map/ppermute | solution.py:413
  94.3 8.3 %copy-start.2 = (f32[16,64,128]{2,1,0:T(8,128)}, f32[16,64,128]{2,1,0:T(8,128)S(1)}, u32[]{:S(2)}) copy-start(f32[16,64,128]{2,1,0:T(8,128)S(1)} %all-to-all-done.2.p_ref) | copy-start | bytes 1572868
  94.4 13.9 %collective-permute-start.5 = (f32[64,128]{1,0:T(8,128)S(1)}, f32[64,128]{1,0:T(8,128)S(1)}, u32[]{:S(2)}, u32[]{:S(2)}) collective-permute-start(f32[64,128]{1,0:T(8,128)S(1)} %reduce_sum.37), channel_id=1, source_target_pairs={{0,64},{4,68},{8,72},{12,76},{16,80},{20,84},{24,88},{28,92},{32,9... | collective-permute-start | bytes 98312 | tf_op jit(solution)/shard_map/ppermute | solution.py:419
  95.4 0.8 copy-start.5
  96.2 0.8 copy-start.6
  108.3 0.6 copy-start.7
  110.8 4.6 %copy-start.9 = (bf16[512,512]{1,0:T(8,128)(2,1)S(1)}, bf16[512,512]{1,0:T(8,128)(2,1)}, u32[]{:S(2)}) copy-start(bf16[512,512]{1,0:T(8,128)(2,1)} %get-tuple-element.51.refs_1_) | copy-start | bytes 1572868
  110.8 51.0 %all-to-all-start.3 = ((bf16[16,144,768]{2,1,0:T(8,128)(2,1)}), bf16[16,144,768]{2,1,0:T(8,128)(2,1)}, u32[]{:S(2)}, u32[]{:S(2)}) async-start(bf16[16,144,768]{2,1,0:T(8,128)(2,1)} %shard_map.128), calls=%async_computation.3 | async-start | bytes 7077888 | tf_op jit(solution)/shard_map/all_to_all | solution.py:422
  115.4 13.7 %collective-permute-start.14 = (bf16[512,512]{1,0:T(8,128)(2,1)S(1)}, bf16[512,512]{1,0:T(8,128)(2,1)S(1)}, u32[]{:S(2)}, u32[]{:S(2)}) collective-permute-start(bf16[512,512]{1,0:T(8,128)(2,1)S(1)} %copy-done.9), channel_id=1, source_target_pairs={{0,2},{1,3},{2,0},{3,1},{4,6},{5,7},{6,4},{7,5},{8,10},{9,11},{10,... | collective-permute-start | bytes 1572872 | tf_op jit(solution)/shard_map/ppermute | solution.py:416
  117.0 24.4 %collective-permute-start.13 = (bf16[512,512]{1,0:T(8,128)(2,1)S(1)}, bf16[512,512]{1,0:T(8,128)(2,1)S(1)}, u32[]{:S(2)}, u32[]{:S(2)}) collective-permute-start(bf16[512,512]{1,0:T(8,128)(2,1)S(1)} %copy-done.9), channel_id=1, source_target_pairs={{0,1},{1,0},{2,3},{3,2},{4,5},{5,4},{6,7},{7,6},{8,9},{9,8},{10,11... | collective-permute-start | bytes 1572872 | tf_op jit(solution)/shard_map/ppermute | solution.py:413
  129.2 12.3 %copy-start.10 = (bf16[512,512]{1,0:T(8,128)(2,1)}, bf16[512,512]{1,0:T(8,128)(2,1)S(1)}, u32[]{:S(2)}) copy-start(bf16[512,512]{1,0:T(8,128)(2,1)S(1)} %collective-permute-done.14.refs_5_) | copy-start | bytes 1572868
  129.2 12.3 %collective-permute-start.15 = (bf16[512,512]{1,0:T(8,128)(2,1)S(1)}, bf16[512,512]{1,0:T(8,128)(2,1)}, u32[]{:S(2)}, u32[]{:S(2)}) collective-permute-start(bf16[512,512]{1,0:T(8,128)(2,1)S(1)} %collective-permute-done.14.refs_5_), channel_id=1, source_target_pairs={{0,1},{1,0},{2,3},{3,2},{4,5},{5,4},{6,7},{7,6},{8,9},{9,8},{10,11... | collective-permute-start | bytes 1572872 | tf_op jit(solution)/shard_map/ppermute | solution.py:413
  141.5 0.8 copy-start.11
  164.1 6.3 %collective-permute-start.16 = (f32[64,768]{1,0:T(8,128)S(1)}, f32[64,768]{1,0:T(8,128)S(1)}, u32[]{:S(2)}, u32[]{:S(2)}) collective-permute-start(f32[64,768]{1,0:T(8,128)S(1)} %get-tuple-element.61), channel_id=1, source_target_pairs={{0,64},{4,68},{8,72},{12,76},{16,80},{20,84},{24,88},{28,92},{32,9... | collective-permute-start | bytes 589832 | tf_op jit(solution)/shard_map/ppermute | solution.py:419

commit v3 on v2

v3 whole, which is shorter than its diff:
```python
import functools

import jax
import jax.numpy as jnp
from jax import lax
from jax.experimental import pallas as pl
from jax.experimental.pallas import tpu as pltpu
from jax.sharding import PartitionSpec as P

HD = 128
F32 = jnp.float32
BF16 = jnp.bfloat16
VMEM_LIMIT = 62 * 1024 * 1024

NT = (((1,), (1,)), ((), ()))
TN = (((0,), (0,)), ((), ()))
NN = (((1,), (0,)), ((), ()))


def dot(a, b, dims):
    return lax.dot_general(a, b, dims, preferred_element_type=F32)


def after(array, *others):
    return lax.optimization_barrier((array,) + others)[0]


def tied(kernel, operands, in_specs, deps):
    count = len(operands)

    def run(*refs):
        kernel(*refs[:count], *refs[count + len(deps) :])

    specs = [pl.BlockSpec(memory_space=pl.ANY)] * len(deps)
    return run, list(operands) + list(deps), list(in_specs) + specs


def params():
    return pltpu.CompilerParams(vmem_limit_bytes=VMEM_LIMIT)


def cost(flops, nbytes):
    return pl.CostEstimate(flops=flops, bytes_accessed=nbytes, transcendentals=0)


def state_kernel(k_ref, v_ref, s_ref):
    for head in range(s_ref.shape[0]):
        cols = slice(head * HD, (head + 1) * HD)
        s_ref[head] = dot(k_ref[:, cols], v_ref[:, cols], TN)


def block_states(keys, values):
    length, inner = keys.shape
    heads = inner // HD
    step = 4
    rows = pl.BlockSpec((length, step * HD), lambda i: (0, i))
    return pl.pallas_call(
        state_kernel,
        grid=(heads // step,),
        in_specs=[rows, rows],
        out_specs=pl.BlockSpec((step, HD, HD), lambda i: (i, 0, 0)),
        out_shape=jax.ShapeDtypeStruct((heads, HD, HD), F32),
        compiler_params=params(),
        cost_estimate=cost(2 * length * inner * HD, 4 * length * inner),
    )(keys, values)


def running_kernel(reverse, count, use_ref, p_ref, offset_ref, *rest):
    out_ref = rest[-1]
    rows, lanes = out_ref.shape[1], p_ref.shape[2]
    groups = p_ref.shape[1] // rows
    if out_ref.shape[2] > groups * lanes:
        out_ref[...] = jnp.zeros(out_ref.shape, out_ref.dtype)
    total = offset_ref[...] * use_ref[0].astype(F32)
    for step in range(count):
        place = count - 1 - step if reverse else step
        piece = total.astype(out_ref.dtype)
        for group in range(groups):
            cols = slice(group * lanes, (group + 1) * lanes)
            out_ref[place, :, cols] = piece[group * rows : (group + 1) * rows]
        if step < count - 1:
            total = total + p_ref[place]


def running_sum(pieces, offset, use, reverse, target=None, deps=()):
    count, rows, lanes = pieces.shape
    in_specs = [
        pl.BlockSpec(memory_space=pltpu.SMEM),
        pl.BlockSpec(pieces.shape, lambda i: (0, 0, 0)),
        pl.BlockSpec(offset.shape, lambda i: (0, 0)),
    ]
    operands = [use, pieces, offset]
    if target is None:
        aliases = {}
        out_spec = pl.BlockSpec(pieces.shape, lambda i: (0, 0, 0))
        out_shape = jax.ShapeDtypeStruct(pieces.shape, BF16)
    else:
        aliases = {3: 0}
        in_specs.append(pl.BlockSpec(memory_space=pl.ANY))
        operands.append(target)
        last = target.shape[1] // 16 - 1
        out_spec = pl.BlockSpec((count, 16, target.shape[2]), lambda i: (0, last, 0))
        out_shape = jax.ShapeDtypeStruct(target.shape, BF16)
    kernel = functools.partial(running_kernel, reverse, count)
    kernel, operands, in_specs = tied(kernel, operands, in_specs, deps)
    return pl.pallas_call(
        kernel,
        grid=(1,),
        in_specs=in_specs,
        out_specs=out_spec,
        out_shape=out_shape,
        input_output_aliases=aliases,
        compiler_params=params(),
        cost_estimate=cost(count * rows * lanes, 6 * count * rows * lanes),
    )(*operands)


def head_term_kernel(sel_ref, a_ref, w_ref, o_ref):
    o_ref[0] = dot(a_ref[...], w_ref[...], NT).astype(o_ref.dtype)


def head_sum_kernel(sel_ref, a_ref, w_ref, r_ref, o_ref):
    total = dot(a_ref[...], w_ref[...], NT) + r_ref[0].astype(F32)
    o_ref[0] = total.astype(o_ref.dtype)


def head_term(places, grad, w_out, width, dtype, received=None, part=0):
    length, features = grad.shape
    count = len(places)
    tile = 512 if count == 1 else width
    tiles = width // tile
    in_specs = [
        pl.BlockSpec((length, features), lambda i, j, s: (0, 0)),
        pl.BlockSpec((tile, features), lambda i, j, s: (s[i] * tiles + j, 0)),
    ]
    operands = [jnp.stack(places).astype(jnp.int32), grad, w_out]
    if received is not None:
        in_specs.append(pl.BlockSpec((1, length, tile), lambda i, j, s: (part, 0, j)))
        operands.append(received)
    return pl.pallas_call(
        head_term_kernel if received is None else head_sum_kernel,
        grid_spec=pltpu.PrefetchScalarGridSpec(
            num_scalar_prefetch=1,
            grid=(count, tiles),
            in_specs=in_specs,
            out_specs=pl.BlockSpec((1, length, tile), lambda i, j, s: (i, 0, j)),
        ),
        out_shape=jax.ShapeDtypeStruct((count, length, width), dtype),
        compiler_params=params(),
        cost_estimate=cost(2 * length * features * width, 4 * width * features),
    )(*operands)


def score_rows(q_ref, k_ref, first, size):
    last = first + size
    scores = dot(q_ref[first:last], k_ref[:last], NT)
    return masked(scores, first)


def masked(scores, first):
    rows = lax.broadcasted_iota(jnp.int32, scores.shape, 0) + first
    cols = lax.broadcasted_iota(jnp.int32, scores.shape, 1)
    return jnp.where(cols <= rows, scores, 0.0).astype(BF16)


def sigmoid(gate):
    return 0.5 * jnp.tanh(0.5 * gate.astype(F32)) + 0.5


def head_out_kernel(
    part, half_ref, q_ref, k_ref, v_ref, g_ref, gain_ref, s_ref, mine_ref, other_ref, attn_ref
):
    length = q_ref.shape[0]
    half = HD // 2
    lane = lax.broadcasted_iota(jnp.int32, (part, HD), 1)
    upper = half_ref[0] == 1
    for pair in range(s_ref.shape[0] // 2):
        packed = slice(pair * HD, (pair + 1) * HD)
        for first in range(0, length, part):
            last = first + part
            outs = []
            for head in (2 * pair, 2 * pair + 1):
                cols = slice(head * HD, (head + 1) * HD)
                queries = q_ref[first:last, cols]
                scores = masked(dot(queries, k_ref[:last, cols], NT), first)
                attn = dot(scores, v_ref[:last, cols], NN) + dot(queries, s_ref[head], NN)
                inv = lax.rsqrt(jnp.mean(attn * attn, axis=-1, keepdims=True) + 1e-06)
                outs.append(attn * inv * gain_ref[:, cols] * sigmoid(g_ref[first:last, cols]))
                attn_ref[first:last, cols] = attn
            low = jnp.where(lane < half, outs[0], pltpu.roll(outs[1], half, 1))
            high = jnp.where(lane < half, pltpu.roll(outs[0], half, 1), outs[1])
            mine_ref[first:last, packed] = jnp.where(upper, high, low).astype(BF16)
            other_ref[first:last, packed] = jnp.where(upper, low, high).astype(BF16)


def head_outputs(half, queries, keys, values, gate, gain, state, deps):
    length, inner = queries.shape
    heads = inner // HD
    step = 4
    rows = pl.BlockSpec((length, step * HD), lambda i: (0, i))
    packed_rows = pl.BlockSpec((length, step * HD // 2), lambda i: (0, i))
    square = pl.BlockSpec((step, HD, HD), lambda i: (i, 0, 0))
    packed = jax.ShapeDtypeStruct((length, inner // 2), BF16)
    in_specs = [
        pl.BlockSpec(memory_space=pltpu.SMEM),
        rows,
        rows,
        rows,
        rows,
        pl.BlockSpec((1, step * HD), lambda i: (0, i)),
        square,
    ]
    operands = [half, queries, keys, values, gate, gain, state]
    kernel = functools.partial(head_out_kernel, 256)
    kernel, operands, in_specs = tied(kernel, operands, in_specs, deps)
    return pl.pallas_call(
        kernel,
        grid=(heads // step,),
        in_specs=in_specs,
        out_specs=[packed_rows, packed_rows, rows],
        out_shape=[packed, packed, jax.ShapeDtypeStruct((length, inner), F32)],
        compiler_params=params(),
        cost_estimate=cost(4 * length * length * inner, 14 * length * inner),
    )(*operands)


def head_back_kernel(
    q_ref, g_ref, gain_ref, attn_ref, own_ref, far_ref, gate_ref, hi_ref, lo_ref, state_ref
):
    for head in range(state_ref.shape[0]):
        cols = slice(head * HD, (head + 1) * HD)
        gain = gain_ref[:, cols]
        attn = attn_ref[:, cols]
        inv = lax.rsqrt(jnp.mean(attn * attn, axis=-1, keepdims=True) + 1e-06)
        sig = sigmoid(g_ref[:, cols])
        grad = own_ref[:, cols] + far_ref[:, cols].astype(F32)
        unit = attn * inv
        scaled = grad * sig * gain
        product = scaled * unit
        gate_ref[:, cols] = (product * (1.0 - sig)).astype(BF16)
        full = inv * (scaled - unit * jnp.mean(product, axis=-1, keepdims=True))
        high = full.astype(BF16)
        hi_ref[:, cols] = high
        lo_ref[:, cols] = (full - high.astype(F32)).astype(BF16)
        state_ref[head] = dot(q_ref[:, cols], high, TN)


def head_back(queries, gate, gain, attn, own, far):
    length, inner = queries.shape
    heads = inner // HD
    step = 4
    rows = pl.BlockSpec((length, step * HD), lambda i: (0, i))
    square = pl.BlockSpec((step, HD, HD), lambda i: (i, 0, 0))
    wide = jax.ShapeDtypeStruct((length, inner), BF16)
    return pl.pallas_call(
        head_back_kernel,
        grid=(heads // step,),
        in_specs=[rows, rows, pl.BlockSpec((1, step * HD), lambda i: (0, i)), rows, rows, rows],
        out_specs=[rows, rows, rows, square],
        out_shape=[wide, wide, wide, jax.ShapeDtypeStruct((heads, HD, HD), F32)],
        compiler_params=params(),
        cost_estimate=cost(2 * length * HD * inner, 20 * length * inner),
    )(queries, gate, gain, attn, own, far)


def grads_kernel(
    part, q_ref, k_ref, v_ref, hi_ref, lo_ref, s_ref, dq_ref, dk_ref, dv_ref
):
    length = q_ref.shape[0]
    for head in range(s_ref.shape[0]):
        cols = slice(head * HD, (head + 1) * HD)
        for first in range(0, length, part):
            last = first + part
            queries, high = q_ref[first:last, cols], hi_ref[first:last, cols]
            keys, values = k_ref[:last, cols], v_ref[:last, cols]
            scores = masked(dot(queries, keys, NT), first)
            prob = dot(high, values, NT) + dot(lo_ref[first:last, cols], values, NT)
            prob = masked(prob, first)
            dq = dot(prob, keys, NN) + dot(high, s_ref[head], NT)
            dq_ref[first:last, cols] = dq.astype(BF16)
            dk = dot(prob, queries, TN)
            dv = dot(scores, high, TN)
            if first:
                dk_ref[:first, cols] += dk[:first]
                dv_ref[:first, cols] += dv[:first]
            dk_ref[first:last, cols] = dk[first:]
            dv_ref[first:last, cols] = dv[first:]


def head_grads(queries, keys, values, high, low, state, deps):
    length, inner = queries.shape
    heads = inner // HD
    step = 2
    rows = pl.BlockSpec((length, step * HD), lambda i: (0, i))
    square = pl.BlockSpec((step, HD, HD), lambda i: (i, 0, 0))
    wide = jax.ShapeDtypeStruct((length, inner), BF16)
    full = jax.ShapeDtypeStruct((length, inner), F32)
    kernel = functools.partial(grads_kernel, 256)
    operands = [queries, keys, values, high, low, state]
    kernel, operands, in_specs = tied(
        kernel, operands, [rows, rows, rows, rows, rows, square], deps
    )
    return pl.pallas_call(
        kernel,
        grid=(heads // step,),
        in_specs=in_specs,
        out_specs=[rows, rows, rows],
        out_shape=[wide, full, full],
        compiler_params=params(),
        cost_estimate=cost(10 * length * length * inner, 20 * length * inner),
    )(*operands)


def later_kernel(k_ref, v_ref, dk_ref, dv_ref, l_ref, dk_out, dv_out):
    groups = HD // (2 * l_ref.shape[1])
    for head in range(l_ref.shape[0] // 2):
        cols = slice(head * HD, (head + 1) * HD)
        later = jnp.concatenate(
            [
                l_ref[2 * head + piece, :, group * HD : (group + 1) * HD]
                for piece in range(2)
                for group in range(groups)
            ],
            axis=0,
        )
        dk_out[:, cols] = (dk_ref[:, cols] + dot(v_ref[:, cols], later, NT)).astype(BF16)
        dv_out[:, cols] = (dv_ref[:, cols] + dot(k_ref[:, cols], later, NN)).astype(BF16)


def later_grads(keys, values, key_part, value_part, parts, deps):
    length, inner = keys.shape
    heads = inner // HD
    step = 4
    rows = pl.BlockSpec((length, step * HD), lambda i: (0, i))
    wide = jax.ShapeDtypeStruct((length, inner), BF16)
    last = parts.shape[1] // 16 - 1
    in_specs = [
        rows,
        rows,
        rows,
        rows,
        pl.BlockSpec((2 * step, 16, parts.shape[2]), lambda i: (i, last, 0)),
    ]
    operands = [keys, values, key_part, value_part, parts]
    kernel, operands, in_specs = tied(later_kernel, operands, in_specs, deps)
    return pl.pallas_call(
        kernel,
        grid=(heads // step,),
        in_specs=in_specs,
        out_specs=[rows, rows],
        out_shape=[wide, wide],
        compiler_params=params(),
        cost_estimate=cost(4 * length * HD * inner, 16 * length * inner),
    )(*operands)


def mixed_kernel(sel_ref, *refs):
    blocks, w_ref, o_ref = refs[:-2], refs[-2], refs[-1]
    half = HD // 2
    total = None
    for place, block in enumerate(blocks):
        rows = []
        for head in range(block.shape[1] // half):
            first = sel_ref[2 * place] * 1024 + sel_ref[2 * place + 1] * half + head * HD
            rows.append(w_ref[pl.ds(pl.multiple_of(first, half), half), :])
        term = dot(block[...], jnp.concatenate(rows, axis=0), NN)
        total = term if total is None else total + term
    o_ref[...] = total.astype(BF16)


def mix(sel, blocks, w_out, deps):
    length, width = blocks[0].shape
    inner, features = w_out.shape
    tile = 256
    whole = pl.BlockSpec((length, width), lambda j, s: (0, 0))
    in_specs = [whole] * len(blocks) + [pl.BlockSpec((inner, tile), lambda j, s: (0, j))]
    kernel, operands, in_specs = tied(mixed_kernel, [sel, *blocks, w_out], in_specs, deps)
    return pl.pallas_call(
        kernel,
        grid_spec=pltpu.PrefetchScalarGridSpec(
            num_scalar_prefetch=1,
            grid=(features // tile,),
            in_specs=in_specs,
            out_specs=pl.BlockSpec((length, tile), lambda j, s: (0, j)),
        ),
        out_shape=jax.ShapeDtypeStruct((length, features), BF16),
        compiler_params=params(),
        cost_estimate=cost(2 * length * inner * features, 2 * inner * features),
    )(*operands)


def weight_kernel(sel_ref, a0_ref, a1_ref, b0_ref, b1_ref, m0_ref, m1_ref, *rest):
    o_ref = rest[-1]
    count, size = o_ref.shape[:2]
    for source, (first, second) in enumerate(((a0_ref, a1_ref), (b0_ref, b1_ref))):

        @pl.when(pl.program_id(0) == source)
        def _(first=first, second=second):
            total = dot(first[...], m0_ref[...], TN) + dot(second[...], m1_ref[...], TN)
            for piece in range(count):
                o_ref[piece] = total[piece * size : (piece + 1) * size].astype(BF16)


def weight_grad(sel, mine, other, grads, across, index, target=None, deps=()):
    length, width = mine[0].shape
    features = grads[0].shape[1]
    size = 2 * width // across
    tile = 512
    tiles, count = width // tile, tile // size
    last = tiles - 1

    def place(i, j, s):
        return ((s[0] + i - 2 * s[0] * i) * tiles + j, index, 0)

    first_rows = pl.BlockSpec((length, tile), lambda i, j, s: (0, jnp.where(i == 0, j, last)))
    second_rows = pl.BlockSpec((length, tile), lambda i, j, s: (0, jnp.where(i == 0, 0, j)))
    whole = pl.BlockSpec((length, features), lambda i, j, s: (0, 0))
    in_specs = [first_rows, first_rows, second_rows, second_rows, whole, whole]
    operands = [sel, mine[0], mine[1], other[0], other[1], *grads]
    aliases = {}
    if target is not None:
        in_specs.append(pl.BlockSpec(memory_space=pl.ANY))
        operands.append(target)
        aliases = {len(operands) - 1: 0}
    kernel, operands, in_specs = tied(weight_kernel, operands, in_specs, deps)
    return pl.pallas_call(
        kernel,
        grid_spec=pltpu.PrefetchScalarGridSpec(
            num_scalar_prefetch=1,
            grid=(2, tiles),
            in_specs=in_specs,
            out_specs=pl.BlockSpec((count, size, features), place),
        ),
        out_shape=jax.ShapeDtypeStruct((across, 2 * size + 16, features), BF16),
        input_output_aliases=aliases,
        compiler_params=params(),
        cost_estimate=cost(8 * length * width * features, 4 * width * features),
    )(*operands)


def per_device(query_rows, key_rows, value_rows, gate_input, norm_gain, w_out, mixed_grad):
    length, inner_dev = query_rows.shape
    heads_dev = inner_dev // HD
    features = w_out.shape[1]
    planes, across = 2, 16
    ctx, fsdp = lax.axis_index("ctx"), lax.axis_index("fsdp")
    y_lo = ctx // across
    y_hi, core = fsdp // 2, fsdp % 2
    groups = [[y * across + i for i in range(across)] for y in range(planes)]
    core_swap = [(0, 1), (1, 0), (2, 3), (3, 2)]
    hi_swap = [(0, 2), (1, 3), (2, 0), (3, 1)]
    lo_swap = [(i, (i + across) % (2 * across)) for i in range(2 * across)]

    def swap_core(array):
        return lax.ppermute(array, "fsdp", core_swap)

    def swap_hi(array):
        return lax.ppermute(array, "fsdp", hi_swap)

    def swap_lo(array):
        return lax.ppermute(array, "ctx", lo_swap)

    def exchange(array):
        return lax.all_to_all(array, "ctx", 0, 0, axis_index_groups=groups)

    def sums_before(pieces, offset, reverse, target=None, deps=()):
        use = (y_lo == (0 if reverse else 1)).astype(jnp.int32).reshape(1)
        return running_sum(pieces, offset, use, reverse, target, deps)

    def split_states(local):
        return exchange(local.reshape(across, heads_dev * HD // across, HD))

    gain = norm_gain.reshape(1, inner_dev)
    peer, far = fsdp + 1 - 2 * core, (fsdp + 2) % 4
    far_peer = (peer + 2) % 4

    def term(place, dtype, received=None, deps=()):
        return head_term(place, mixed_grad, w_out, inner_dev, dtype, received, deps)

    def term(places, dtype, received=None, part=0):
        return head_term(places, mixed_grad, w_out, inner_dev, dtype, received, part)

    grad_pair = swap_lo(mixed_grad)
    sent = term([far_peer, peer], BF16)
    got = swap_core(sent)
    local_state = block_states(after(key_rows, sent), value_rows)
    pieces = split_states(local_state)
    total = jnp.sum(pieces, axis=0)
    offset = swap_lo(total)
    far_part = term([after(far, total)], BF16, got, 0)[0]
    grad_far = swap_hi(after(far_part, offset, grad_pair))
    sums = sums_before(after(pieces, far_part), offset, False)
    grad_own = term([after(fsdp, sums)], F32, got, 1)[0]
    prev_state = exchange(sums).reshape(heads_dev, HD, HD)

    half = y_lo.astype(jnp.int32).reshape(1)
    out, out_other, attn = head_outputs(
        half, after(query_rows, grad_own), key_rows, value_rows, gate_input, gain, prev_state, []
    )
    gate_grad, high, low, grad_state = head_back(
        query_rows, gate_input, gain, attn, grad_own, grad_far
    )
    later_pieces = split_states(grad_state)
    later_total = jnp.sum(later_pieces, axis=0)

    across_y = []
    for place in range(2 * across):
        for part in range(4):
            target = ((place + across) % (2 * across)) * 4 + (part + 2) % 4
            across_y.append((place * 4 + part, target))
    out_pair = swap_lo(out_other)
    out_far = swap_hi(out)
    out_far_pair = lax.ppermute(out_other, ("ctx", "fsdp"), across_y)
    out_core, out_pair_core = (
        swap_core(after(out, grad_state)), swap_core(after(out_pair, grad_state))
    )
    out_far_core, out_far_pair_core = swap_core(out_far), swap_core(out_far_pair)
    select = core.astype(jnp.int32).reshape(1)
    grads = [mixed_grad, grad_pair]
    weight = weight_grad(
        select, [out, out_pair], [out_core, out_pair_core], grads, across, 0, deps=[grad_state]
    )
    weight = weight_grad(
        select, [out_far, out_far_pair], [out_far_core, out_far_pair_core], grads, across, 1,
        weight,
    )
    later_offset = swap_lo(later_total)
    weight = sums_before(later_pieces, later_offset, True, weight)
    parts = exchange(weight)
    far_other = swap_hi(out_other)
    query_grad, key_part, value_part = head_grads(
        query_rows, key_rows, value_rows, high, low, prev_state, [weight]
    )

    blocks = [out, out_other, out_core, swap_core(out_other)]
    blocks += [out_far, far_other, out_far_core, swap_core(far_other)]
    order = []
    for heads in (fsdp, peer, far, far_peer):
        order += [heads, y_lo, heads, 1 - y_lo]
    order = jnp.stack(order).astype(jnp.int32)
    mixed = mix(order, blocks, w_out, [query_grad])

    parts = after(parts, mixed)
    key_grad, value_grad = later_grads(key_rows, value_rows, key_part, value_part, parts, [])
    size = 2 * inner_dev // (2 * across)
    near_sum = jnp.sum(parts[:, :size].astype(F32), axis=0)
    far_sum = jnp.sum(parts[:, size : 2 * size].astype(F32), axis=0)
    keeps = y_hi == y_lo
    kept = jnp.where(keeps, near_sum, far_sum)
    received = swap_lo(jnp.where(keeps, far_sum, near_sum))
    w_out_grad = jnp.where(
        y_lo == 0,
        jnp.concatenate([kept, received], axis=0),
        jnp.concatenate([received, kept], axis=0),
    )
    return (mixed, w_out_grad, query_grad, key_grad, value_grad, gate_grad)


def solution(mesh):
    return jax.shard_map(
        per_device,
        mesh=mesh,
        in_specs=(
            P("ctx", "fsdp"),
            P("ctx", "fsdp"),
            P("ctx", "fsdp"),
            P("ctx", "fsdp"),
            P("fsdp"),
            P(None, "fsdp"),
            P("ctx", "fsdp"),
        ),
        out_specs=(
            P("ctx", "fsdp"),
            P("ctx", "fsdp"),
            P("ctx", "fsdp"),
            P("ctx", "fsdp"),
            P("ctx", "fsdp"),
            P("ctx", "fsdp"),
        ),
        check_vma=False,
    )
```

time: 172 us -> 166 us (0.965)
  Pallas kernels: 73.3 us -> 63.7 us
  waiting for transfers between devices: 53.4 us -> 57.8 us
    pallas_call x10, Pallas kernels: 59 us -> 50.6 us  [the longest x1 10.1 us: head_grads(): pl.pallas_call(kernel, grid=(heads // step,), in_specs=in_specs, out_spec...]
    all_to_all x4, waiting for transfers between devices: 30.4 us -> 35.2 us  [exchange(): return lax.all_to_all(array, 'ctx', 0, 0, axis_index_groups=groups)]
    ppermute x3, waiting for transfers between devices: 15.7 us -> 12.3 us  [swap_hi(): return lax.ppermute(array, 'fsdp', hi_swap)]
    ppermute x1, waiting for transfers between devices: 2.46 us -> 4.89 us  [per_device(): out_far_pair = lax.ppermute(out_other, ('ctx', 'fsdp'), across_y)]
    ppermute x5, waiting for transfers between devices: 3.57 us -> 5.31 us  [swap_lo(): return lax.ppermute(array, 'ctx', lo_swap)]
    pallas_call x4 -> x3, Pallas kernels: 14.3 us -> 13.1 us  [head_term(): pl.pallas_call(head_term_kernel if received is None else head_sum_kernel,...]
    unnamed x24 -> x28, local copies, waits for them, and re-layouts: 4.66 us -> 4.66 us
  transfers between devices with their start and end apart: 21 -> 20, of which waited for: 10 -> 8; matrix products, arithmetic and copies ran while one was open for 0% -> 0% of each run, Pallas kernels for 37% -> 34%
where the time goes in v3:
time: 166 us; the launch traced here: 165 us
  Pallas kernels  63.7 us (38%)
  waiting for transfers between devices  57.8 us (35%)
  starting transfers between devices  34 us (20%)
  local copies, waits for them, and re-layouts  5.33 us (3%)
  other arithmetic  3.81 us (2%)
    all_to_all x4, waiting for transfers between devices, exchange(): return lax.all_to_all(array, 'ctx', 0, 0, axis_index_groups=groups)  35.2 us
    all_to_all x4, starting transfers between devices, exchange(): return lax.all_to_all(array, 'ctx', 0, 0, axis_index_groups=groups)  19.7 us
    pallas_call x3, Pallas kernels, head_term(): pl.pallas_call(head_term_kernel if received is None else head_sum_kernel,...  13.1 us
    ppermute x3, waiting for transfers between devices, swap_hi(): return lax.ppermute(array, 'fsdp', hi_swap)  12.3 us
    pallas_call x1, Pallas kernels, head_grads(): pl.pallas_call(kernel, grid=(heads // step,), in_specs=in_specs, out_spec...  10.1 us
    pallas_call x2, Pallas kernels, weight_grad(): pl.pallas_call(kernel, grid_spec=pltpu.PrefetchScalarGridSpec(num_scalar_...  9.99 us
    pallas_call x1, Pallas kernels, mix(): pl.pallas_call(kernel, grid_spec=pltpu.PrefetchScalarGridSpec(num_scalar_...  8.39 us
    ppermute x3, starting transfers between devices, swap_hi(): return lax.ppermute(array, 'fsdp', hi_swap)  7.26 us
  transfers between devices with their start and end apart: 20, of which 8 were waited for; matrix products, arithmetic and copies ran while one was open for 0% of the time, Pallas kernels for 34%

profile of v3, /device:TPU:0, one launch (start us, length us, event | category | flops | bytes accessed | tf_op | source)
XLA Modules:
  0.0 165.5 jit_solution(11000530950812260085)
XLA Ops:
  0.7 0.6 pad_add_fusion.sel_ref
  1.3 5.7 %shard_map.118 = bf16[2,512,1024]{2,1,0:T(8,128)(2,1)} custom-call(s32[2]{0:T(128)} %pad_add_fusion.sel_ref, bf16[512,768]{1,0:T(8,128)(2,1)} %refs_5_.3, bf16[4096,768]{1,0:T(8,128)(2,1)} %refs_9_.1), custom_call_target="tpu_custom_call" | custom-call | flops 805306368 | bytes 3145728 | tf_op jit(solution)/shard_map/pallas_call | solution.py:140
  7.0 1.7 %collective-permute-start.2 = (bf16[512,768]{1,0:T(8,128)(2,1)S(1)}, bf16[512,768]{1,0:T(8,128)(2,1)}, u32[]{:S(2)}, u32[]{:S(2)}) collective-permute-start(bf16[512,768]{1,0:T(8,128)(2,1)S(1)} %copy-done), channel_id=1, source_target_pairs={{0,64},{4,68},{8,72},{12,76},{16,80},{20,84},{24,88},{28,92},{32,9... | collective-permute-start | bytes 2359304 | tf_op jit(solution)/shard_map/ppermute | solution.py:461
  8.7 2.6 %shard_map.119 = f32[8,128,128]{2,1,0:T(8,128)} custom-call(bf16[512,1024]{1,0:T(8,128)(2,1)} %refs_0_.3, bf16[512,1024]{1,0:T(8,128)(2,1)} %refs_1_.4), custom_call_target="tpu_custom_call" | custom-call | flops 134217728 | bytes 2097152 | tf_op jit(solution)/shard_map/pallas_call | solution.py:57
  11.4 7.9 %all-to-all-start = ((f32[16,64,128]{2,1,0:T(8,128)}), f32[16,64,128]{2,1,0:T(8,128)S(1)}, u32[]{:S(2)}, u32[]{:S(2)}) async-start(f32[16,64,128]{2,1,0:T(8,128)} %bitcast.18), calls=%async_computation | async-start | bytes 1048576 | tf_op jit(solution)/shard_map/all_to_all | solution.py:464
  19.3 11.8 %all-to-all-done.refs_1_ = f32[16,64,128]{2,1,0:T(8,128)S(1)} async-done(((f32[16,64,128]{2,1,0:T(8,128)}), f32[16,64,128]{2,1,0:T(8,128)S(1)}, u32[]{:S(2)}, u32[]{:S(2)}) %all-to-all-start) | async-done | bytes 524320 | tf_op jit(solution)/shard_map/all_to_all | solution.py:464
  31.1 0.5 collective-permute-start.1
  31.6 3.6 %shard_map.120 = bf16[1,512,1024]{2,1,0:T(8,128)(2,1)} custom-call(s32[1]{0:T(128)} %bitcast.8.sel_ref, bf16[512,768]{1,0:T(8,128)(2,1)} %refs_5_.3, bf16[4096,768]{1,0:T(8,128)(2,1)} %refs_9_.1, bf16[2,512,1024]{2,1,0:T(8,128)(2,1)} %collective-permute-done.r_ref), custom_call_target="tpu_custom_call" | custom-call | flops 805306368 | bytes 3145728 | tf_op jit(solution)/shard_map/pallas_call | solution.py:140
  35.2 0.0 copy-start.13
  35.2 3.2 %collective-permute-start.3 = (bf16[512,1024]{1,0:T(8,128)(2,1)}, bf16[512,1024]{1,0:T(8,128)(2,1)S(1)}, u32[]{:S(2)}, u32[]{:S(2)}) collective-permute-start(bf16[512,1024]{1,0:T(8,128)(2,1)} %bitcast.20), channel_id=1, source_target_pairs={{0,2},{1,3},{2,0},{3,1},{4,6},{5,7},{6,4},{7,5},{8,10},{9,11},{10,... | collective-permute-start | bytes 3145736 | tf_op jit(solution)/shard_map/ppermute | solution.py:458
  38.4 1.8 %shard_map.121 = bf16[16,64,128]{2,1,0:T(8,128)(2,1)} custom-call(s32[1]{0:T(128)} %bitcast.6.refs_0_, f32[16,64,128]{2,1,0:T(8,128)} %copy-done.1, f32[64,128]{1,0:T(8,128)} %copy-done.13), custom_call_target="tpu_custom_call" | custom-call | flops 131072 | bytes 786432 | tf_op jit(solution)/shard_map/pallas_call | solution.py:106
  40.2 3.5 %all-to-all-start.1 = ((bf16[16,64,128]{2,1,0:T(8,128)(2,1)}), bf16[16,64,128]{2,1,0:T(8,128)(2,1)S(1)}, u32[]{:S(2)}, u32[]{:S(2)}) async-start(bf16[16,64,128]{2,1,0:T(8,128)(2,1)} %shard_map.121), calls=%async_computation.1 | async-start | bytes 524288 | tf_op jit(solution)/shard_map/all_to_all | solution.py:464
  43.8 3.8 %shard_map.122 = f32[1,512,1024]{2,1,0:T(8,128)} custom-call(s32[1]{0:T(128)} %bitcast.10.sel_ref, bf16[512,768]{1,0:T(8,128)(2,1)} %refs_5_.3, bf16[4096,768]{1,0:T(8,128)(2,1)} %refs_9_.1, bf16[2,512,1024]{2,1,0:T(8,128)(2,1)} %collective-permute-done.r_ref), custom_call_target="tpu_custom_call" | custom-call | flops 805306368 | bytes 3145728 | tf_op jit(solution)/shard_map/pallas_call | solution.py:140
  47.6 4.6 %all-to-all-done.1 = bf16[16,64,128]{2,1,0:T(8,128)(2,1)S(1)} async-done(((bf16[16,64,128]{2,1,0:T(8,128)(2,1)}), bf16[16,64,128]{2,1,0:T(8,128)(2,1)S(1)}, u32[]{:S(2)}, u32[]{:S(2)}) %all-to-all-start.1) | async-done | bytes 262176 | tf_op jit(solution)/shard_map/all_to_all | solution.py:464
  52.2 0.7 copy-done.7
  52.9 6.2 %shard_map.123 = (bf16[512,512]{1,0:T(8,128)(2,1)}, bf16[512,512]{1,0:T(8,128)(2,1)}, f32[512,1024]{1,0:T(8,128)}) custom-call(s32[1]{0:T(128)} %bitcast.1.refs_0_, bf16[512,1024]{1,0:T(8,128)(2,1)} %refs_0_.2, bf16[512,1024]{1,0:T(8,128)(2,1)} %refs_0_.3, bf16[512,1024]{1,0:T(8,128)(2,1)} %refs_1_.4, bf16[512,1024]{1,0:T(8,128)(2,1)} %g_ref.1, ...), custom_call_target="tpu_custom_call" | custom-call | flops 1073741824 | bytes 7340032 | tf_op jit(solution)/shard_map/pallas_call | solution.py:216
  59.1 0.7 collective-permute-start.13
  59.7 0.5 collective-permute-start.11
  60.3 2.9 %collective-permute-start.6 = (bf16[512,512]{1,0:T(8,128)(2,1)}, bf16[512,512]{1,0:T(8,128)(2,1)S(1)}, u32[]{:S(2)}, u32[]{:S(2)}) collective-permute-start(bf16[512,512]{1,0:T(8,128)(2,1)} %get-tuple-element.37.refs_1_), channel_id=1, source_target_pairs={{0,2},{1,3},{2,0},{3,1},{4,6},{5,7},{6,4},{7,5},{8,10},{9,11},{10,... | collective-permute-start | bytes 1572872 | tf_op jit(solution)/shard_map/ppermute | solution.py:458
  63.2 1.0 copy-done.6
  64.1 5.5 %shard_map.124 = (bf16[512,1024]{1,0:T(8,128)(2,1)}, bf16[512,1024]{1,0:T(8,128)(2,1)}, bf16[512,1024]{1,0:T(8,128)(2,1)}, f32[8,128,128]{2,1,0:T(8,128)}) custom-call(bf16[512,1024]{1,0:T(8,128)(2,1)} %refs_0_.2, bf16[512,1024]{1,0:T(8,128)(2,1)} %g_ref.1, f32[1,1024]{1,0:T(1,128)} %bitcast.24, f32[512,1024]{1,0:T(8,128)} %get-tuple-element.34.attn_ref, ...), custom_call_target="tpu_custom_call" | custom-call | flops 134217728 | bytes 10485760 | tf_op jit(solution)/shard_map/pallas_call | solution.py:255
  69.6 4.7 %collective-permute-done.13.refs_2_ = bf16[512,512]{1,0:T(8,128)(2,1)} collective-permute-done((bf16[512,512]{1,0:T(8,128)(2,1)}, bf16[512,512]{1,0:T(8,128)(2,1)}, u32[]{:S(2)}, u32[]{:S(2)}) %collective-permute-start.13) | collective-permute-done | bytes 524320 | tf_op jit(solution)/shard_map/ppermute | solution.py:461
  74.2 0.5 collective-permute-start.4
  74.7 3.7 %all-to-all-start.2 = ((f32[16,64,128]{2,1,0:T(8,128)}), f32[16,64,128]{2,1,0:T(8,128)S(1)}, u32[]{:S(2)}, u32[]{:S(2)}) async-start(f32[16,64,128]{2,1,0:T(8,128)} %bitcast.19), calls=%async_computation.2 | async-start | bytes 1048576 | tf_op jit(solution)/shard_map/all_to_all | solution.py:464
  78.4 4.9 %collective-permute-done.11.refs_2_ = bf16[512,512]{1,0:T(8,128)(2,1)} collective-permute-done((bf16[512,512]{1,0:T(8,128)(2,1)}, bf16[512,512]{1,0:T(8,128)(2,1)}, u32[]{:S(2)}, u32[]{:S(2)}) %collective-permute-start.11) | collective-permute-done | bytes 524320 | tf_op jit(solution)/shard_map/ppermute | solution.py:513
  83.3 0.5 collective-permute-start.8
  83.8 6.4 %all-to-all-done.2.refs_1_ = f32[16,64,128]{2,1,0:T(8,128)S(1)} async-done(((f32[16,64,128]{2,1,0:T(8,128)}), f32[16,64,128]{2,1,0:T(8,128)S(1)}, u32[]{:S(2)}, u32[]{:S(2)}) %all-to-all-start.2) | async-done | bytes 524320 | tf_op jit(solution)/shard_map/all_to_all | solution.py:464
  90.3 1.7 %collective-permute-start.10 = (f32[64,128]{1,0:T(8,128)S(1)}, f32[64,128]{1,0:T(8,128)S(1)}, u32[]{:S(2)}, u32[]{:S(2)}) collective-permute-start(f32[64,128]{1,0:T(8,128)S(1)} %reduce_sum.37), channel_id=1, source_target_pairs={{0,64},{4,68},{8,72},{12,76},{16,80},{20,84},{24,88},{28,92},{32,9... | collective-permute-start | bytes 98312 | tf_op jit(solution)/shard_map/ppermute | solution.py:461
  92.0 0.8 copy-done.11
  92.8 0.8 copy-done.5
  93.6 5.0 %shard_map.125.refs_7_ = bf16[16,144,768]{2,1,0:T(8,128)(2,1)} custom-call(s32[1]{0:T(128)} %bitcast.16.refs_0_, bf16[512,512]{1,0:T(8,128)(2,1)} %get-tuple-element.37.refs_1_, bf16[512,512]{1,0:T(8,128)(2,1)} %collective-permute-done.13.refs_2_, bf16[512,512]{1,0:T(8,128)(2,1)} %copy-done.5, bf16[512,512]{1,0:T(8,128)(2,1)} %copy-done.11, ...), custom_call_target="tpu_custom_call" | custom-call | flops 1610612736 | bytes 1572864 | tf_op jit(solution)/shard_map/pallas_call | solution.py:426
  98.6 5.0 %shard_map.126.refs_3_ = bf16[16,144,768]{2,1,0:T(8,128)(2,1)} custom-call(s32[1]{0:T(128)} %bitcast.16.refs_0_, bf16[512,512]{1,0:T(8,128)(2,1)} %copy-done.4, bf16[512,512]{1,0:T(8,128)(2,1)} %collective-permute-done.11.refs_2_, bf16[512,512]{1,0:T(8,128)(2,1)} %collective-permute-done.8.refs_3_.refs_7_, ...), custom_call_target="tpu_custom_call", output_to_operand_aliasing={{}: (7, {})} | custom-call | flops 1610612736 | bytes 1572864 | tf_op jit(solution)/shard_map/pallas_call | solution.py:426
  103.6 0.6 copy-done.12
  104.2 1.8 %shard_map.127.refs_6_ = bf16[16,144,768]{2,1,0:T(8,128)(2,1)} custom-call(s32[1]{0:T(128)} %bitcast.14.refs_0_, f32[16,64,128]{2,1,0:T(8,128)} %copy-done.2, f32[64,128]{1,0:T(8,128)} %copy-done.12, bf16[16,144,768]{2,1,0:T(8,128)(2,1)} %shard_map.126.refs_3_), custom_call_target="tpu_custom_call", output_to_operand_aliasing={{}: (3, {})} | custom-call | flops 131072 | bytes 786432 | tf_op jit(solution)/shard_map/pallas_call | solution.py:106
  106.1 4.6 %all-to-all-start.3 = ((bf16[16,144,768]{2,1,0:T(8,128)(2,1)}), bf16[16,144,768]{2,1,0:T(8,128)(2,1)}, u32[]{:S(2)}, u32[]{:S(2)}) async-start(bf16[16,144,768]{2,1,0:T(8,128)(2,1)} %shard_map.127.refs_6_), calls=%async_computation.3 | async-start | bytes 7077888 | tf_op jit(solution)/shard_map/all_to_all | solution.py:464
  110.7 1.2 collective-permute-start.7
  111.9 12.3 %collective-permute-done.7.refs_6_ = bf16[512,512]{1,0:T(8,128)(2,1)S(1)} collective-permute-done((bf16[512,512]{1,0:T(8,128)(2,1)S(1)}, bf16[512,512]{1,0:T(8,128)(2,1)S(1)}, u32[]{:S(2)}, u32[]{:S(2)}) %collective-permute-start.7) | collective-permute-done | bytes 524320 | tf_op jit(solution)/shard_map/ppermute | solution.py:458
  124.2 0.7 stack.48.refs_0_
  124.9 10.1 %shard_map.128 = (bf16[512,1024]{1,0:T(8,128)(2,1)}, f32[512,1024]{1,0:T(8,128)}, f32[512,1024]{1,0:T(8,128)}) custom-call(bf16[512,1024]{1,0:T(8,128)(2,1)} %refs_0_.2, bf16[512,1024]{1,0:T(8,128)(2,1)} %refs_0_.3, bf16[512,1024]{1,0:T(8,128)(2,1)} %refs_1_.4, bf16[512,1024]{1,0:T(8,128)(2,1)} %get-tuple-element.38.refs_3_, ...), custom_call_target="tpu_custom_call" | custom-call | flops 2684354560 | bytes 10485760 | tf_op jit(solution)/shard_map/pallas_call | solution.py:303
  135.0 0.0 copy-start.10
  135.0 0.8 copy-done.10
  135.8 8.4 %shard_map.129 = bf16[512,768]{1,0:T(8,128)(2,1)} custom-call(s32[16]{0:T(128)} %stack.48.refs_0_, bf16[512,512]{1,0:T(8,128)(2,1)} %get-tuple-element.37.refs_1_, bf16[512,512]{1,0:T(8,128)(2,1)} %get-tuple-element.33.refs_2_, bf16[512,512]{1,0:T(8,128)(2,1)} %copy-done.5, bf16[512,512]{1,0:T(8,128)(2,1)} %copy-done.10, bf16[512,512]{1,0:T(8,128)(2,1)} %copy-done.4, ...), custom_call_target="tpu_custom_call" | custom-call | flops 3221225472 | bytes 6291456 | tf_op jit(solution)/shard_map/pallas_call | solution.py:378
  144.2 12.4 %all-to-all-done.3.refs_4_ = bf16[16,144,768]{2,1,0:T(8,128)(2,1)} async-done(((bf16[16,144,768]{2,1,0:T(8,128)(2,1)}), bf16[16,144,768]{2,1,0:T(8,128)(2,1)}, u32[]{:S(2)}, u32[]{:S(2)}) %all-to-all-start.3) | async-done | bytes 3538976 | tf_op jit(solution)/shard_map/all_to_all | solution.py:464
  156.6 2.3 %convert_reduce_fusion.1 = (f32[64,768]{1,0:T(8,128)S(1)}, f32[64,768]{1,0:T(8,128)S(1)}) fusion(bf16[16,144,768]{2,1,0:T(8,128)(2,1)} %all-to-all-done.3.refs_4_), kind=kLoop, calls=%fused_computation.1 | loop fusion | flops 3047424 | bytes 3538944 | tf_op jit(solution)/shard_map/reduce_sum | solution.py:546
  159.0 0.8 collective-permute-start.15
  159.8 4.3 %shard_map.130 = (bf16[512,1024]{1,0:T(8,128)(2,1)}, bf16[512,1024]{1,0:T(8,128)(2,1)}) custom-call(bf16[512,1024]{1,0:T(8,128)(2,1)} %refs_0_.3, bf16[512,1024]{1,0:T(8,128)(2,1)} %refs_1_.4, f32[512,1024]{1,0:T(8,128)} %get-tuple-element.43.refs_2_, f32[512,1024]{1,0:T(8,128)} %get-tuple-element.44.refs_3_, bf16[16,144,768]{2,1,0:T(8,128)(2,1)} %all-to-all-done.3.refs_4_), custom_call_target="tpu_custom_call" | custom-call | flops 268435456 | bytes 8388608 | tf_op jit(solution)/shard_map/pallas_call | solution.py:346
  164.1 0.6 collective-permute-done.15
  164.7 0.8 maximum_select_fusion
  (40 shorter events, 0.2 us)
Async XLA Ops:
  1.2 5.8 %copy-start = (bf16[512,768]{1,0:T(8,128)(2,1)S(1)}, bf16[512,768]{1,0:T(8,128)(2,1)}, u32[]{:S(2)}) copy-start(bf16[512,768]{1,0:T(8,128)(2,1)} %refs_5_.3) | copy-start | bytes 2359300
  7.0 24.6 %collective-permute-start = (bf16[2,512,1024]{2,1,0:T(8,128)(2,1)}, bf16[2,512,1024]{2,1,0:T(8,128)(2,1)}, u32[]{:S(2)}, u32[]{:S(2)}) collective-permute-start(bf16[2,512,1024]{2,1,0:T(8,128)(2,1)} %shard_map.118), channel_id=1, source_target_pairs={{0,1},{1,0},{2,3},{3,2},{4,5},{5,4},{6,7},{7,6},{8,9},{9,8},{10,11... | collective-permute-start | bytes 6291464 | tf_op jit(solution)/shard_map/ppermute | solution.py:455
  7.0 28.2 %collective-permute-start.2 = (bf16[512,768]{1,0:T(8,128)(2,1)S(1)}, bf16[512,768]{1,0:T(8,128)(2,1)}, u32[]{:S(2)}, u32[]{:S(2)}) collective-permute-start(bf16[512,768]{1,0:T(8,128)(2,1)S(1)} %copy-done), channel_id=1, source_target_pairs={{0,64},{4,68},{8,72},{12,76},{16,80},{20,84},{24,88},{28,92},{32,9... | collective-permute-start | bytes 2359304 | tf_op jit(solution)/shard_map/ppermute | solution.py:461
  11.4 19.7 %all-to-all-start = ((f32[16,64,128]{2,1,0:T(8,128)}), f32[16,64,128]{2,1,0:T(8,128)S(1)}, u32[]{:S(2)}, u32[]{:S(2)}) async-start(f32[16,64,128]{2,1,0:T(8,128)} %bitcast.18), calls=%async_computation | async-start | bytes 1048576 | tf_op jit(solution)/shard_map/all_to_all | solution.py:464
  31.1 4.1 %copy-start.1 = (f32[16,64,128]{2,1,0:T(8,128)}, f32[16,64,128]{2,1,0:T(8,128)S(1)}, u32[]{:S(2)}) copy-start(f32[16,64,128]{2,1,0:T(8,128)S(1)} %all-to-all-done.refs_1_) | copy-start | bytes 1572868
  31.1 4.1 %collective-permute-start.1 = (f32[64,128]{1,0:T(8,128)S(1)}, f32[64,128]{1,0:T(8,128)S(1)}, u32[]{:S(2)}, u32[]{:S(2)}) collective-permute-start(f32[64,128]{1,0:T(8,128)S(1)} %reduce_sum.36), channel_id=1, source_target_pairs={{0,64},{4,68},{8,72},{12,76},{16,80},{20,84},{24,88},{28,92},{32,9... | collective-permute-start | bytes 98312 | tf_op jit(solution)/shard_map/ppermute | solution.py:461
  35.2 3.2 %copy-start.13 = (f32[64,128]{1,0:T(8,128)}, f32[64,128]{1,0:T(8,128)S(1)}, u32[]{:S(2)}) copy-start(f32[64,128]{1,0:T(8,128)S(1)} %collective-permute-done.1.refs_2_) | copy-start | bytes 98308
  35.2 27.9 %collective-permute-start.3 = (bf16[512,1024]{1,0:T(8,128)(2,1)}, bf16[512,1024]{1,0:T(8,128)(2,1)S(1)}, u32[]{:S(2)}, u32[]{:S(2)}) collective-permute-start(bf16[512,1024]{1,0:T(8,128)(2,1)} %bitcast.20), channel_id=1, source_target_pairs={{0,2},{1,3},{2,0},{3,1},{4,6},{5,7},{6,4},{7,5},{8,10},{9,11},{10,... | collective-permute-start | bytes 3145736 | tf_op jit(solution)/shard_map/ppermute | solution.py:458
  40.2 12.0 %all-to-all-start.1 = ((bf16[16,64,128]{2,1,0:T(8,128)(2,1)}), bf16[16,64,128]{2,1,0:T(8,128)(2,1)S(1)}, u32[]{:S(2)}, u32[]{:S(2)}) async-start(bf16[16,64,128]{2,1,0:T(8,128)(2,1)} %shard_map.121), calls=%async_computation.1 | async-start | bytes 524288 | tf_op jit(solution)/shard_map/all_to_all | solution.py:464
  52.2 0.7 copy-start.7
  59.1 15.2 %collective-permute-start.13 = (bf16[512,512]{1,0:T(8,128)(2,1)}, bf16[512,512]{1,0:T(8,128)(2,1)}, u32[]{:S(2)}, u32[]{:S(2)}) collective-permute-start(bf16[512,512]{1,0:T(8,128)(2,1)} %get-tuple-element.33.refs_2_), channel_id=1, source_target_pairs={{0,64},{4,68},{8,72},{12,76},{16,80},{20,84},{24,88},{28,92},{32,9... | collective-permute-start | bytes 1572872 | tf_op jit(solution)/shard_map/ppermute | solution.py:461
  59.7 23.6 %collective-permute-start.11 = (bf16[512,512]{1,0:T(8,128)(2,1)}, bf16[512,512]{1,0:T(8,128)(2,1)}, u32[]{:S(2)}, u32[]{:S(2)}) collective-permute-start(bf16[512,512]{1,0:T(8,128)(2,1)} %get-tuple-element.33.refs_2_), channel_id=1, source_target_pairs={{0,66},{1,67},{2,64},{3,65},{4,70},{5,71},{6,68},{7,69},{8,74},{9,... | collective-permute-start | bytes 1572872 | tf_op jit(solution)/shard_map/ppermute | solution.py:513
  60.3 23.0 %collective-permute-start.6 = (bf16[512,512]{1,0:T(8,128)(2,1)}, bf16[512,512]{1,0:T(8,128)(2,1)S(1)}, u32[]{:S(2)}, u32[]{:S(2)}) collective-permute-start(bf16[512,512]{1,0:T(8,128)(2,1)} %get-tuple-element.37.refs_1_), channel_id=1, source_target_pairs={{0,2},{1,3},{2,0},{3,1},{4,6},{5,7},{6,4},{7,5},{8,10},{9,11},{10,... | collective-permute-start | bytes 1572872 | tf_op jit(solution)/shard_map/ppermute | solution.py:458
  63.2 1.0 copy-start.6
  64.1 10.1 %copy-start.3 = (bf16[512,512]{1,0:T(8,128)(2,1)S(1)}, bf16[512,512]{1,0:T(8,128)(2,1)}, u32[]{:S(2)}) copy-start(bf16[512,512]{1,0:T(8,128)(2,1)} %get-tuple-element.37.refs_1_) | copy-start | bytes 1572868
  74.2 17.8 %collective-permute-start.14 = (bf16[512,512]{1,0:T(8,128)(2,1)}, bf16[512,512]{1,0:T(8,128)(2,1)S(1)}, u32[]{:S(2)}, u32[]{:S(2)}) collective-permute-start(bf16[512,512]{1,0:T(8,128)(2,1)} %collective-permute-done.13.refs_2_), channel_id=1, source_target_pairs={{0,1},{1,0},{2,3},{3,2},{4,5},{5,4},{6,7},{7,6},{8,9},{9,8},{10,11... | collective-permute-start | bytes 1572872 | tf_op jit(solution)/shard_map/ppermute | solution.py:455
  74.2 17.8 %collective-permute-start.4 = (bf16[512,512]{1,0:T(8,128)(2,1)S(1)}, bf16[512,512]{1,0:T(8,128)(2,1)S(1)}, u32[]{:S(2)}, u32[]{:S(2)}) collective-permute-start(bf16[512,512]{1,0:T(8,128)(2,1)S(1)} %copy-done.3), channel_id=1, source_target_pairs={{0,1},{1,0},{2,3},{3,2},{4,5},{5,4},{6,7},{7,6},{8,9},{9,8},{10,11... | collective-permute-start | bytes 1572872 | tf_op jit(solution)/shard_map/ppermute | solution.py:455
  74.7 15.5 %all-to-all-start.2 = ((f32[16,64,128]{2,1,0:T(8,128)}), f32[16,64,128]{2,1,0:T(8,128)S(1)}, u32[]{:S(2)}, u32[]{:S(2)}) async-start(f32[16,64,128]{2,1,0:T(8,128)} %bitcast.19), calls=%async_computation.2 | async-start | bytes 1048576 | tf_op jit(solution)/shard_map/all_to_all | solution.py:464
  83.3 15.3 %collective-permute-start.12 = (bf16[512,512]{1,0:T(8,128)(2,1)}, bf16[512,512]{1,0:T(8,128)(2,1)}, u32[]{:S(2)}, u32[]{:S(2)}) collective-permute-start(bf16[512,512]{1,0:T(8,128)(2,1)} %collective-permute-done.11.refs_2_), channel_id=1, source_target_pairs={{0,1},{1,0},{2,3},{3,2},{4,5},{5,4},{6,7},{7,6},{8,9},{9,8},{10,11... | collective-permute-start | bytes 1572872 | tf_op jit(solution)/shard_map/ppermute | solution.py:455
  83.3 15.3 %copy-start.4 = (bf16[512,512]{1,0:T(8,128)(2,1)}, bf16[512,512]{1,0:T(8,128)(2,1)S(1)}, u32[]{:S(2)}) copy-start(bf16[512,512]{1,0:T(8,128)(2,1)S(1)} %collective-permute-done.6.refs_1_.refs_5_) | copy-start | bytes 1572868
  83.3 15.3 %collective-permute-start.8 = (bf16[512,512]{1,0:T(8,128)(2,1)S(1)}, bf16[512,512]{1,0:T(8,128)(2,1)}, u32[]{:S(2)}, u32[]{:S(2)}) collective-permute-start(bf16[512,512]{1,0:T(8,128)(2,1)S(1)} %collective-permute-done.6.refs_1_.refs_5_), channel_id=1, source_target_pairs={{0,1},{1,0},{2,3},{3,2},{4,5},{5,4},{6,7},{7,6},{8,9},{9,8},{10,11... | collective-permute-start | bytes 1572872 | tf_op jit(solution)/shard_map/ppermute | solution.py:455
  90.2 8.3 %copy-start.2 = (f32[16,64,128]{2,1,0:T(8,128)}, f32[16,64,128]{2,1,0:T(8,128)S(1)}, u32[]{:S(2)}) copy-start(f32[16,64,128]{2,1,0:T(8,128)S(1)} %all-to-all-done.2.refs_1_) | copy-start | bytes 1572868
  90.3 13.3 %collective-permute-start.10 = (f32[64,128]{1,0:T(8,128)S(1)}, f32[64,128]{1,0:T(8,128)S(1)}, u32[]{:S(2)}, u32[]{:S(2)}) collective-permute-start(f32[64,128]{1,0:T(8,128)S(1)} %reduce_sum.37), channel_id=1, source_target_pairs={{0,64},{4,68},{8,72},{12,76},{16,80},{20,84},{24,88},{28,92},{32,9... | collective-permute-start | bytes 98312 | tf_op jit(solution)/shard_map/ppermute | solution.py:461
  92.0 0.8 copy-start.11
  92.8 0.8 copy-start.5
  103.6 0.6 copy-start.12
  106.1 4.6 %copy-start.8 = (bf16[512,512]{1,0:T(8,128)(2,1)S(1)}, bf16[512,512]{1,0:T(8,128)(2,1)}, u32[]{:S(2)}) copy-start(bf16[512,512]{1,0:T(8,128)(2,1)} %get-tuple-element.33.refs_2_) | copy-start | bytes 1572868
  106.1 50.5 %all-to-all-start.3 = ((bf16[16,144,768]{2,1,0:T(8,128)(2,1)}), bf16[16,144,768]{2,1,0:T(8,128)(2,1)}, u32[]{:S(2)}, u32[]{:S(2)}) async-start(bf16[16,144,768]{2,1,0:T(8,128)(2,1)} %shard_map.127.refs_6_), calls=%async_computation.3 | async-start | bytes 7077888 | tf_op jit(solution)/shard_map/all_to_all | solution.py:464
  110.7 13.5 %collective-permute-start.7 = (bf16[512,512]{1,0:T(8,128)(2,1)S(1)}, bf16[512,512]{1,0:T(8,128)(2,1)S(1)}, u32[]{:S(2)}, u32[]{:S(2)}) collective-permute-start(bf16[512,512]{1,0:T(8,128)(2,1)S(1)} %copy-done.8), channel_id=1, source_target_pairs={{0,2},{1,3},{2,0},{3,1},{4,6},{5,7},{6,4},{7,5},{8,10},{9,11},{10,... | collective-permute-start | bytes 1572872 | tf_op jit(solution)/shard_map/ppermute | solution.py:458
  111.9 23.1 %collective-permute-start.5 = (bf16[512,512]{1,0:T(8,128)(2,1)S(1)}, bf16[512,512]{1,0:T(8,128)(2,1)S(1)}, u32[]{:S(2)}, u32[]{:S(2)}) collective-permute-start(bf16[512,512]{1,0:T(8,128)(2,1)S(1)} %copy-done.8), channel_id=1, source_target_pairs={{0,1},{1,0},{2,3},{3,2},{4,5},{5,4},{6,7},{7,6},{8,9},{9,8},{10,11... | collective-permute-start | bytes 1572872 | tf_op jit(solution)/shard_map/ppermute | solution.py:455
  124.2 10.7 %copy-start.9 = (bf16[512,512]{1,0:T(8,128)(2,1)}, bf16[512,512]{1,0:T(8,128)(2,1)S(1)}, u32[]{:S(2)}) copy-start(bf16[512,512]{1,0:T(8,128)(2,1)S(1)} %collective-permute-done.7.refs_6_) | copy-start | bytes 1572868
  124.2 10.8 %collective-permute-start.9 = (bf16[512,512]{1,0:T(8,128)(2,1)S(1)}, bf16[512,512]{1,0:T(8,128)(2,1)}, u32[]{:S(2)}, u32[]{:S(2)}) collective-permute-start(bf16[512,512]{1,0:T(8,128)(2,1)S(1)} %collective-permute-done.7.refs_6_), channel_id=1, source_target_pairs={{0,1},{1,0},{2,3},{3,2},{4,5},{5,4},{6,7},{7,6},{8,9},{9,8},{10,11... | collective-permute-start | bytes 1572872 | tf_op jit(solution)/shard_map/ppermute | solution.py:455
  135.0 0.8 copy-start.10
  159.0 5.7 %collective-permute-start.15 = (f32[64,768]{1,0:T(8,128)S(1)}, f32[64,768]{1,0:T(8,128)S(1)}, u32[]{:S(2)}, u32[]{:S(2)}) collective-permute-start(f32[64,768]{1,0:T(8,128)S(1)} %get-tuple-element.51), channel_id=1, source_target_pairs={{0,64},{4,68},{8,72},{12,76},{16,80},{20,84},{24,88},{28,92},{32,9... | collective-permute-start | bytes 589832 | tf_op jit(solution)/shard_map/ppermute | solution.py:461

commit v4 on v3

--- a/solution.py
+++ b/solution.py
@@ -10,7 +10,7 @@
 HD = 128
 F32 = jnp.float32
 BF16 = jnp.bfloat16
-VMEM_LIMIT = 62 * 1024 * 1024
+VMEM_LIMIT = 52 * 1024 * 1024
 
 NT = (((1,), (1,)), ((), ()))
 TN = (((0,), (0,)), ((), ()))
@@ -485,9 +485,9 @@
     got = swap_core(sent)
     local_state = block_states(after(key_rows, sent), value_rows)
     pieces = split_states(local_state)
-    total = jnp.sum(pieces, axis=0)
+    far_part = term([far], BF16, got, 0)[0]
+    total = jnp.sum(after(pieces, far_part), axis=0)
     offset = swap_lo(total)
-    far_part = term([after(far, total)], BF16, got, 0)[0]
     grad_far = swap_hi(after(far_part, offset, grad_pair))
     sums = sums_before(after(pieces, far_part), offset, False)
     grad_own = term([after(fsdp, sums)], F32, got, 1)[0]

time: 166 us -> 162 us (0.976)
  Pallas kernels: 63.7 us -> 58.6 us
  waiting for transfers between devices: 57.8 us -> 61.7 us
  local copies, waits for them, and re-layouts: 5.33 us -> 3.21 us
    ppermute x5, waiting for transfers between devices: 5.31 us -> 8.65 us  [swap_lo(): return lax.ppermute(array, 'ctx', lo_swap)]
    ppermute x3, waiting for transfers between devices: 12.3 us -> 15 us  [swap_hi(): return lax.ppermute(array, 'fsdp', hi_swap)]
    all_to_all x4, waiting for transfers between devices: 35.2 us -> 33.1 us  [exchange(): return lax.all_to_all(array, 'ctx', 0, 0, axis_index_groups=groups)]
    pallas_call x2, Pallas kernels: 3.62 us -> 1.54 us  [running_sum(): pl.pallas_call(kernel, grid=(1,), in_specs=in_specs, out_specs=out_spec,...]
    unnamed x28 -> x26, local copies, waits for them, and re-layouts: 4.66 us -> 3.12 us
  transfers between devices with their start and end apart: 20 -> 20, of which waited for: 8 -> 10; matrix products, arithmetic and copies ran while one was open for 0% -> 0% of each run, Pallas kernels for 34% -> 33%
where the time goes in v4:
time: 162 us
  waiting for transfers between devices  61.7 us (38%)
  Pallas kernels  58.6 us (36%)
  starting transfers between devices  34.1 us (21%)
  other arithmetic  3.29 us (2%)
  local copies, waits for them, and re-layouts  3.21 us (2%)
    all_to_all x4, waiting for transfers between devices, exchange(): return lax.all_to_all(array, 'ctx', 0, 0, axis_index_groups=groups)  33.1 us
    all_to_all x4, starting transfers between devices, exchange(): return lax.all_to_all(array, 'ctx', 0, 0, axis_index_groups=groups)  19.7 us
    ppermute x3, waiting for transfers between devices, swap_hi(): return lax.ppermute(array, 'fsdp', hi_swap)  15 us
    pallas_call x3, Pallas kernels, head_term(): pl.pallas_call(head_term_kernel if received is None else head_sum_kernel,...  11.9 us
    pallas_call x1, Pallas kernels, head_grads(): pl.pallas_call(kernel, grid=(heads // step,), in_specs=in_specs, out_spec...  10.1 us
    pallas_call x2, Pallas kernels, weight_grad(): pl.pallas_call(kernel, grid_spec=pltpu.PrefetchScalarGridSpec(num_scalar_...  9.52 us
    ppermute x5, waiting for transfers between devices, swap_lo(): return lax.ppermute(array, 'ctx', lo_swap)  8.65 us
    pallas_call x1, Pallas kernels, mix(): pl.pallas_call(kernel, grid_spec=pltpu.PrefetchScalarGridSpec(num_scalar_...  7.8 us
  transfers between devices with their start and end apart: 20, of which 10 were waited for; matrix products, arithmetic and copies ran while one was open for 0% of the time, Pallas kernels for 33%

profile of v4, /device:TPU:0, one launch (start us, length us, event | category | flops | bytes accessed | tf_op | source)
XLA Modules:
  0.0 161.7 jit_solution(10974725746255536159)
XLA Ops:
  0.7 0.1 pad_add_fusion.sel_ref
  0.7 5.2 %shard_map.118 = bf16[2,512,1024]{2,1,0:T(8,128)(2,1)} custom-call(s32[2]{0:T(128)S(1)} %pad_add_fusion.sel_ref, bf16[512,768]{1,0:T(8,128)(2,1)} %refs_5_.3, bf16[4096,768]{1,0:T(8,128)(2,1)} %refs_9_.1), custom_call_target="tpu_custom_call" | custom-call | flops 805306368 | bytes 3145728 | tf_op jit(solution)/shard_map/pallas_call | solution.py:140
  5.9 0.0 collective-permute-start
  5.9 1.7 %collective-permute-start.2 = (bf16[512,768]{1,0:T(8,128)(2,1)}, bf16[512,768]{1,0:T(8,128)(2,1)S(1)}, u32[]{:S(2)}, u32[]{:S(2)}) collective-permute-start(bf16[512,768]{1,0:T(8,128)(2,1)} %refs_5_.3), channel_id=1, source_target_pairs={{0,64},{4,68},{8,72},{12,76},{16,80},{20,84},{24,88},{28,92},{32,9... | collective-permute-start | bytes 2359304 | tf_op jit(solution)/shard_map/ppermute | solution.py:461
  7.6 2.5 %shard_map.119 = f32[8,128,128]{2,1,0:T(8,128)} custom-call(bf16[512,1024]{1,0:T(8,128)(2,1)S(1)} %copy-done, bf16[512,1024]{1,0:T(8,128)(2,1)} %refs_1_.4), custom_call_target="tpu_custom_call" | custom-call | flops 134217728 | bytes 2097152 | tf_op jit(solution)/shard_map/pallas_call | solution.py:57
  10.1 7.9 %all-to-all-start = ((f32[16,64,128]{2,1,0:T(8,128)}), f32[16,64,128]{2,1,0:T(8,128)S(1)}, u32[]{:S(2)}, u32[]{:S(2)}) async-start(f32[16,64,128]{2,1,0:T(8,128)} %bitcast.7), calls=%async_computation | async-start | bytes 1048576 | tf_op jit(solution)/shard_map/all_to_all | solution.py:464
  18.0 1.3 copy-done.9
  19.3 2.9 %shard_map.120 = bf16[1,512,1024]{2,1,0:T(8,128)(2,1)S(1)} custom-call(s32[1]{0:T(128)} %bitcast.4.sel_ref, bf16[512,768]{1,0:T(8,128)(2,1)} %refs_5_.3, bf16[4096,768]{1,0:T(8,128)(2,1)} %refs_9_.1, bf16[2,512,1024]{2,1,0:T(8,128)(2,1)} %copy-done.9), custom_call_target="tpu_custom_call" | custom-call | flops 805306368 | bytes 3145728 | tf_op jit(solution)/shard_map/pallas_call | solution.py:140
  22.2 7.7 %all-to-all-done.refs_1_ = f32[16,64,128]{2,1,0:T(8,128)S(1)} async-done(((f32[16,64,128]{2,1,0:T(8,128)}), f32[16,64,128]{2,1,0:T(8,128)S(1)}, u32[]{:S(2)}, u32[]{:S(2)}) %all-to-all-start) | async-done | bytes 524320 | tf_op jit(solution)/shard_map/all_to_all | solution.py:464
  29.9 0.5 collective-permute-start.1
  30.4 0.0 collective-permute-done.2.refs_6_
  30.4 3.5 %collective-permute-done.1.refs_2_ = f32[64,128]{1,0:T(8,128)S(1)} collective-permute-done((f32[64,128]{1,0:T(8,128)S(1)}, f32[64,128]{1,0:T(8,128)S(1)}, u32[]{:S(2)}, u32[]{:S(2)}) %collective-permute-start.1) | collective-permute-done | bytes 32800 | tf_op jit(solution)/shard_map/ppermute | solution.py:461
  33.9 3.3 %collective-permute-start.3 = (bf16[512,1024]{1,0:T(8,128)(2,1)S(1)}, bf16[512,1024]{1,0:T(8,128)(2,1)}, u32[]{:S(2)}, u32[]{:S(2)}) collective-permute-start(bf16[512,1024]{1,0:T(8,128)(2,1)S(1)} %bitcast.16), channel_id=1, source_target_pairs={{0,2},{1,3},{2,0},{3,1},{4,6},{5,7},{6,4},{7,5},{8,10},{9,11},{10,... | collective-permute-start | bytes 3145736 | tf_op jit(solution)/shard_map/ppermute | solution.py:458
  37.1 0.7 shard_map.121
  37.9 3.5 %all-to-all-start.1 = ((bf16[16,64,128]{2,1,0:T(8,128)(2,1)}), bf16[16,64,128]{2,1,0:T(8,128)(2,1)S(1)}, u32[]{:S(2)}, u32[]{:S(2)}) async-start(bf16[16,64,128]{2,1,0:T(8,128)(2,1)} %shard_map.121), calls=%async_computation.1 | async-start | bytes 524288 | tf_op jit(solution)/shard_map/all_to_all | solution.py:464
  41.4 0.0 copy-start.7
  41.4 3.8 %shard_map.122 = f32[1,512,1024]{2,1,0:T(8,128)} custom-call(s32[1]{0:T(128)} %bitcast.9.sel_ref, bf16[512,768]{1,0:T(8,128)(2,1)} %refs_5_.3, bf16[4096,768]{1,0:T(8,128)(2,1)} %refs_9_.1, bf16[2,512,1024]{2,1,0:T(8,128)(2,1)} %copy-done.9), custom_call_target="tpu_custom_call" | custom-call | flops 805306368 | bytes 3145728 | tf_op jit(solution)/shard_map/pallas_call | solution.py:140
  45.2 4.6 %all-to-all-done.1 = bf16[16,64,128]{2,1,0:T(8,128)(2,1)S(1)} async-done(((bf16[16,64,128]{2,1,0:T(8,128)(2,1)}), bf16[16,64,128]{2,1,0:T(8,128)(2,1)S(1)}, u32[]{:S(2)}, u32[]{:S(2)}) %all-to-all-start.1) | async-done | bytes 262176 | tf_op jit(solution)/shard_map/all_to_all | solution.py:464
  49.9 6.0 %shard_map.123 = (bf16[512,512]{1,0:T(8,128)(2,1)S(1)}, bf16[512,512]{1,0:T(8,128)(2,1)S(1)}, f32[512,1024]{1,0:T(8,128)}) custom-call(s32[1]{0:T(128)} %bitcast.1.refs_0_, bf16[512,1024]{1,0:T(8,128)(2,1)} %refs_0_.2, bf16[512,1024]{1,0:T(8,128)(2,1)} %refs_0_.3, bf16[512,1024]{1,0:T(8,128)(2,1)} %refs_1_.4, bf16[512,1024]{1,0:T(8,128)(2,1)} %g_ref.1, ...), custom_call_target="tpu_custom_call" | custom-call | flops 1073741824 | bytes 7340032 | tf_op jit(solution)/shard_map/pallas_call | solution.py:216
  55.8 0.0 collective-permute-start.13
  55.9 0.8 collective-permute-start.11
  56.7 3.2 %collective-permute-start.6 = (bf16[512,512]{1,0:T(8,128)(2,1)S(1)}, bf16[512,512]{1,0:T(8,128)(2,1)S(1)}, u32[]{:S(2)}, u32[]{:S(2)}) collective-permute-start(bf16[512,512]{1,0:T(8,128)(2,1)S(1)} %get-tuple-element.35.refs_1_), channel_id=1, source_target_pairs={{0,2},{1,3},{2,0},{3,1},{4,6},{5,7},{6,4},{7,5},{8,10},{9,11},{10,... | collective-permute-start | bytes 1572872 | tf_op jit(solution)/shard_map/ppermute | solution.py:458
  59.9 1.7 %collective-permute-done.3.far_ref = bf16[512,1024]{1,0:T(8,128)(2,1)} collective-permute-done((bf16[512,1024]{1,0:T(8,128)(2,1)S(1)}, bf16[512,1024]{1,0:T(8,128)(2,1)}, u32[]{:S(2)}, u32[]{:S(2)}) %collective-permute-start.3) | collective-permute-done | bytes 1048608 | tf_op jit(solution)/shard_map/ppermute | solution.py:458
  61.6 5.3 %shard_map.124 = (bf16[512,1024]{1,0:T(8,128)(2,1)}, bf16[512,1024]{1,0:T(8,128)(2,1)S(1)}, bf16[512,1024]{1,0:T(8,128)(2,1)}, f32[8,128,128]{2,1,0:T(8,128)}) custom-call(bf16[512,1024]{1,0:T(8,128)(2,1)} %refs_0_.2, bf16[512,1024]{1,0:T(8,128)(2,1)} %g_ref.1, f32[1,1024]{1,0:T(1,128)S(1)} %bitcast.20, f32[512,1024]{1,0:T(8,128)} %get-tuple-element.32.attn_ref, ...), custom_call_target="tpu_custom_call" | custom-call | flops 134217728 | bytes 10485760 | tf_op jit(solution)/shard_map/pallas_call | solution.py:255
  66.9 1.0 copy-done.8
  67.9 4.1 %collective-permute-done.13.refs_2_ = bf16[512,512]{1,0:T(8,128)(2,1)} collective-permute-done((bf16[512,512]{1,0:T(8,128)(2,1)S(1)}, bf16[512,512]{1,0:T(8,128)(2,1)}, u32[]{:S(2)}, u32[]{:S(2)}) %collective-permute-start.13) | collective-permute-done | bytes 524320 | tf_op jit(solution)/shard_map/ppermute | solution.py:461
  72.0 0.5 collective-permute-start.4
  72.5 3.7 %all-to-all-start.2 = ((f32[16,64,128]{2,1,0:T(8,128)}), f32[16,64,128]{2,1,0:T(8,128)S(1)}, u32[]{:S(2)}, u32[]{:S(2)}) async-start(f32[16,64,128]{2,1,0:T(8,128)} %bitcast.14), calls=%async_computation.2 | async-start | bytes 1048576 | tf_op jit(solution)/shard_map/all_to_all | solution.py:464
  76.2 4.9 %collective-permute-done.11.refs_2_ = bf16[512,512]{1,0:T(8,128)(2,1)} collective-permute-done((bf16[512,512]{1,0:T(8,128)(2,1)S(1)}, bf16[512,512]{1,0:T(8,128)(2,1)}, u32[]{:S(2)}, u32[]{:S(2)}) %collective-permute-start.11) | collective-permute-done | bytes 524320 | tf_op jit(solution)/shard_map/ppermute | solution.py:513
  81.1 0.5 collective-permute-start.8
  81.6 6.4 %all-to-all-done.2.refs_1_ = f32[16,64,128]{2,1,0:T(8,128)S(1)} async-done(((f32[16,64,128]{2,1,0:T(8,128)}), f32[16,64,128]{2,1,0:T(8,128)S(1)}, u32[]{:S(2)}, u32[]{:S(2)}) %all-to-all-start.2) | async-done | bytes 524320 | tf_op jit(solution)/shard_map/all_to_all | solution.py:464
  88.0 2.8 %collective-permute-start.10 = (f32[64,128]{1,0:T(8,128)S(1)}, f32[64,128]{1,0:T(8,128)S(1)}, u32[]{:S(2)}, u32[]{:S(2)}) collective-permute-start(f32[64,128]{1,0:T(8,128)S(1)} %reduce_sum.37), channel_id=1, source_target_pairs={{0,64},{4,68},{8,72},{12,76},{16,80},{20,84},{24,88},{28,92},{32,9... | collective-permute-start | bytes 98312 | tf_op jit(solution)/shard_map/ppermute | solution.py:461
  90.9 0.8 copy-done.12
  91.7 4.6 %shard_map.125.refs_7_ = bf16[16,144,768]{2,1,0:T(8,128)(2,1)} custom-call(s32[1]{0:T(128)} %bitcast.15.refs_0_, bf16[512,512]{1,0:T(8,128)(2,1)S(1)} %get-tuple-element.35.refs_1_, bf16[512,512]{1,0:T(8,128)(2,1)} %collective-permute-done.13.refs_2_, bf16[512,512]{1,0:T(8,128)(2,1)S(1)} %collective-permute-done.4.refs_3_, bf16[512,512]{1,0:T(8,128)(2,1)} %copy-done.12, ...), custom_call_target="tpu_custom_call" | custom-call | flops 1610612736 | bytes 1572864 | tf_op jit(solution)/shard_map/pallas_call | solution.py:426
  96.3 4.9 %shard_map.126.refs_3_ = bf16[16,144,768]{2,1,0:T(8,128)(2,1)} custom-call(s32[1]{0:T(128)} %bitcast.15.refs_0_, bf16[512,512]{1,0:T(8,128)(2,1)S(1)} %collective-permute-done.6.refs_1_.refs_5_, bf16[512,512]{1,0:T(8,128)(2,1)} %collective-permute-done.11.refs_2_, ...), custom_call_target="tpu_custom_call", output_to_operand_aliasing={{}: (7, {})} | custom-call | flops 1610612736 | bytes 1572864 | tf_op jit(solution)/shard_map/pallas_call | solution.py:426
  101.2 0.8 shard_map.127.refs_6_
  102.0 4.6 %all-to-all-start.3 = ((bf16[16,144,768]{2,1,0:T(8,128)(2,1)}), bf16[16,144,768]{2,1,0:T(8,128)(2,1)}, u32[]{:S(2)}, u32[]{:S(2)}) async-start(bf16[16,144,768]{2,1,0:T(8,128)(2,1)} %shard_map.127.refs_6_), calls=%async_computation.3 | async-start | bytes 7077888 | tf_op jit(solution)/shard_map/all_to_all | solution.py:464
  106.7 0.4 collective-permute-start.7
  107.1 13.3 %collective-permute-done.7.refs_6_ = bf16[512,512]{1,0:T(8,128)(2,1)S(1)} collective-permute-done((bf16[512,512]{1,0:T(8,128)(2,1)S(1)}, bf16[512,512]{1,0:T(8,128)(2,1)S(1)}, u32[]{:S(2)}, u32[]{:S(2)}) %collective-permute-start.7) | collective-permute-done | bytes 524320 | tf_op jit(solution)/shard_map/ppermute | solution.py:458
  120.4 0.1 stack.46.refs_0_
  120.5 10.1 %shard_map.128 = (bf16[512,1024]{1,0:T(8,128)(2,1)}, f32[512,1024]{1,0:T(8,128)}, f32[512,1024]{1,0:T(8,128)}) custom-call(bf16[512,1024]{1,0:T(8,128)(2,1)S(1)} %copy-done.2, bf16[512,1024]{1,0:T(8,128)(2,1)} %refs_0_.3, bf16[512,1024]{1,0:T(8,128)(2,1)} %refs_1_.4, bf16[512,1024]{1,0:T(8,128)(2,1)} %copy-done.8, ...), custom_call_target="tpu_custom_call" | custom-call | flops 2684354560 | bytes 10485760 | tf_op jit(solution)/shard_map/pallas_call | solution.py:303
  130.5 7.8 %shard_map.129 = bf16[512,768]{1,0:T(8,128)(2,1)} custom-call(s32[16]{0:T(128)S(1)} %stack.46.refs_0_, bf16[512,512]{1,0:T(8,128)(2,1)S(1)} %get-tuple-element.35.refs_1_, bf16[512,512]{1,0:T(8,128)(2,1)S(1)} %copy-done.6, bf16[512,512]{1,0:T(8,128)(2,1)S(1)} %collective-permute-done.4.refs_3_, bf16[512,512]{1,0:T(8,128)(2,1)} %collective-permute-done.5.refs_4_, ...), custom_call_target="tpu_custom_call" | custom-call | flops 3221225472 | bytes 6291456 | tf_op jit(solution)/shard_map/pallas_call | solution.py:378
  138.4 14.5 %all-to-all-done.3.refs_4_ = bf16[16,144,768]{2,1,0:T(8,128)(2,1)} async-done(((bf16[16,144,768]{2,1,0:T(8,128)(2,1)}), bf16[16,144,768]{2,1,0:T(8,128)(2,1)}, u32[]{:S(2)}, u32[]{:S(2)}) %all-to-all-start.3) | async-done | bytes 3538976 | tf_op jit(solution)/shard_map/all_to_all | solution.py:464
  152.8 2.3 %convert_reduce_fusion.1 = (f32[64,768]{1,0:T(8,128)S(1)}, f32[64,768]{1,0:T(8,128)S(1)}) fusion(bf16[16,144,768]{2,1,0:T(8,128)(2,1)} %all-to-all-done.3.refs_4_), kind=kLoop, calls=%fused_computation.1 | loop fusion | flops 3047424 | bytes 3538944 | tf_op jit(solution)/shard_map/reduce_sum | solution.py:546
  155.2 0.7 collective-permute-start.15
  155.9 4.0 %shard_map.130 = (bf16[512,1024]{1,0:T(8,128)(2,1)}, bf16[512,1024]{1,0:T(8,128)(2,1)}) custom-call(bf16[512,1024]{1,0:T(8,128)(2,1)S(1)} %copy-done.1, bf16[512,1024]{1,0:T(8,128)(2,1)} %refs_1_.4, f32[512,1024]{1,0:T(8,128)} %get-tuple-element.41.refs_2_, f32[512,1024]{1,0:T(8,128)} %get-tuple-element.42.refs_3_, bf16[16,144,768]{2,1,0:T(8,128)(2,1)} %all-to-all-done.3.refs_4_), custom_call_target="tpu_custom_call" | custom-call | flops 268435456 | bytes 8388608 | tf_op jit(solution)/shard_map/pallas_call | solution.py:346
  159.9 1.1 collective-permute-done.15
  161.0 0.8 maximum_select_fusion
  (38 shorter events, 0.2 us)
Async XLA Ops:
  0.7 6.8 %copy-start = (bf16[512,1024]{1,0:T(8,128)(2,1)S(1)}, bf16[512,1024]{1,0:T(8,128)(2,1)}, u32[]{:S(2)}) copy-start(bf16[512,1024]{1,0:T(8,128)(2,1)} %refs_0_.3) | copy-start | bytes 3145732
  5.9 12.1 %collective-permute-start = (bf16[2,512,1024]{2,1,0:T(8,128)(2,1)}, bf16[2,512,1024]{2,1,0:T(8,128)(2,1)S(1)}, u32[]{:S(2)}, u32[]{:S(2)}) collective-permute-start(bf16[2,512,1024]{2,1,0:T(8,128)(2,1)} %shard_map.118), channel_id=1, source_target_pairs={{0,1},{1,0},{2,3},{3,2},{4,5},{5,4},{6,7},{7,6},{8,9},{9,8},{10,11... | collective-permute-start | bytes 6291464 | tf_op jit(solution)/shard_map/ppermute | solution.py:455
  5.9 24.5 %collective-permute-start.2 = (bf16[512,768]{1,0:T(8,128)(2,1)}, bf16[512,768]{1,0:T(8,128)(2,1)S(1)}, u32[]{:S(2)}, u32[]{:S(2)}) collective-permute-start(bf16[512,768]{1,0:T(8,128)(2,1)} %refs_5_.3), channel_id=1, source_target_pairs={{0,64},{4,68},{8,72},{12,76},{16,80},{20,84},{24,88},{28,92},{32,9... | collective-permute-start | bytes 2359304 | tf_op jit(solution)/shard_map/ppermute | solution.py:461
  10.1 19.8 %all-to-all-start = ((f32[16,64,128]{2,1,0:T(8,128)}), f32[16,64,128]{2,1,0:T(8,128)S(1)}, u32[]{:S(2)}, u32[]{:S(2)}) async-start(f32[16,64,128]{2,1,0:T(8,128)} %bitcast.7), calls=%async_computation | async-start | bytes 1048576 | tf_op jit(solution)/shard_map/all_to_all | solution.py:464
  18.0 1.3 copy-start.9
  29.9 4.0 %collective-permute-start.1 = (f32[64,128]{1,0:T(8,128)S(1)}, f32[64,128]{1,0:T(8,128)S(1)}, u32[]{:S(2)}, u32[]{:S(2)}) collective-permute-start(f32[64,128]{1,0:T(8,128)S(1)} %reduce_sum.36), channel_id=1, source_target_pairs={{0,64},{4,68},{8,72},{12,76},{16,80},{20,84},{24,88},{28,92},{32,9... | collective-permute-start | bytes 98312 | tf_op jit(solution)/shard_map/ppermute | solution.py:461
  30.4 11.0 %copy-start.10 = (bf16[512,768]{1,0:T(8,128)(2,1)}, bf16[512,768]{1,0:T(8,128)(2,1)S(1)}, u32[]{:S(2)}) copy-start(bf16[512,768]{1,0:T(8,128)(2,1)S(1)} %collective-permute-done.2.refs_6_) | copy-start | bytes 2359300
  33.9 27.7 %collective-permute-start.3 = (bf16[512,1024]{1,0:T(8,128)(2,1)S(1)}, bf16[512,1024]{1,0:T(8,128)(2,1)}, u32[]{:S(2)}, u32[]{:S(2)}) collective-permute-start(bf16[512,1024]{1,0:T(8,128)(2,1)S(1)} %bitcast.16), channel_id=1, source_target_pairs={{0,2},{1,3},{2,0},{3,1},{4,6},{5,7},{6,4},{7,5},{8,10},{9,11},{10,... | collective-permute-start | bytes 3145736 | tf_op jit(solution)/shard_map/ppermute | solution.py:458
  37.9 12.0 %all-to-all-start.1 = ((bf16[16,64,128]{2,1,0:T(8,128)(2,1)}), bf16[16,64,128]{2,1,0:T(8,128)(2,1)S(1)}, u32[]{:S(2)}, u32[]{:S(2)}) async-start(bf16[16,64,128]{2,1,0:T(8,128)(2,1)} %shard_map.121), calls=%async_computation.1 | async-start | bytes 524288 | tf_op jit(solution)/shard_map/all_to_all | solution.py:464
  41.4 8.4 %copy-start.7 = (f32[1024]{0:T(1024)S(1)}, f32[1024]{0:T(1024)}, u32[]{:S(2)}) copy-start(f32[1024]{0:T(1024)} %param.11) | copy-start | bytes 12292
  55.8 11.1 %copy-start.5 = (bf16[512,512]{1,0:T(8,128)(2,1)}, bf16[512,512]{1,0:T(8,128)(2,1)S(1)}, u32[]{:S(2)}) copy-start(bf16[512,512]{1,0:T(8,128)(2,1)S(1)} %get-tuple-element.31.refs_2_) | copy-start | bytes 1572868
  55.8 16.1 %collective-permute-start.13 = (bf16[512,512]{1,0:T(8,128)(2,1)S(1)}, bf16[512,512]{1,0:T(8,128)(2,1)}, u32[]{:S(2)}, u32[]{:S(2)}) collective-permute-start(bf16[512,512]{1,0:T(8,128)(2,1)S(1)} %get-tuple-element.31.refs_2_), channel_id=1, source_target_pairs={{0,64},{4,68},{8,72},{12,76},{16,80},{20,84},{24,88},{28,92},{32,9... | collective-permute-start | bytes 1572872 | tf_op jit(solution)/shard_map/ppermute | solution.py:461
  55.9 25.2 %collective-permute-start.11 = (bf16[512,512]{1,0:T(8,128)(2,1)S(1)}, bf16[512,512]{1,0:T(8,128)(2,1)}, u32[]{:S(2)}, u32[]{:S(2)}) collective-permute-start(bf16[512,512]{1,0:T(8,128)(2,1)S(1)} %get-tuple-element.31.refs_2_), channel_id=1, source_target_pairs={{0,66},{1,67},{2,64},{3,65},{4,70},{5,71},{6,68},{7,69},{8,74},{9,... | collective-permute-start | bytes 1572872 | tf_op jit(solution)/shard_map/ppermute | solution.py:513
  56.7 24.4 %collective-permute-start.6 = (bf16[512,512]{1,0:T(8,128)(2,1)S(1)}, bf16[512,512]{1,0:T(8,128)(2,1)S(1)}, u32[]{:S(2)}, u32[]{:S(2)}) collective-permute-start(bf16[512,512]{1,0:T(8,128)(2,1)S(1)} %get-tuple-element.35.refs_1_), channel_id=1, source_target_pairs={{0,2},{1,3},{2,0},{3,1},{4,6},{5,7},{6,4},{7,5},{8,10},{9,11},{10,... | collective-permute-start | bytes 1572872 | tf_op jit(solution)/shard_map/ppermute | solution.py:458
  66.9 1.0 copy-start.8
  72.0 18.9 %collective-permute-start.14 = (bf16[512,512]{1,0:T(8,128)(2,1)}, bf16[512,512]{1,0:T(8,128)(2,1)S(1)}, u32[]{:S(2)}, u32[]{:S(2)}) collective-permute-start(bf16[512,512]{1,0:T(8,128)(2,1)} %collective-permute-done.13.refs_2_), channel_id=1, source_target_pairs={{0,1},{1,0},{2,3},{3,2},{4,5},{5,4},{6,7},{7,6},{8,9},{9,8},{10,11... | collective-permute-start | bytes 1572872 | tf_op jit(solution)/shard_map/ppermute | solution.py:455
  72.0 18.9 %collective-permute-start.4 = (bf16[512,512]{1,0:T(8,128)(2,1)S(1)}, bf16[512,512]{1,0:T(8,128)(2,1)S(1)}, u32[]{:S(2)}, u32[]{:S(2)}) collective-permute-start(bf16[512,512]{1,0:T(8,128)(2,1)S(1)} %get-tuple-element.35.refs_1_), channel_id=1, source_target_pairs={{0,1},{1,0},{2,3},{3,2},{4,5},{5,4},{6,7},{7,6},{8,9},{9,8},{10,11... | collective-permute-start | bytes 1572872 | tf_op jit(solution)/shard_map/ppermute | solution.py:455
  72.5 15.5 %all-to-all-start.2 = ((f32[16,64,128]{2,1,0:T(8,128)}), f32[16,64,128]{2,1,0:T(8,128)S(1)}, u32[]{:S(2)}, u32[]{:S(2)}) async-start(f32[16,64,128]{2,1,0:T(8,128)} %bitcast.14), calls=%async_computation.2 | async-start | bytes 1048576 | tf_op jit(solution)/shard_map/all_to_all | solution.py:464
  81.1 15.2 %collective-permute-start.12 = (bf16[512,512]{1,0:T(8,128)(2,1)}, bf16[512,512]{1,0:T(8,128)(2,1)}, u32[]{:S(2)}, u32[]{:S(2)}) collective-permute-start(bf16[512,512]{1,0:T(8,128)(2,1)} %collective-permute-done.11.refs_2_), channel_id=1, source_target_pairs={{0,1},{1,0},{2,3},{3,2},{4,5},{5,4},{6,7},{7,6},{8,9},{9,8},{10,11... | collective-permute-start | bytes 1572872 | tf_op jit(solution)/shard_map/ppermute | solution.py:455
  81.1 15.2 %copy-start.3 = (bf16[512,512]{1,0:T(8,128)(2,1)}, bf16[512,512]{1,0:T(8,128)(2,1)S(1)}, u32[]{:S(2)}) copy-start(bf16[512,512]{1,0:T(8,128)(2,1)S(1)} %collective-permute-done.6.refs_1_.refs_5_) | copy-start | bytes 1572868
  81.1 15.2 %collective-permute-start.8 = (bf16[512,512]{1,0:T(8,128)(2,1)S(1)}, bf16[512,512]{1,0:T(8,128)(2,1)S(1)}, u32[]{:S(2)}, u32[]{:S(2)}) collective-permute-start(bf16[512,512]{1,0:T(8,128)(2,1)S(1)} %collective-permute-done.6.refs_1_.refs_5_), channel_id=1, source_target_pairs={{0,1},{1,0},{2,3},{3,2},{4,5},{5,4},{6,7},{7,6},{8,9},{9,8},{10,11... | collective-permute-start | bytes 1572872 | tf_op jit(solution)/shard_map/ppermute | solution.py:455
  88.0 13.2 %collective-permute-start.10 = (f32[64,128]{1,0:T(8,128)S(1)}, f32[64,128]{1,0:T(8,128)S(1)}, u32[]{:S(2)}, u32[]{:S(2)}) collective-permute-start(f32[64,128]{1,0:T(8,128)S(1)} %reduce_sum.37), channel_id=1, source_target_pairs={{0,64},{4,68},{8,72},{12,76},{16,80},{20,84},{24,88},{28,92},{32,9... | collective-permute-start | bytes 98312 | tf_op jit(solution)/shard_map/ppermute | solution.py:461
  90.9 0.8 copy-start.12
  96.3 4.9 %copy-start.4 = (bf16[512,512]{1,0:T(8,128)(2,1)}, bf16[512,512]{1,0:T(8,128)(2,1)S(1)}, u32[]{:S(2)}) copy-start(bf16[512,512]{1,0:T(8,128)(2,1)S(1)} %collective-permute-done.8.refs_3_.refs_7_) | copy-start | bytes 1572868
  102.0 4.7 %copy-start.6 = (bf16[512,512]{1,0:T(8,128)(2,1)S(1)}, bf16[512,512]{1,0:T(8,128)(2,1)}, u32[]{:S(2)}) copy-start(bf16[512,512]{1,0:T(8,128)(2,1)} %copy-done.5) | copy-start | bytes 1572868
  102.0 18.4 %copy-start.2 = (bf16[512,1024]{1,0:T(8,128)(2,1)S(1)}, bf16[512,1024]{1,0:T(8,128)(2,1)}, u32[]{:S(2)}) copy-start(bf16[512,1024]{1,0:T(8,128)(2,1)} %refs_0_.2) | copy-start | bytes 3145732
  102.0 50.8 %all-to-all-start.3 = ((bf16[16,144,768]{2,1,0:T(8,128)(2,1)}), bf16[16,144,768]{2,1,0:T(8,128)(2,1)}, u32[]{:S(2)}, u32[]{:S(2)}) async-start(bf16[16,144,768]{2,1,0:T(8,128)(2,1)} %shard_map.127.refs_6_), calls=%async_computation.3 | async-start | bytes 7077888 | tf_op jit(solution)/shard_map/all_to_all | solution.py:464
  106.7 13.7 %collective-permute-start.7 = (bf16[512,512]{1,0:T(8,128)(2,1)S(1)}, bf16[512,512]{1,0:T(8,128)(2,1)S(1)}, u32[]{:S(2)}, u32[]{:S(2)}) collective-permute-start(bf16[512,512]{1,0:T(8,128)(2,1)S(1)} %copy-done.6), channel_id=1, source_target_pairs={{0,2},{1,3},{2,0},{3,1},{4,6},{5,7},{6,4},{7,5},{8,10},{9,11},{10,... | collective-permute-start | bytes 1572872 | tf_op jit(solution)/shard_map/ppermute | solution.py:458
  107.1 23.5 %collective-permute-start.5 = (bf16[512,512]{1,0:T(8,128)(2,1)S(1)}, bf16[512,512]{1,0:T(8,128)(2,1)}, u32[]{:S(2)}, u32[]{:S(2)}) collective-permute-start(bf16[512,512]{1,0:T(8,128)(2,1)S(1)} %copy-done.6), channel_id=1, source_target_pairs={{0,1},{1,0},{2,3},{3,2},{4,5},{5,4},{6,7},{7,6},{8,9},{9,8},{10,11... | collective-permute-start | bytes 1572872 | tf_op jit(solution)/shard_map/ppermute | solution.py:455
  120.4 10.2 %copy-start.11 = (bf16[512,512]{1,0:T(8,128)(2,1)}, bf16[512,512]{1,0:T(8,128)(2,1)S(1)}, u32[]{:S(2)}) copy-start(bf16[512,512]{1,0:T(8,128)(2,1)S(1)} %collective-permute-done.7.refs_6_) | copy-start | bytes 1572868
  120.4 10.2 %collective-permute-start.9 = (bf16[512,512]{1,0:T(8,128)(2,1)S(1)}, bf16[512,512]{1,0:T(8,128)(2,1)}, u32[]{:S(2)}, u32[]{:S(2)}) collective-permute-start(bf16[512,512]{1,0:T(8,128)(2,1)S(1)} %collective-permute-done.7.refs_6_), channel_id=1, source_target_pairs={{0,1},{1,0},{2,3},{3,2},{4,5},{5,4},{6,7},{7,6},{8,9},{9,8},{10,11... | collective-permute-start | bytes 1572872 | tf_op jit(solution)/shard_map/ppermute | solution.py:455
  138.3 17.5 %copy-start.1 = (bf16[512,1024]{1,0:T(8,128)(2,1)S(1)}, bf16[512,1024]{1,0:T(8,128)(2,1)}, u32[]{:S(2)}) copy-start(bf16[512,1024]{1,0:T(8,128)(2,1)} %refs_0_.3) | copy-start | bytes 3145732
  155.2 5.7 %collective-permute-start.15 = (f32[64,768]{1,0:T(8,128)S(1)}, f32[64,768]{1,0:T(8,128)S(1)}, u32[]{:S(2)}, u32[]{:S(2)}) collective-permute-start(f32[64,768]{1,0:T(8,128)S(1)} %get-tuple-element.49), channel_id=1, source_target_pairs={{0,64},{4,68},{8,72},{12,76},{16,80},{20,84},{24,88},{28,92},{32,9... | collective-permute-start | bytes 589832 | tf_op jit(solution)/shard_map/ppermute | solution.py:461

commit v5 on v4

--- a/solution.py
+++ b/solution.py
@@ -10,7 +10,7 @@
 HD = 128
 F32 = jnp.float32
 BF16 = jnp.bfloat16
-VMEM_LIMIT = 52 * 1024 * 1024
+VMEM_LIMIT = 44 * 1024 * 1024
 
 NT = (((1,), (1,)), ((), ()))
 TN = (((0,), (0,)), ((), ()))

time: 162 us -> 162 us (level)
  local copies, waits for them, and re-layouts: 3.21 us -> 28.5 us
  waiting for transfers between devices: 61.7 us -> 47.3 us
  Pallas kernels: 58.6 us -> 49.4 us
  other arithmetic: 3.29 us -> 1.37 us
    unnamed x26 -> x72, local copies, waits for them, and re-layouts: 3.12 us -> 28.4 us
    all_to_all x4, waiting for transfers between devices: 33.1 us -> 20.2 us  [exchange(): return lax.all_to_all(array, 'ctx', 0, 0, axis_index_groups=groups)]
    reduce_sum x1, other arithmetic: 2.35 us -> 0.42 us  [per_device(): near_sum = jnp.sum(parts[:, :size].astype(F32), axis=0)]
    pallas_call x1, Pallas kernels: 4.03 us -> 2.35 us  [later_grads(): pl.pallas_call(kernel, grid=(heads // step,), in_specs=in_specs, out_spec...]
  transfers between devices with their start and end apart: 20 -> 20, of which waited for: 10 -> 9; matrix products, arithmetic and copies ran while one was open for 0% -> 0% of each run, Pallas kernels for 33% -> 27%
where the time goes in v5:
time: 162 us; the launch traced here: 161 us
  Pallas kernels  49.4 us (30%)
  waiting for transfers between devices  47.3 us (29%)
  starting transfers between devices  33 us (20%)
  local copies, waits for them, and re-layouts  28.5 us (18%)
    unnamed x72, local copies, waits for them, and re-layouts  28.4 us
    all_to_all x4, waiting for transfers between devices, exchange(): return lax.all_to_all(array, 'ctx', 0, 0, axis_index_groups=groups)  20.2 us
    all_to_all x4, starting transfers between devices, exchange(): return lax.all_to_all(array, 'ctx', 0, 0, axis_index_groups=groups)  19.2 us
    ppermute x3, waiting for transfers between devices, swap_hi(): return lax.ppermute(array, 'fsdp', hi_swap)  14.7 us
    pallas_call x3, Pallas kernels, head_term(): pl.pallas_call(head_term_kernel if received is None else head_sum_kernel,...  10.4 us
    pallas_call x2, Pallas kernels, weight_grad(): pl.pallas_call(kernel, grid_spec=pltpu.PrefetchScalarGridSpec(num_scalar_...  9.06 us
    pallas_call x1, Pallas kernels, head_grads(): pl.pallas_call(kernel, grid=(heads // step,), in_specs=in_specs, out_spec...  9.06 us
    pallas_call x1, Pallas kernels, mix(): pl.pallas_call(kernel, grid_spec=pltpu.PrefetchScalarGridSpec(num_scalar_...  7.95 us
  transfers between devices with their start and end apart: 20, of which 9 were waited for; matrix products, arithmetic and copies ran while one was open for 0% of the time, Pallas kernels for 27%

profile of v5, /device:TPU:0, one launch (start us, length us, event | category | flops | bytes accessed | tf_op | source)
XLA Modules:
  0.0 160.6 jit_solution(3361032355212722183)
XLA Ops:
  0.7 2.8 %copy-done = bf16[4096,768]{1,0:T(8,128)(2,1)S(1)} copy-done((bf16[4096,768]{1,0:T(8,128)(2,1)S(1)}, bf16[4096,768]{1,0:T(8,128)(2,1)}, u32[]{:S(2)}) %copy-start) | copy-done | bytes 6291480
  3.5 4.8 %shard_map.118 = bf16[2,512,1024]{2,1,0:T(8,128)(2,1)} custom-call(s32[2]{0:T(128)S(1)} %pad_add_fusion.sel_ref, bf16[512,768]{1,0:T(8,128)(2,1)} %refs_5_.3, bf16[4096,768]{1,0:T(8,128)(2,1)S(1)} %copy-done), custom_call_target="tpu_custom_call" | custom-call | flops 805306368 | bytes 3145728 | tf_op jit(solution)/shard_map/pallas_call | solution.py:140
  8.3 1.7 %collective-permute-start.2 = (bf16[512,768]{1,0:T(8,128)(2,1)}, bf16[512,768]{1,0:T(8,128)(2,1)S(1)}, u32[]{:S(2)}, u32[]{:S(2)}) collective-permute-start(bf16[512,768]{1,0:T(8,128)(2,1)} %refs_5_.3), channel_id=1, source_target_pairs={{0,64},{4,68},{8,72},{12,76},{16,80},{20,84},{24,88},{28,92},{32,9... | collective-permute-start | bytes 2359304 | tf_op jit(solution)/shard_map/ppermute | solution.py:461
  10.0 0.9 shard_map.119
  11.7 7.9 %all-to-all-start = ((f32[16,64,128]{2,1,0:T(8,128)}), f32[16,64,128]{2,1,0:T(8,128)S(1)}, u32[]{:S(2)}, u32[]{:S(2)}) async-start(f32[16,64,128]{2,1,0:T(8,128)} %bitcast.17), calls=%async_computation | async-start | bytes 1048576 | tf_op jit(solution)/shard_map/all_to_all | solution.py:464
  19.6 2.8 %copy-done.1 = bf16[4096,768]{1,0:T(8,128)(2,1)S(1)} copy-done((bf16[4096,768]{1,0:T(8,128)(2,1)S(1)}, bf16[4096,768]{1,0:T(8,128)(2,1)}, u32[]{:S(2)}) %copy-start.1) | copy-done | bytes 6291480
  22.4 2.6 %shard_map.120 = bf16[1,512,1024]{2,1,0:T(8,128)(2,1)S(1)} custom-call(s32[1]{0:T(128)} %bitcast.4.sel_ref, bf16[512,768]{1,0:T(8,128)(2,1)} %refs_5_.3, bf16[4096,768]{1,0:T(8,128)(2,1)S(1)} %copy-done.1, bf16[2,512,1024]{2,1,0:T(8,128)(2,1)} %collective-permute-done.r_ref), custom_call_target="tpu_custom_call" | custom-call | flops 805306368 | bytes 3145728 | tf_op jit(solution)/shard_map/pallas_call | solution.py:140
  25.0 1.0 copy-done.26
  25.9 5.5 %all-to-all-done.refs_1_ = f32[16,64,128]{2,1,0:T(8,128)S(1)} async-done(((f32[16,64,128]{2,1,0:T(8,128)}), f32[16,64,128]{2,1,0:T(8,128)S(1)}, u32[]{:S(2)}, u32[]{:S(2)}) %all-to-all-start) | async-done | bytes 524320 | tf_op jit(solution)/shard_map/all_to_all | solution.py:464
  32.0 3.4 %collective-permute-done.1.refs_2_ = f32[64,128]{1,0:T(8,128)S(1)} collective-permute-done((f32[64,128]{1,0:T(8,128)S(1)}, f32[64,128]{1,0:T(8,128)S(1)}, u32[]{:S(2)}, u32[]{:S(2)}) %collective-permute-start.1) | collective-permute-done | bytes 32800 | tf_op jit(solution)/shard_map/ppermute | solution.py:461
  35.5 3.2 %collective-permute-start.3 = (bf16[512,1024]{1,0:T(8,128)(2,1)}, bf16[512,1024]{1,0:T(8,128)(2,1)}, u32[]{:S(2)}, u32[]{:S(2)}) collective-permute-start(bf16[512,1024]{1,0:T(8,128)(2,1)} %bitcast.19), channel_id=1, source_target_pairs={{0,2},{1,3},{2,0},{3,1},{4,6},{5,7},{6,4},{7,5},{8,10},{9,11},{10,... | collective-permute-start | bytes 3145736 | tf_op jit(solution)/shard_map/ppermute | solution.py:458
  39.3 3.5 %all-to-all-start.1 = ((bf16[16,64,128]{2,1,0:T(8,128)(2,1)}), bf16[16,64,128]{2,1,0:T(8,128)(2,1)S(1)}, u32[]{:S(2)}, u32[]{:S(2)}) async-start(bf16[16,64,128]{2,1,0:T(8,128)(2,1)} %copy-done.28), calls=%async_computation.1 | async-start | bytes 524288 | tf_op jit(solution)/shard_map/all_to_all | solution.py:464
  42.9 3.0 %shard_map.122 = f32[1,512,1024]{2,1,0:T(8,128)S(1)} custom-call(s32[1]{0:T(128)} %bitcast.9.sel_ref, bf16[512,768]{1,0:T(8,128)(2,1)} %refs_5_.3, bf16[4096,768]{1,0:T(8,128)(2,1)} %refs_9_.1, bf16[2,512,1024]{2,1,0:T(8,128)(2,1)} %collective-permute-done.r_ref), custom_call_target="tpu_custom_call" | custom-call | flops 805306368 | bytes 3145728 | tf_op jit(solution)/shard_map/pallas_call | solution.py:140
  46.0 1.3 copy-done.8
  47.3 4.0 %all-to-all-done.1 = bf16[16,64,128]{2,1,0:T(8,128)(2,1)S(1)} async-done(((bf16[16,64,128]{2,1,0:T(8,128)(2,1)}), bf16[16,64,128]{2,1,0:T(8,128)(2,1)S(1)}, u32[]{:S(2)}, u32[]{:S(2)}) %all-to-all-start.1) | async-done | bytes 262176 | tf_op jit(solution)/shard_map/all_to_all | solution.py:464
  51.4 1.4 copy-done.11
  52.7 4.6 %shard_map.123 = (bf16[512,512]{1,0:T(8,128)(2,1)}, bf16[512,512]{1,0:T(8,128)(2,1)}, f32[512,1024]{1,0:T(8,128)S(1)}) custom-call(s32[1]{0:T(128)} %bitcast.1.refs_0_, bf16[512,1024]{1,0:T(8,128)(2,1)S(1)} %copy-done.11, bf16[512,1024]{1,0:T(8,128)(2,1)S(1)} %copy-done.2, bf16[512,1024]{1,0:T(8,128)(2,1)S(1)} %copy-done.5, ...), custom_call_target="tpu_custom_call" | custom-call | flops 1073741824 | bytes 7340032 | tf_op jit(solution)/shard_map/pallas_call | solution.py:216
  57.3 0.9 collective-permute-start.11
  58.2 3.2 %collective-permute-start.6 = (bf16[512,512]{1,0:T(8,128)(2,1)}, bf16[512,512]{1,0:T(8,128)(2,1)}, u32[]{:S(2)}, u32[]{:S(2)}) collective-permute-start(bf16[512,512]{1,0:T(8,128)(2,1)} %get-tuple-element.35.refs_1_), channel_id=1, source_target_pairs={{0,2},{1,3},{2,0},{3,1},{4,6},{5,7},{6,4},{7,5},{8,10},{9,11},{10,... | collective-permute-start | bytes 1572872 | tf_op jit(solution)/shard_map/ppermute | solution.py:458
  61.4 0.9 collective-permute-done.3.far_ref
  62.3 4.2 %shard_map.124 = (bf16[512,1024]{1,0:T(8,128)(2,1)}, bf16[512,1024]{1,0:T(8,128)(2,1)S(1)}, bf16[512,1024]{1,0:T(8,128)(2,1)S(1)}, f32[8,128,128]{2,1,0:T(8,128)S(1)}) custom-call(bf16[512,1024]{1,0:T(8,128)(2,1)S(1)} %copy-done.11, bf16[512,1024]{1,0:T(8,128)(2,1)S(1)} %copy-done.10, f32[1,1024]{1,0:T(1,128)S(1)} %bitcast.23, ...), custom_call_target="tpu_custom_call" | custom-call | flops 134217728 | bytes 10485760 | tf_op jit(solution)/shard_map/pallas_call | solution.py:255
  67.3 1.0 copy-done.32
  68.3 1.0 copy-done.34
  69.2 4.3 %collective-permute-done.13.refs_2_ = bf16[512,512]{1,0:T(8,128)(2,1)} collective-permute-done((bf16[512,512]{1,0:T(8,128)(2,1)}, bf16[512,512]{1,0:T(8,128)(2,1)}, u32[]{:S(2)}, u32[]{:S(2)}) %collective-permute-start.13) | collective-permute-done | bytes 524320 | tf_op jit(solution)/shard_map/ppermute | solution.py:461
  74.0 4.0 %all-to-all-start.2 = ((f32[16,64,128]{2,1,0:T(8,128)}), f32[16,64,128]{2,1,0:T(8,128)S(1)}, u32[]{:S(2)}, u32[]{:S(2)}) async-start(f32[16,64,128]{2,1,0:T(8,128)} %bitcast.18), calls=%async_computation.2 | async-start | bytes 1048576 | tf_op jit(solution)/shard_map/all_to_all | solution.py:464
  78.1 4.6 %collective-permute-done.11.refs_2_ = bf16[512,512]{1,0:T(8,128)(2,1)} collective-permute-done((bf16[512,512]{1,0:T(8,128)(2,1)}, bf16[512,512]{1,0:T(8,128)(2,1)}, u32[]{:S(2)}, u32[]{:S(2)}) %collective-permute-start.11) | collective-permute-done | bytes 524320 | tf_op jit(solution)/shard_map/ppermute | solution.py:513
  83.2 6.6 %all-to-all-done.2.refs_1_ = f32[16,64,128]{2,1,0:T(8,128)S(1)} async-done(((f32[16,64,128]{2,1,0:T(8,128)}), f32[16,64,128]{2,1,0:T(8,128)S(1)}, u32[]{:S(2)}, u32[]{:S(2)}) %all-to-all-start.2) | async-done | bytes 524320 | tf_op jit(solution)/shard_map/all_to_all | solution.py:464
  89.8 2.5 %collective-permute-start.10 = (f32[64,128]{1,0:T(8,128)S(1)}, f32[64,128]{1,0:T(8,128)S(1)}, u32[]{:S(2)}, u32[]{:S(2)}) collective-permute-start(f32[64,128]{1,0:T(8,128)S(1)} %reduce_sum.37), channel_id=1, source_target_pairs={{0,64},{4,68},{8,72},{12,76},{16,80},{20,84},{24,88},{28,92},{32,9... | collective-permute-start | bytes 98312 | tf_op jit(solution)/shard_map/ppermute | solution.py:461
  92.3 1.2 copy-done.25
  93.6 4.5 %shard_map.125.refs_7_ = bf16[16,144,768]{2,1,0:T(8,128)(2,1)} custom-call(s32[1]{0:T(128)} %bitcast.15.refs_0_, bf16[512,512]{1,0:T(8,128)(2,1)} %get-tuple-element.35.refs_1_, bf16[512,512]{1,0:T(8,128)(2,1)} %collective-permute-done.13.refs_2_, bf16[512,512]{1,0:T(8,128)(2,1)S(1)} %collective-permute-done.4.refs_3_, ...), custom_call_target="tpu_custom_call" | custom-call | flops 1610612736 | bytes 1572864 | tf_op jit(solution)/shard_map/pallas_call | solution.py:426
  98.0 4.6 %shard_map.126.refs_3_ = bf16[16,144,768]{2,1,0:T(8,128)(2,1)} custom-call(s32[1]{0:T(128)} %bitcast.15.refs_0_, bf16[512,512]{1,0:T(8,128)(2,1)} %collective-permute-done.6.refs_1_.refs_5_, bf16[512,512]{1,0:T(8,128)(2,1)} %collective-permute-done.11.refs_2_, ...), custom_call_target="tpu_custom_call", output_to_operand_aliasing={{}: (7, {})} | custom-call | flops 1610612736 | bytes 1572864 | tf_op jit(solution)/shard_map/pallas_call | solution.py:426
  102.7 0.8 shard_map.127.refs_6_
  103.5 3.8 %all-to-all-start.3 = ((bf16[16,144,768]{2,1,0:T(8,128)(2,1)}), bf16[16,144,768]{2,1,0:T(8,128)(2,1)S(1)}, u32[]{:S(2)}, u32[]{:S(2)}) async-start(bf16[16,144,768]{2,1,0:T(8,128)(2,1)} %shard_map.127.refs_6_), calls=%async_computation.3 | async-start | bytes 7077888 | tf_op jit(solution)/shard_map/all_to_all | solution.py:464
  107.5 13.8 %collective-permute-done.7.refs_6_ = bf16[512,512]{1,0:T(8,128)(2,1)} collective-permute-done((bf16[512,512]{1,0:T(8,128)(2,1)}, bf16[512,512]{1,0:T(8,128)(2,1)}, u32[]{:S(2)}, u32[]{:S(2)}) %collective-permute-start.7) | collective-permute-done | bytes 524320 | tf_op jit(solution)/shard_map/ppermute | solution.py:458
  121.4 1.2 copy-done.3
  122.6 1.2 copy-done.6
  123.8 1.2 copy-done.12
  125.1 0.9 copy-done.30
  126.0 1.2 copy-done.33
  127.2 1.2 copy-done.35
  128.5 9.1 %shard_map.128 = (bf16[512,1024]{1,0:T(8,128)(2,1)}, f32[512,1024]{1,0:T(8,128)S(1)}, f32[512,1024]{1,0:T(8,128)S(1)}) custom-call(bf16[512,1024]{1,0:T(8,128)(2,1)S(1)} %copy-done.12, bf16[512,1024]{1,0:T(8,128)(2,1)S(1)} %copy-done.3, bf16[512,1024]{1,0:T(8,128)(2,1)S(1)} %copy-done.6, bf16[512,1024]{1,0:T(8,128)(2,1)S(1)} %copy-done.33, ...), custom_call_target="tpu_custom_call" | custom-call | flops 2684354560 | bytes 10485760 | tf_op jit(solution)/shard_map/pallas_call | solution.py:303
  137.5 1.3 copy-done.15
  138.9 1.3 copy-done.17
  140.2 1.2 copy-done.27
  141.4 8.0 %shard_map.129 = bf16[512,768]{1,0:T(8,128)(2,1)} custom-call(s32[16]{0:T(128)S(1)} %stack.46.refs_0_, bf16[512,512]{1,0:T(8,128)(2,1)} %get-tuple-element.35.refs_1_, bf16[512,512]{1,0:T(8,128)(2,1)} %get-tuple-element.31.refs_2_, bf16[512,512]{1,0:T(8,128)(2,1)S(1)} %copy-done.21, bf16[512,512]{1,0:T(8,128)(2,1)} %collective-permute-done.5.refs_4_, ...), custom_call_target="tpu_custom_call" | custom-call | flops 3221225472 | bytes 6291456 | tf_op jit(solution)/shard_map/pallas_call | solution.py:378
  149.4 4.2 %all-to-all-done.3.refs_4_ = bf16[16,144,768]{2,1,0:T(8,128)(2,1)S(1)} async-done(((bf16[16,144,768]{2,1,0:T(8,128)(2,1)}), bf16[16,144,768]{2,1,0:T(8,128)(2,1)S(1)}, u32[]{:S(2)}, u32[]{:S(2)}) %all-to-all-start.3) | async-done | bytes 3538976 | tf_op jit(solution)/shard_map/all_to_all | solution.py:464
  155.8 1.6 copy-done.18
  157.4 2.3 %shard_map.130 = (bf16[512,1024]{1,0:T(8,128)(2,1)}, bf16[512,1024]{1,0:T(8,128)(2,1)}) custom-call(bf16[512,1024]{1,0:T(8,128)(2,1)S(1)} %copy-done.4, bf16[512,1024]{1,0:T(8,128)(2,1)S(1)} %copy-done.7, f32[512,1024]{1,0:T(8,128)S(1)} %copy-done.16, f32[512,1024]{1,0:T(8,128)S(1)} %copy-done.18, bf16[16,144,768]{2,1,0:T(8,128)(2,1)S(1)} %all-to-all-done.3.refs_4_), custom_call_target="tpu_custom_call" | custom-call | flops 268435456 | bytes 8388608 | tf_op jit(solution)/shard_map/pallas_call | solution.py:346
  (84 shorter events, 7.4 us)
Async XLA Ops:
  0.7 2.8 %copy-start = (bf16[4096,768]{1,0:T(8,128)(2,1)S(1)}, bf16[4096,768]{1,0:T(8,128)(2,1)}, u32[]{:S(2)}) copy-start(bf16[4096,768]{1,0:T(8,128)(2,1)} %refs_9_.1) | copy-start | bytes 18874372
  3.5 6.5 %copy-start.2 = (bf16[512,1024]{1,0:T(8,128)(2,1)S(1)}, bf16[512,1024]{1,0:T(8,128)(2,1)}, u32[]{:S(2)}) copy-start(bf16[512,1024]{1,0:T(8,128)(2,1)} %refs_0_.3) | copy-start | bytes 3145732
  3.5 6.5 %copy-start.5 = (bf16[512,1024]{1,0:T(8,128)(2,1)S(1)}, bf16[512,1024]{1,0:T(8,128)(2,1)}, u32[]{:S(2)}) copy-start(bf16[512,1024]{1,0:T(8,128)(2,1)} %refs_1_.4) | copy-start | bytes 3145732
  8.3 11.2 %collective-permute-start = (bf16[2,512,1024]{2,1,0:T(8,128)(2,1)}, bf16[2,512,1024]{2,1,0:T(8,128)(2,1)}, u32[]{:S(2)}, u32[]{:S(2)}) collective-permute-start(bf16[2,512,1024]{2,1,0:T(8,128)(2,1)} %shard_map.118), channel_id=1, source_target_pairs={{0,1},{1,0},{2,3},{3,2},{4,5},{5,4},{6,7},{7,6},{8,9},{9,8},{10,11... | collective-permute-start | bytes 6291464 | tf_op jit(solution)/shard_map/ppermute | solution.py:455
  8.3 23.7 %collective-permute-start.2 = (bf16[512,768]{1,0:T(8,128)(2,1)}, bf16[512,768]{1,0:T(8,128)(2,1)S(1)}, u32[]{:S(2)}, u32[]{:S(2)}) collective-permute-start(bf16[512,768]{1,0:T(8,128)(2,1)} %refs_5_.3), channel_id=1, source_target_pairs={{0,64},{4,68},{8,72},{12,76},{16,80},{20,84},{24,88},{28,92},{32,9... | collective-permute-start | bytes 2359304 | tf_op jit(solution)/shard_map/ppermute | solution.py:461
  11.7 19.8 %all-to-all-start = ((f32[16,64,128]{2,1,0:T(8,128)}), f32[16,64,128]{2,1,0:T(8,128)S(1)}, u32[]{:S(2)}, u32[]{:S(2)}) async-start(f32[16,64,128]{2,1,0:T(8,128)} %bitcast.17), calls=%async_computation | async-start | bytes 1048576 | tf_op jit(solution)/shard_map/all_to_all | solution.py:464
  19.6 2.8 %copy-start.1 = (bf16[4096,768]{1,0:T(8,128)(2,1)S(1)}, bf16[4096,768]{1,0:T(8,128)(2,1)}, u32[]{:S(2)}) copy-start(bf16[4096,768]{1,0:T(8,128)(2,1)} %refs_9_.1) | copy-start | bytes 18874372
  31.5 4.0 %collective-permute-start.1 = (f32[64,128]{1,0:T(8,128)S(1)}, f32[64,128]{1,0:T(8,128)S(1)}, u32[]{:S(2)}, u32[]{:S(2)}) collective-permute-start(f32[64,128]{1,0:T(8,128)S(1)} %reduce_sum.36), channel_id=1, source_target_pairs={{0,64},{4,68},{8,72},{12,76},{16,80},{20,84},{24,88},{28,92},{32,9... | collective-permute-start | bytes 98312 | tf_op jit(solution)/shard_map/ppermute | solution.py:461
  32.0 10.9 %copy-start.13 = (bf16[512,768]{1,0:T(8,128)(2,1)}, bf16[512,768]{1,0:T(8,128)(2,1)S(1)}, u32[]{:S(2)}) copy-start(bf16[512,768]{1,0:T(8,128)(2,1)S(1)} %collective-permute-done.2.refs_6_) | copy-start | bytes 2359300
  35.5 26.8 %collective-permute-start.3 = (bf16[512,1024]{1,0:T(8,128)(2,1)}, bf16[512,1024]{1,0:T(8,128)(2,1)}, u32[]{:S(2)}, u32[]{:S(2)}) collective-permute-start(bf16[512,1024]{1,0:T(8,128)(2,1)} %bitcast.19), channel_id=1, source_target_pairs={{0,2},{1,3},{2,0},{3,1},{4,6},{5,7},{6,4},{7,5},{8,10},{9,11},{10,... | collective-permute-start | bytes 3145736 | tf_op jit(solution)/shard_map/ppermute | solution.py:458
  39.3 12.0 %all-to-all-start.1 = ((bf16[16,64,128]{2,1,0:T(8,128)(2,1)}), bf16[16,64,128]{2,1,0:T(8,128)(2,1)S(1)}, u32[]{:S(2)}, u32[]{:S(2)}) async-start(bf16[16,64,128]{2,1,0:T(8,128)(2,1)} %copy-done.28), calls=%async_computation.1 | async-start | bytes 524288 | tf_op jit(solution)/shard_map/all_to_all | solution.py:464
  42.9 8.4 %copy-start.10 = (bf16[512,1024]{1,0:T(8,128)(2,1)S(1)}, bf16[512,1024]{1,0:T(8,128)(2,1)}, u32[]{:S(2)}) copy-start(bf16[512,1024]{1,0:T(8,128)(2,1)} %g_ref.1) | copy-start | bytes 3145732
  42.9 8.4 %copy-start.31 = (f32[1024]{0:T(1024)S(1)}, f32[1024]{0:T(1024)}, u32[]{:S(2)}) copy-start(f32[1024]{0:T(1024)} %param.11) | copy-start | bytes 12292
  46.0 1.3 copy-start.8
  51.3 15.2 %copy-start.29 = (bf16[16,64,128]{2,1,0:T(8,128)(2,1)}, bf16[16,64,128]{2,1,0:T(8,128)(2,1)S(1)}, u32[]{:S(2)}) copy-start(bf16[16,64,128]{2,1,0:T(8,128)(2,1)S(1)} %all-to-all-done.1) | copy-start | bytes 786436
  51.3 11.0 %copy-start.9 = (f32[1,512,1024]{2,1,0:T(8,128)S(1)}, f32[1,512,1024]{2,1,0:T(8,128)}, u32[]{:S(2)}) copy-start(f32[1,512,1024]{2,1,0:T(8,128)} %copy-done.8) | copy-start | bytes 6291460
  51.3 1.4 copy-start.11
  57.3 16.2 %collective-permute-start.13 = (bf16[512,512]{1,0:T(8,128)(2,1)}, bf16[512,512]{1,0:T(8,128)(2,1)}, u32[]{:S(2)}, u32[]{:S(2)}) collective-permute-start(bf16[512,512]{1,0:T(8,128)(2,1)} %get-tuple-element.31.refs_2_), channel_id=1, source_target_pairs={{0,64},{4,68},{8,72},{12,76},{16,80},{20,84},{24,88},{28,92},{32,9... | collective-permute-start | bytes 1572872 | tf_op jit(solution)/shard_map/ppermute | solution.py:461
  57.3 25.4 %collective-permute-start.11 = (bf16[512,512]{1,0:T(8,128)(2,1)}, bf16[512,512]{1,0:T(8,128)(2,1)}, u32[]{:S(2)}, u32[]{:S(2)}) collective-permute-start(bf16[512,512]{1,0:T(8,128)(2,1)} %get-tuple-element.31.refs_2_), channel_id=1, source_target_pairs={{0,66},{1,67},{2,64},{3,65},{4,70},{5,71},{6,68},{7,69},{8,74},{9,... | collective-permute-start | bytes 1572872 | tf_op jit(solution)/shard_map/ppermute | solution.py:513
  58.2 24.4 %collective-permute-start.6 = (bf16[512,512]{1,0:T(8,128)(2,1)}, bf16[512,512]{1,0:T(8,128)(2,1)}, u32[]{:S(2)}, u32[]{:S(2)}) collective-permute-start(bf16[512,512]{1,0:T(8,128)(2,1)} %get-tuple-element.35.refs_1_), channel_id=1, source_target_pairs={{0,2},{1,3},{2,0},{3,1},{4,6},{5,7},{6,4},{7,5},{8,10},{9,11},{10,... | collective-permute-start | bytes 1572872 | tf_op jit(solution)/shard_map/ppermute | solution.py:458
  62.3 30.0 %copy-start.14 = (bf16[512,768]{1,0:T(8,128)(2,1)S(1)}, bf16[512,768]{1,0:T(8,128)(2,1)}, u32[]{:S(2)}) copy-start(bf16[512,768]{1,0:T(8,128)(2,1)} %copy-done.13) | copy-start | bytes 2359300
  73.5 18.8 %collective-permute-start.14 = (bf16[512,512]{1,0:T(8,128)(2,1)}, bf16[512,512]{1,0:T(8,128)(2,1)S(1)}, u32[]{:S(2)}, u32[]{:S(2)}) collective-permute-start(bf16[512,512]{1,0:T(8,128)(2,1)} %collective-permute-done.13.refs_2_), channel_id=1, source_target_pairs={{0,1},{1,0},{2,3},{3,2},{4,5},{5,4},{6,7},{7,6},{8,9},{9,8},{10,11... | collective-permute-start | bytes 1572872 | tf_op jit(solution)/shard_map/ppermute | solution.py:455
  73.5 18.8 %collective-permute-start.4 = (bf16[512,512]{1,0:T(8,128)(2,1)}, bf16[512,512]{1,0:T(8,128)(2,1)S(1)}, u32[]{:S(2)}, u32[]{:S(2)}) collective-permute-start(bf16[512,512]{1,0:T(8,128)(2,1)} %get-tuple-element.35.refs_1_), channel_id=1, source_target_pairs={{0,1},{1,0},{2,3},{3,2},{4,5},{5,4},{6,7},{7,6},{8,9},{9,8},{10,11... | collective-permute-start | bytes 1572872 | tf_op jit(solution)/shard_map/ppermute | solution.py:455
  74.0 15.7 %all-to-all-start.2 = ((f32[16,64,128]{2,1,0:T(8,128)}), f32[16,64,128]{2,1,0:T(8,128)S(1)}, u32[]{:S(2)}, u32[]{:S(2)}) async-start(f32[16,64,128]{2,1,0:T(8,128)} %bitcast.18), calls=%async_computation.2 | async-start | bytes 1048576 | tf_op jit(solution)/shard_map/all_to_all | solution.py:464
  82.7 15.4 %collective-permute-start.12 = (bf16[512,512]{1,0:T(8,128)(2,1)}, bf16[512,512]{1,0:T(8,128)(2,1)S(1)}, u32[]{:S(2)}, u32[]{:S(2)}) collective-permute-start(bf16[512,512]{1,0:T(8,128)(2,1)} %collective-permute-done.11.refs_2_), channel_id=1, source_target_pairs={{0,1},{1,0},{2,3},{3,2},{4,5},{5,4},{6,7},{7,6},{8,9},{9,8},{10,11... | collective-permute-start | bytes 1572872 | tf_op jit(solution)/shard_map/ppermute | solution.py:455
  82.7 15.4 %collective-permute-start.8 = (bf16[512,512]{1,0:T(8,128)(2,1)}, bf16[512,512]{1,0:T(8,128)(2,1)S(1)}, u32[]{:S(2)}, u32[]{:S(2)}) collective-permute-start(bf16[512,512]{1,0:T(8,128)(2,1)} %collective-permute-done.6.refs_1_.refs_5_), channel_id=1, source_target_pairs={{0,1},{1,0},{2,3},{3,2},{4,5},{5,4},{6,7},{7,6},{8,9},{9,8},{10,11... | collective-permute-start | bytes 1572872 | tf_op jit(solution)/shard_map/ppermute | solution.py:455
  89.8 12.9 %collective-permute-start.10 = (f32[64,128]{1,0:T(8,128)S(1)}, f32[64,128]{1,0:T(8,128)S(1)}, u32[]{:S(2)}, u32[]{:S(2)}) collective-permute-start(f32[64,128]{1,0:T(8,128)S(1)} %reduce_sum.37), channel_id=1, source_target_pairs={{0,64},{4,68},{8,72},{12,76},{16,80},{20,84},{24,88},{28,92},{32,9... | collective-permute-start | bytes 98312 | tf_op jit(solution)/shard_map/ppermute | solution.py:461
  92.3 5.7 %copy-start.20 = (bf16[512,512]{1,0:T(8,128)(2,1)}, bf16[512,512]{1,0:T(8,128)(2,1)S(1)}, u32[]{:S(2)}) copy-start(bf16[512,512]{1,0:T(8,128)(2,1)S(1)} %collective-permute-done.4.refs_3_) | copy-start | bytes 1572868
  92.3 1.2 copy-start.25
  98.0 4.6 %copy-start.22 = (bf16[512,512]{1,0:T(8,128)(2,1)}, bf16[512,512]{1,0:T(8,128)(2,1)S(1)}, u32[]{:S(2)}) copy-start(bf16[512,512]{1,0:T(8,128)(2,1)S(1)} %collective-permute-done.8.refs_3_.refs_7_) | copy-start | bytes 1572868
  103.5 50.0 %all-to-all-start.3 = ((bf16[16,144,768]{2,1,0:T(8,128)(2,1)}), bf16[16,144,768]{2,1,0:T(8,128)(2,1)S(1)}, u32[]{:S(2)}, u32[]{:S(2)}) async-start(bf16[16,144,768]{2,1,0:T(8,128)(2,1)} %shard_map.127.refs_6_), calls=%async_computation.3 | async-start | bytes 7077888 | tf_op jit(solution)/shard_map/all_to_all | solution.py:464
  107.3 14.0 %collective-permute-start.7 = (bf16[512,512]{1,0:T(8,128)(2,1)}, bf16[512,512]{1,0:T(8,128)(2,1)}, u32[]{:S(2)}, u32[]{:S(2)}) collective-permute-start(bf16[512,512]{1,0:T(8,128)(2,1)} %get-tuple-element.31.refs_2_), channel_id=1, source_target_pairs={{0,2},{1,3},{2,0},{3,1},{4,6},{5,7},{6,4},{7,5},{8,10},{9,11},{10,... | collective-permute-start | bytes 1572872 | tf_op jit(solution)/shard_map/ppermute | solution.py:458
  107.4 32.8 %collective-permute-start.5 = (bf16[512,512]{1,0:T(8,128)(2,1)}, bf16[512,512]{1,0:T(8,128)(2,1)}, u32[]{:S(2)}, u32[]{:S(2)}) collective-permute-start(bf16[512,512]{1,0:T(8,128)(2,1)} %get-tuple-element.31.refs_2_), channel_id=1, source_target_pairs={{0,1},{1,0},{2,3},{3,2},{4,5},{5,4},{6,7},{7,6},{8,9},{9,8},{10,11... | collective-permute-start | bytes 1572872 | tf_op jit(solution)/shard_map/ppermute | solution.py:455
  121.3 18.9 %collective-permute-start.9 = (bf16[512,512]{1,0:T(8,128)(2,1)}, bf16[512,512]{1,0:T(8,128)(2,1)}, u32[]{:S(2)}, u32[]{:S(2)}) collective-permute-start(bf16[512,512]{1,0:T(8,128)(2,1)} %collective-permute-done.7.refs_6_), channel_id=1, source_target_pairs={{0,1},{1,0},{2,3},{3,2},{4,5},{5,4},{6,7},{7,6},{8,9},{9,8},{10,11... | collective-permute-start | bytes 1572872 | tf_op jit(solution)/shard_map/ppermute | solution.py:455
  121.4 1.2 copy-start.3
  123.8 1.2 copy-start.12
  126.0 1.2 copy-start.33
  127.2 1.2 copy-start.35
  128.5 11.8 %copy-start.21 = (bf16[512,512]{1,0:T(8,128)(2,1)S(1)}, bf16[512,512]{1,0:T(8,128)(2,1)}, u32[]{:S(2)}) copy-start(bf16[512,512]{1,0:T(8,128)(2,1)} %copy-done.20) | copy-start | bytes 1572868
  128.5 11.8 %copy-start.23 = (bf16[512,512]{1,0:T(8,128)(2,1)S(1)}, bf16[512,512]{1,0:T(8,128)(2,1)}, u32[]{:S(2)}) copy-start(bf16[512,512]{1,0:T(8,128)(2,1)} %copy-done.22) | copy-start | bytes 1572868
  137.5 1.3 copy-start.15
  138.9 1.3 copy-start.17
  140.2 1.2 copy-start.27
  153.6 1.2 copy-start.4
  153.6 1.5 copy-start.7
  153.6 2.2 %copy-start.16 = (f32[512,1024]{1,0:T(8,128)S(1)}, f32[512,1024]{1,0:T(8,128)}, u32[]{:S(2)}) copy-start(f32[512,1024]{1,0:T(8,128)} %copy-done.15) | copy-start | bytes 6291460
  154.0 5.7 %collective-permute-start.15 = (f32[64,768]{1,0:T(8,128)S(1)}, f32[64,768]{1,0:T(8,128)S(1)}, u32[]{:S(2)}, u32[]{:S(2)}) collective-permute-start(f32[64,768]{1,0:T(8,128)S(1)} %get-tuple-element.49), channel_id=1, source_target_pairs={{0,64},{4,68},{8,72},{12,76},{16,80},{20,84},{24,88},{28,92},{32,9... | collective-permute-start | bytes 589832 | tf_op jit(solution)/shard_map/ppermute | solution.py:461
  155.8 1.6 copy-start.18
  (8 other events, 7.4 us)

commit v6 on v5

--- a/solution.py
+++ b/solution.py
@@ -158,9 +158,13 @@
 
 
 def masked(scores, first):
-    rows = lax.broadcasted_iota(jnp.int32, scores.shape, 0) + first
-    cols = lax.broadcasted_iota(jnp.int32, scores.shape, 1)
-    return jnp.where(cols <= rows, scores, 0.0).astype(BF16)
+    size = scores.shape[0]
+    rows = lax.broadcasted_iota(jnp.int32, (size, size), 0)
+    cols = lax.broadcasted_iota(jnp.int32, (size, size), 1)
+    last = jnp.where(cols <= rows, scores[:, first:], 0.0).astype(BF16)
+    if not first:
+        return last
+    return jnp.concatenate([scores[:, :first].astype(BF16), last], axis=1)
 
 
 def sigmoid(gate):

time: 162 us -> 162 us (level)
  no operation moved by 1% of the time
where the time goes in v6:
time: 162 us; the launch traced here: 161 us
  Pallas kernels  49.3 us (30%)
  waiting for transfers between devices  47.4 us (29%)
  starting transfers between devices  33 us (20%)
  local copies, waits for them, and re-layouts  28.5 us (18%)
    unnamed x72, local copies, waits for them, and re-layouts  28.4 us
    all_to_all x4, waiting for transfers between devices, exchange(): return lax.all_to_all(array, 'ctx', 0, 0, axis_index_groups=groups)  20.2 us
    all_to_all x4, starting transfers between devices, exchange(): return lax.all_to_all(array, 'ctx', 0, 0, axis_index_groups=groups)  19.2 us
    ppermute x3, waiting for transfers between devices, swap_hi(): return lax.ppermute(array, 'fsdp', hi_swap)  14.8 us
    pallas_call x3, Pallas kernels, head_term(): pl.pallas_call(head_term_kernel if received is None else head_sum_kernel,...  10.4 us
    pallas_call x2, Pallas kernels, weight_grad(): pl.pallas_call(kernel, grid_spec=pltpu.PrefetchScalarGridSpec(num_scalar_...  9.06 us
    pallas_call x1, Pallas kernels, head_grads(): pl.pallas_call(kernel, grid=(heads // step,), in_specs=in_specs, out_spec...  9.05 us
    pallas_call x1, Pallas kernels, mix(): pl.pallas_call(kernel, grid_spec=pltpu.PrefetchScalarGridSpec(num_scalar_...  7.96 us
  transfers between devices with their start and end apart: 20, of which 9 were waited for; matrix products, arithmetic and copies ran while one was open for 0% of the time, Pallas kernels for 27%

profile of v6, /device:TPU:0, one launch (start us, length us, event | category | flops | bytes accessed | tf_op | source)
XLA Modules:
  0.0 160.6 jit_solution(18105311323135933953)
XLA Ops:
  0.7 2.8 %copy-done = bf16[4096,768]{1,0:T(8,128)(2,1)S(1)} copy-done((bf16[4096,768]{1,0:T(8,128)(2,1)S(1)}, bf16[4096,768]{1,0:T(8,128)(2,1)}, u32[]{:S(2)}) %copy-start) | copy-done | bytes 6291480
  3.5 4.8 %shard_map.118 = bf16[2,512,1024]{2,1,0:T(8,128)(2,1)} custom-call(s32[2]{0:T(128)S(1)} %pad_add_fusion.sel_ref, bf16[512,768]{1,0:T(8,128)(2,1)} %refs_5_.3, bf16[4096,768]{1,0:T(8,128)(2,1)S(1)} %copy-done), custom_call_target="tpu_custom_call" | custom-call | flops 805306368 | bytes 3145728 | tf_op jit(solution)/shard_map/pallas_call | solution.py:140
  8.3 1.7 %collective-permute-start.2 = (bf16[512,768]{1,0:T(8,128)(2,1)}, bf16[512,768]{1,0:T(8,128)(2,1)S(1)}, u32[]{:S(2)}, u32[]{:S(2)}) collective-permute-start(bf16[512,768]{1,0:T(8,128)(2,1)} %refs_5_.3), channel_id=1, source_target_pairs={{0,64},{4,68},{8,72},{12,76},{16,80},{20,84},{24,88},{28,92},{32,9... | collective-permute-start | bytes 2359304 | tf_op jit(solution)/shard_map/ppermute | solution.py:465
  10.0 0.9 shard_map.119
  11.7 7.9 %all-to-all-start = ((f32[16,64,128]{2,1,0:T(8,128)}), f32[16,64,128]{2,1,0:T(8,128)S(1)}, u32[]{:S(2)}, u32[]{:S(2)}) async-start(f32[16,64,128]{2,1,0:T(8,128)} %bitcast.17), calls=%async_computation | async-start | bytes 1048576 | tf_op jit(solution)/shard_map/all_to_all | solution.py:468
  19.6 2.8 %copy-done.1 = bf16[4096,768]{1,0:T(8,128)(2,1)S(1)} copy-done((bf16[4096,768]{1,0:T(8,128)(2,1)S(1)}, bf16[4096,768]{1,0:T(8,128)(2,1)}, u32[]{:S(2)}) %copy-start.1) | copy-done | bytes 6291480
  22.4 2.6 %shard_map.120 = bf16[1,512,1024]{2,1,0:T(8,128)(2,1)S(1)} custom-call(s32[1]{0:T(128)} %bitcast.4.sel_ref, bf16[512,768]{1,0:T(8,128)(2,1)} %refs_5_.3, bf16[4096,768]{1,0:T(8,128)(2,1)S(1)} %copy-done.1, bf16[2,512,1024]{2,1,0:T(8,128)(2,1)} %collective-permute-done.r_ref), custom_call_target="tpu_custom_call" | custom-call | flops 805306368 | bytes 3145728 | tf_op jit(solution)/shard_map/pallas_call | solution.py:140
  25.0 1.0 copy-done.26
  25.9 5.5 %all-to-all-done.refs_1_ = f32[16,64,128]{2,1,0:T(8,128)S(1)} async-done(((f32[16,64,128]{2,1,0:T(8,128)}), f32[16,64,128]{2,1,0:T(8,128)S(1)}, u32[]{:S(2)}, u32[]{:S(2)}) %all-to-all-start) | async-done | bytes 524320 | tf_op jit(solution)/shard_map/all_to_all | solution.py:468
  32.0 3.4 %collective-permute-done.1.refs_2_ = f32[64,128]{1,0:T(8,128)S(1)} collective-permute-done((f32[64,128]{1,0:T(8,128)S(1)}, f32[64,128]{1,0:T(8,128)S(1)}, u32[]{:S(2)}, u32[]{:S(2)}) %collective-permute-start.1) | collective-permute-done | bytes 32800 | tf_op jit(solution)/shard_map/ppermute | solution.py:465
  35.5 3.2 %collective-permute-start.3 = (bf16[512,1024]{1,0:T(8,128)(2,1)}, bf16[512,1024]{1,0:T(8,128)(2,1)}, u32[]{:S(2)}, u32[]{:S(2)}) collective-permute-start(bf16[512,1024]{1,0:T(8,128)(2,1)} %bitcast.19), channel_id=1, source_target_pairs={{0,2},{1,3},{2,0},{3,1},{4,6},{5,7},{6,4},{7,5},{8,10},{9,11},{10,... | collective-permute-start | bytes 3145736 | tf_op jit(solution)/shard_map/ppermute | solution.py:462
  39.3 3.5 %all-to-all-start.1 = ((bf16[16,64,128]{2,1,0:T(8,128)(2,1)}), bf16[16,64,128]{2,1,0:T(8,128)(2,1)S(1)}, u32[]{:S(2)}, u32[]{:S(2)}) async-start(bf16[16,64,128]{2,1,0:T(8,128)(2,1)} %copy-done.28), calls=%async_computation.1 | async-start | bytes 524288 | tf_op jit(solution)/shard_map/all_to_all | solution.py:468
  42.9 3.0 %shard_map.122 = f32[1,512,1024]{2,1,0:T(8,128)S(1)} custom-call(s32[1]{0:T(128)} %bitcast.9.sel_ref, bf16[512,768]{1,0:T(8,128)(2,1)} %refs_5_.3, bf16[4096,768]{1,0:T(8,128)(2,1)} %refs_9_.1, bf16[2,512,1024]{2,1,0:T(8,128)(2,1)} %collective-permute-done.r_ref), custom_call_target="tpu_custom_call" | custom-call | flops 805306368 | bytes 3145728 | tf_op jit(solution)/shard_map/pallas_call | solution.py:140
  46.0 1.3 copy-done.8
  47.3 4.0 %all-to-all-done.1 = bf16[16,64,128]{2,1,0:T(8,128)(2,1)S(1)} async-done(((bf16[16,64,128]{2,1,0:T(8,128)(2,1)}), bf16[16,64,128]{2,1,0:T(8,128)(2,1)S(1)}, u32[]{:S(2)}, u32[]{:S(2)}) %all-to-all-start.1) | async-done | bytes 262176 | tf_op jit(solution)/shard_map/all_to_all | solution.py:468
  51.4 1.4 copy-done.11
  52.7 4.5 %shard_map.123 = (bf16[512,512]{1,0:T(8,128)(2,1)}, bf16[512,512]{1,0:T(8,128)(2,1)}, f32[512,1024]{1,0:T(8,128)S(1)}) custom-call(s32[1]{0:T(128)} %bitcast.1.refs_0_, bf16[512,1024]{1,0:T(8,128)(2,1)S(1)} %copy-done.11, bf16[512,1024]{1,0:T(8,128)(2,1)S(1)} %copy-done.2, bf16[512,1024]{1,0:T(8,128)(2,1)S(1)} %copy-done.5, ...), custom_call_target="tpu_custom_call" | custom-call | flops 1073741824 | bytes 7340032 | tf_op jit(solution)/shard_map/pallas_call | solution.py:220
  57.3 0.9 collective-permute-start.11
  58.2 3.1 %collective-permute-start.6 = (bf16[512,512]{1,0:T(8,128)(2,1)}, bf16[512,512]{1,0:T(8,128)(2,1)}, u32[]{:S(2)}, u32[]{:S(2)}) collective-permute-start(bf16[512,512]{1,0:T(8,128)(2,1)} %get-tuple-element.35.refs_1_), channel_id=1, source_target_pairs={{0,2},{1,3},{2,0},{3,1},{4,6},{5,7},{6,4},{7,5},{8,10},{9,11},{10,... | collective-permute-start | bytes 1572872 | tf_op jit(solution)/shard_map/ppermute | solution.py:462
  61.4 1.0 collective-permute-done.3.far_ref
  62.3 4.2 %shard_map.124 = (bf16[512,1024]{1,0:T(8,128)(2,1)}, bf16[512,1024]{1,0:T(8,128)(2,1)S(1)}, bf16[512,1024]{1,0:T(8,128)(2,1)S(1)}, f32[8,128,128]{2,1,0:T(8,128)S(1)}) custom-call(bf16[512,1024]{1,0:T(8,128)(2,1)S(1)} %copy-done.11, bf16[512,1024]{1,0:T(8,128)(2,1)S(1)} %copy-done.10, f32[1,1024]{1,0:T(1,128)S(1)} %bitcast.23, ...), custom_call_target="tpu_custom_call" | custom-call | flops 134217728 | bytes 10485760 | tf_op jit(solution)/shard_map/pallas_call | solution.py:259
  67.3 1.0 copy-done.32
  68.3 1.0 copy-done.34
  69.3 4.3 %collective-permute-done.13.refs_2_ = bf16[512,512]{1,0:T(8,128)(2,1)} collective-permute-done((bf16[512,512]{1,0:T(8,128)(2,1)}, bf16[512,512]{1,0:T(8,128)(2,1)}, u32[]{:S(2)}, u32[]{:S(2)}) %collective-permute-start.13) | collective-permute-done | bytes 524320 | tf_op jit(solution)/shard_map/ppermute | solution.py:465
  74.1 4.0 %all-to-all-start.2 = ((f32[16,64,128]{2,1,0:T(8,128)}), f32[16,64,128]{2,1,0:T(8,128)S(1)}, u32[]{:S(2)}, u32[]{:S(2)}) async-start(f32[16,64,128]{2,1,0:T(8,128)} %bitcast.18), calls=%async_computation.2 | async-start | bytes 1048576 | tf_op jit(solution)/shard_map/all_to_all | solution.py:468
  78.1 4.6 %collective-permute-done.11.refs_2_ = bf16[512,512]{1,0:T(8,128)(2,1)} collective-permute-done((bf16[512,512]{1,0:T(8,128)(2,1)}, bf16[512,512]{1,0:T(8,128)(2,1)}, u32[]{:S(2)}, u32[]{:S(2)}) %collective-permute-start.11) | collective-permute-done | bytes 524320 | tf_op jit(solution)/shard_map/ppermute | solution.py:517
  83.2 6.6 %all-to-all-done.2.refs_1_ = f32[16,64,128]{2,1,0:T(8,128)S(1)} async-done(((f32[16,64,128]{2,1,0:T(8,128)}), f32[16,64,128]{2,1,0:T(8,128)S(1)}, u32[]{:S(2)}, u32[]{:S(2)}) %all-to-all-start.2) | async-done | bytes 524320 | tf_op jit(solution)/shard_map/all_to_all | solution.py:468
  89.8 2.5 %collective-permute-start.10 = (f32[64,128]{1,0:T(8,128)S(1)}, f32[64,128]{1,0:T(8,128)S(1)}, u32[]{:S(2)}, u32[]{:S(2)}) collective-permute-start(f32[64,128]{1,0:T(8,128)S(1)} %reduce_sum.37), channel_id=1, source_target_pairs={{0,64},{4,68},{8,72},{12,76},{16,80},{20,84},{24,88},{28,92},{32,9... | collective-permute-start | bytes 98312 | tf_op jit(solution)/shard_map/ppermute | solution.py:465
  92.4 1.2 copy-done.25
  93.6 4.4 %shard_map.125.refs_7_ = bf16[16,144,768]{2,1,0:T(8,128)(2,1)} custom-call(s32[1]{0:T(128)} %bitcast.15.refs_0_, bf16[512,512]{1,0:T(8,128)(2,1)} %get-tuple-element.35.refs_1_, bf16[512,512]{1,0:T(8,128)(2,1)} %collective-permute-done.13.refs_2_, bf16[512,512]{1,0:T(8,128)(2,1)S(1)} %collective-permute-done.4.refs_3_, ...), custom_call_target="tpu_custom_call" | custom-call | flops 1610612736 | bytes 1572864 | tf_op jit(solution)/shard_map/pallas_call | solution.py:430
  98.1 4.6 %shard_map.126.refs_3_ = bf16[16,144,768]{2,1,0:T(8,128)(2,1)} custom-call(s32[1]{0:T(128)} %bitcast.15.refs_0_, bf16[512,512]{1,0:T(8,128)(2,1)} %collective-permute-done.6.refs_1_.refs_5_, bf16[512,512]{1,0:T(8,128)(2,1)} %collective-permute-done.11.refs_2_, ...), custom_call_target="tpu_custom_call", output_to_operand_aliasing={{}: (7, {})} | custom-call | flops 1610612736 | bytes 1572864 | tf_op jit(solution)/shard_map/pallas_call | solution.py:430
  102.7 0.8 shard_map.127.refs_6_
  103.5 3.8 %all-to-all-start.3 = ((bf16[16,144,768]{2,1,0:T(8,128)(2,1)}), bf16[16,144,768]{2,1,0:T(8,128)(2,1)S(1)}, u32[]{:S(2)}, u32[]{:S(2)}) async-start(bf16[16,144,768]{2,1,0:T(8,128)(2,1)} %shard_map.127.refs_6_), calls=%async_computation.3 | async-start | bytes 7077888 | tf_op jit(solution)/shard_map/all_to_all | solution.py:468
  107.5 13.8 %collective-permute-done.7.refs_6_ = bf16[512,512]{1,0:T(8,128)(2,1)} collective-permute-done((bf16[512,512]{1,0:T(8,128)(2,1)}, bf16[512,512]{1,0:T(8,128)(2,1)}, u32[]{:S(2)}, u32[]{:S(2)}) %collective-permute-start.7) | collective-permute-done | bytes 524320 | tf_op jit(solution)/shard_map/ppermute | solution.py:462
  121.4 1.2 copy-done.3
  122.6 1.2 copy-done.6
  123.9 1.2 copy-done.12
  125.1 0.9 copy-done.30
  126.0 1.2 copy-done.33
  127.3 1.2 copy-done.35
  128.5 9.0 %shard_map.128 = (bf16[512,1024]{1,0:T(8,128)(2,1)}, f32[512,1024]{1,0:T(8,128)S(1)}, f32[512,1024]{1,0:T(8,128)S(1)}) custom-call(bf16[512,1024]{1,0:T(8,128)(2,1)S(1)} %copy-done.12, bf16[512,1024]{1,0:T(8,128)(2,1)S(1)} %copy-done.3, bf16[512,1024]{1,0:T(8,128)(2,1)S(1)} %copy-done.6, bf16[512,1024]{1,0:T(8,128)(2,1)S(1)} %copy-done.33, ...), custom_call_target="tpu_custom_call" | custom-call | flops 2684354560 | bytes 10485760 | tf_op jit(solution)/shard_map/pallas_call | solution.py:307
  137.5 1.3 copy-done.15
  138.9 1.3 copy-done.17
  140.3 1.2 copy-done.27
  141.5 8.0 %shard_map.129 = bf16[512,768]{1,0:T(8,128)(2,1)} custom-call(s32[16]{0:T(128)S(1)} %stack.46.refs_0_, bf16[512,512]{1,0:T(8,128)(2,1)} %get-tuple-element.35.refs_1_, bf16[512,512]{1,0:T(8,128)(2,1)} %get-tuple-element.31.refs_2_, bf16[512,512]{1,0:T(8,128)(2,1)S(1)} %copy-done.21, bf16[512,512]{1,0:T(8,128)(2,1)} %collective-permute-done.5.refs_4_, ...), custom_call_target="tpu_custom_call" | custom-call | flops 3221225472 | bytes 6291456 | tf_op jit(solution)/shard_map/pallas_call | solution.py:382
  149.4 4.2 %all-to-all-done.3.refs_4_ = bf16[16,144,768]{2,1,0:T(8,128)(2,1)S(1)} async-done(((bf16[16,144,768]{2,1,0:T(8,128)(2,1)}), bf16[16,144,768]{2,1,0:T(8,128)(2,1)S(1)}, u32[]{:S(2)}, u32[]{:S(2)}) %all-to-all-start.3) | async-done | bytes 3538976 | tf_op jit(solution)/shard_map/all_to_all | solution.py:468
  155.8 1.6 copy-done.18
  157.4 2.3 %shard_map.130 = (bf16[512,1024]{1,0:T(8,128)(2,1)}, bf16[512,1024]{1,0:T(8,128)(2,1)}) custom-call(bf16[512,1024]{1,0:T(8,128)(2,1)S(1)} %copy-done.4, bf16[512,1024]{1,0:T(8,128)(2,1)S(1)} %copy-done.7, f32[512,1024]{1,0:T(8,128)S(1)} %copy-done.16, f32[512,1024]{1,0:T(8,128)S(1)} %copy-done.18, bf16[16,144,768]{2,1,0:T(8,128)(2,1)S(1)} %all-to-all-done.3.refs_4_), custom_call_target="tpu_custom_call" | custom-call | flops 268435456 | bytes 8388608 | tf_op jit(solution)/shard_map/pallas_call | solution.py:350
  (84 shorter events, 7.4 us)
Async XLA Ops:
  0.7 2.8 %copy-start = (bf16[4096,768]{1,0:T(8,128)(2,1)S(1)}, bf16[4096,768]{1,0:T(8,128)(2,1)}, u32[]{:S(2)}) copy-start(bf16[4096,768]{1,0:T(8,128)(2,1)} %refs_9_.1) | copy-start | bytes 18874372
  3.5 6.5 %copy-start.2 = (bf16[512,1024]{1,0:T(8,128)(2,1)S(1)}, bf16[512,1024]{1,0:T(8,128)(2,1)}, u32[]{:S(2)}) copy-start(bf16[512,1024]{1,0:T(8,128)(2,1)} %refs_0_.3) | copy-start | bytes 3145732
  3.5 6.5 %copy-start.5 = (bf16[512,1024]{1,0:T(8,128)(2,1)S(1)}, bf16[512,1024]{1,0:T(8,128)(2,1)}, u32[]{:S(2)}) copy-start(bf16[512,1024]{1,0:T(8,128)(2,1)} %refs_1_.4) | copy-start | bytes 3145732
  8.3 11.2 %collective-permute-start = (bf16[2,512,1024]{2,1,0:T(8,128)(2,1)}, bf16[2,512,1024]{2,1,0:T(8,128)(2,1)}, u32[]{:S(2)}, u32[]{:S(2)}) collective-permute-start(bf16[2,512,1024]{2,1,0:T(8,128)(2,1)} %shard_map.118), channel_id=1, source_target_pairs={{0,1},{1,0},{2,3},{3,2},{4,5},{5,4},{6,7},{7,6},{8,9},{9,8},{10,11... | collective-permute-start | bytes 6291464 | tf_op jit(solution)/shard_map/ppermute | solution.py:459
  8.3 23.7 %collective-permute-start.2 = (bf16[512,768]{1,0:T(8,128)(2,1)}, bf16[512,768]{1,0:T(8,128)(2,1)S(1)}, u32[]{:S(2)}, u32[]{:S(2)}) collective-permute-start(bf16[512,768]{1,0:T(8,128)(2,1)} %refs_5_.3), channel_id=1, source_target_pairs={{0,64},{4,68},{8,72},{12,76},{16,80},{20,84},{24,88},{28,92},{32,9... | collective-permute-start | bytes 2359304 | tf_op jit(solution)/shard_map/ppermute | solution.py:465
  11.7 19.8 %all-to-all-start = ((f32[16,64,128]{2,1,0:T(8,128)}), f32[16,64,128]{2,1,0:T(8,128)S(1)}, u32[]{:S(2)}, u32[]{:S(2)}) async-start(f32[16,64,128]{2,1,0:T(8,128)} %bitcast.17), calls=%async_computation | async-start | bytes 1048576 | tf_op jit(solution)/shard_map/all_to_all | solution.py:468
  19.6 2.8 %copy-start.1 = (bf16[4096,768]{1,0:T(8,128)(2,1)S(1)}, bf16[4096,768]{1,0:T(8,128)(2,1)}, u32[]{:S(2)}) copy-start(bf16[4096,768]{1,0:T(8,128)(2,1)} %refs_9_.1) | copy-start | bytes 18874372
  31.5 4.0 %collective-permute-start.1 = (f32[64,128]{1,0:T(8,128)S(1)}, f32[64,128]{1,0:T(8,128)S(1)}, u32[]{:S(2)}, u32[]{:S(2)}) collective-permute-start(f32[64,128]{1,0:T(8,128)S(1)} %reduce_sum.36), channel_id=1, source_target_pairs={{0,64},{4,68},{8,72},{12,76},{16,80},{20,84},{24,88},{28,92},{32,9... | collective-permute-start | bytes 98312 | tf_op jit(solution)/shard_map/ppermute | solution.py:465
  32.0 10.9 %copy-start.13 = (bf16[512,768]{1,0:T(8,128)(2,1)}, bf16[512,768]{1,0:T(8,128)(2,1)S(1)}, u32[]{:S(2)}) copy-start(bf16[512,768]{1,0:T(8,128)(2,1)S(1)} %collective-permute-done.2.refs_6_) | copy-start | bytes 2359300
  35.5 26.9 %collective-permute-start.3 = (bf16[512,1024]{1,0:T(8,128)(2,1)}, bf16[512,1024]{1,0:T(8,128)(2,1)}, u32[]{:S(2)}, u32[]{:S(2)}) collective-permute-start(bf16[512,1024]{1,0:T(8,128)(2,1)} %bitcast.19), channel_id=1, source_target_pairs={{0,2},{1,3},{2,0},{3,1},{4,6},{5,7},{6,4},{7,5},{8,10},{9,11},{10,... | collective-permute-start | bytes 3145736 | tf_op jit(solution)/shard_map/ppermute | solution.py:462
  39.3 12.0 %all-to-all-start.1 = ((bf16[16,64,128]{2,1,0:T(8,128)(2,1)}), bf16[16,64,128]{2,1,0:T(8,128)(2,1)S(1)}, u32[]{:S(2)}, u32[]{:S(2)}) async-start(bf16[16,64,128]{2,1,0:T(8,128)(2,1)} %copy-done.28), calls=%async_computation.1 | async-start | bytes 524288 | tf_op jit(solution)/shard_map/all_to_all | solution.py:468
  42.9 8.4 %copy-start.10 = (bf16[512,1024]{1,0:T(8,128)(2,1)S(1)}, bf16[512,1024]{1,0:T(8,128)(2,1)}, u32[]{:S(2)}) copy-start(bf16[512,1024]{1,0:T(8,128)(2,1)} %g_ref.1) | copy-start | bytes 3145732
  42.9 8.4 %copy-start.31 = (f32[1024]{0:T(1024)S(1)}, f32[1024]{0:T(1024)}, u32[]{:S(2)}) copy-start(f32[1024]{0:T(1024)} %param.11) | copy-start | bytes 12292
  46.0 1.3 copy-start.8
  51.3 15.2 %copy-start.29 = (bf16[16,64,128]{2,1,0:T(8,128)(2,1)}, bf16[16,64,128]{2,1,0:T(8,128)(2,1)S(1)}, u32[]{:S(2)}) copy-start(bf16[16,64,128]{2,1,0:T(8,128)(2,1)S(1)} %all-to-all-done.1) | copy-start | bytes 786436
  51.3 11.0 %copy-start.9 = (f32[1,512,1024]{2,1,0:T(8,128)S(1)}, f32[1,512,1024]{2,1,0:T(8,128)}, u32[]{:S(2)}) copy-start(f32[1,512,1024]{2,1,0:T(8,128)} %copy-done.8) | copy-start | bytes 6291460
  51.3 1.4 copy-start.11
  57.3 16.3 %collective-permute-start.13 = (bf16[512,512]{1,0:T(8,128)(2,1)}, bf16[512,512]{1,0:T(8,128)(2,1)}, u32[]{:S(2)}, u32[]{:S(2)}) collective-permute-start(bf16[512,512]{1,0:T(8,128)(2,1)} %get-tuple-element.31.refs_2_), channel_id=1, source_target_pairs={{0,64},{4,68},{8,72},{12,76},{16,80},{20,84},{24,88},{28,92},{32,9... | collective-permute-start | bytes 1572872 | tf_op jit(solution)/shard_map/ppermute | solution.py:465
  57.3 25.4 %collective-permute-start.11 = (bf16[512,512]{1,0:T(8,128)(2,1)}, bf16[512,512]{1,0:T(8,128)(2,1)}, u32[]{:S(2)}, u32[]{:S(2)}) collective-permute-start(bf16[512,512]{1,0:T(8,128)(2,1)} %get-tuple-element.31.refs_2_), channel_id=1, source_target_pairs={{0,66},{1,67},{2,64},{3,65},{4,70},{5,71},{6,68},{7,69},{8,74},{9,... | collective-permute-start | bytes 1572872 | tf_op jit(solution)/shard_map/ppermute | solution.py:517
  58.2 24.4 %collective-permute-start.6 = (bf16[512,512]{1,0:T(8,128)(2,1)}, bf16[512,512]{1,0:T(8,128)(2,1)}, u32[]{:S(2)}, u32[]{:S(2)}) collective-permute-start(bf16[512,512]{1,0:T(8,128)(2,1)} %get-tuple-element.35.refs_1_), channel_id=1, source_target_pairs={{0,2},{1,3},{2,0},{3,1},{4,6},{5,7},{6,4},{7,5},{8,10},{9,11},{10,... | collective-permute-start | bytes 1572872 | tf_op jit(solution)/shard_map/ppermute | solution.py:462
  62.3 30.0 %copy-start.14 = (bf16[512,768]{1,0:T(8,128)(2,1)S(1)}, bf16[512,768]{1,0:T(8,128)(2,1)}, u32[]{:S(2)}) copy-start(bf16[512,768]{1,0:T(8,128)(2,1)} %copy-done.13) | copy-start | bytes 2359300
  73.6 18.8 %collective-permute-start.14 = (bf16[512,512]{1,0:T(8,128)(2,1)}, bf16[512,512]{1,0:T(8,128)(2,1)S(1)}, u32[]{:S(2)}, u32[]{:S(2)}) collective-permute-start(bf16[512,512]{1,0:T(8,128)(2,1)} %collective-permute-done.13.refs_2_), channel_id=1, source_target_pairs={{0,1},{1,0},{2,3},{3,2},{4,5},{5,4},{6,7},{7,6},{8,9},{9,8},{10,11... | collective-permute-start | bytes 1572872 | tf_op jit(solution)/shard_map/ppermute | solution.py:459
  73.6 18.8 %collective-permute-start.4 = (bf16[512,512]{1,0:T(8,128)(2,1)}, bf16[512,512]{1,0:T(8,128)(2,1)S(1)}, u32[]{:S(2)}, u32[]{:S(2)}) collective-permute-start(bf16[512,512]{1,0:T(8,128)(2,1)} %get-tuple-element.35.refs_1_), channel_id=1, source_target_pairs={{0,1},{1,0},{2,3},{3,2},{4,5},{5,4},{6,7},{7,6},{8,9},{9,8},{10,11... | collective-permute-start | bytes 1572872 | tf_op jit(solution)/shard_map/ppermute | solution.py:459
  74.1 15.7 %all-to-all-start.2 = ((f32[16,64,128]{2,1,0:T(8,128)}), f32[16,64,128]{2,1,0:T(8,128)S(1)}, u32[]{:S(2)}, u32[]{:S(2)}) async-start(f32[16,64,128]{2,1,0:T(8,128)} %bitcast.18), calls=%async_computation.2 | async-start | bytes 1048576 | tf_op jit(solution)/shard_map/all_to_all | solution.py:468
  82.7 15.4 %collective-permute-start.12 = (bf16[512,512]{1,0:T(8,128)(2,1)}, bf16[512,512]{1,0:T(8,128)(2,1)S(1)}, u32[]{:S(2)}, u32[]{:S(2)}) collective-permute-start(bf16[512,512]{1,0:T(8,128)(2,1)} %collective-permute-done.11.refs_2_), channel_id=1, source_target_pairs={{0,1},{1,0},{2,3},{3,2},{4,5},{5,4},{6,7},{7,6},{8,9},{9,8},{10,11... | collective-permute-start | bytes 1572872 | tf_op jit(solution)/shard_map/ppermute | solution.py:459
  82.7 15.4 %collective-permute-start.8 = (bf16[512,512]{1,0:T(8,128)(2,1)}, bf16[512,512]{1,0:T(8,128)(2,1)S(1)}, u32[]{:S(2)}, u32[]{:S(2)}) collective-permute-start(bf16[512,512]{1,0:T(8,128)(2,1)} %collective-permute-done.6.refs_1_.refs_5_), channel_id=1, source_target_pairs={{0,1},{1,0},{2,3},{3,2},{4,5},{5,4},{6,7},{7,6},{8,9},{9,8},{10,11... | collective-permute-start | bytes 1572872 | tf_op jit(solution)/shard_map/ppermute | solution.py:459
  89.8 12.9 %collective-permute-start.10 = (f32[64,128]{1,0:T(8,128)S(1)}, f32[64,128]{1,0:T(8,128)S(1)}, u32[]{:S(2)}, u32[]{:S(2)}) collective-permute-start(f32[64,128]{1,0:T(8,128)S(1)} %reduce_sum.37), channel_id=1, source_target_pairs={{0,64},{4,68},{8,72},{12,76},{16,80},{20,84},{24,88},{28,92},{32,9... | collective-permute-start | bytes 98312 | tf_op jit(solution)/shard_map/ppermute | solution.py:465
  92.3 5.7 %copy-start.20 = (bf16[512,512]{1,0:T(8,128)(2,1)}, bf16[512,512]{1,0:T(8,128)(2,1)S(1)}, u32[]{:S(2)}) copy-start(bf16[512,512]{1,0:T(8,128)(2,1)S(1)} %collective-permute-done.4.refs_3_) | copy-start | bytes 1572868
  92.3 1.2 copy-start.25
  98.0 4.6 %copy-start.22 = (bf16[512,512]{1,0:T(8,128)(2,1)}, bf16[512,512]{1,0:T(8,128)(2,1)S(1)}, u32[]{:S(2)}) copy-start(bf16[512,512]{1,0:T(8,128)(2,1)S(1)} %collective-permute-done.8.refs_3_.refs_7_) | copy-start | bytes 1572868
  103.5 50.1 %all-to-all-start.3 = ((bf16[16,144,768]{2,1,0:T(8,128)(2,1)}), bf16[16,144,768]{2,1,0:T(8,128)(2,1)S(1)}, u32[]{:S(2)}, u32[]{:S(2)}) async-start(bf16[16,144,768]{2,1,0:T(8,128)(2,1)} %shard_map.127.refs_6_), calls=%async_computation.3 | async-start | bytes 7077888 | tf_op jit(solution)/shard_map/all_to_all | solution.py:468
  107.3 14.0 %collective-permute-start.7 = (bf16[512,512]{1,0:T(8,128)(2,1)}, bf16[512,512]{1,0:T(8,128)(2,1)}, u32[]{:S(2)}, u32[]{:S(2)}) collective-permute-start(bf16[512,512]{1,0:T(8,128)(2,1)} %get-tuple-element.31.refs_2_), channel_id=1, source_target_pairs={{0,2},{1,3},{2,0},{3,1},{4,6},{5,7},{6,4},{7,5},{8,10},{9,11},{10,... | collective-permute-start | bytes 1572872 | tf_op jit(solution)/shard_map/ppermute | solution.py:462
  107.4 32.8 %collective-permute-start.5 = (bf16[512,512]{1,0:T(8,128)(2,1)}, bf16[512,512]{1,0:T(8,128)(2,1)}, u32[]{:S(2)}, u32[]{:S(2)}) collective-permute-start(bf16[512,512]{1,0:T(8,128)(2,1)} %get-tuple-element.31.refs_2_), channel_id=1, source_target_pairs={{0,1},{1,0},{2,3},{3,2},{4,5},{5,4},{6,7},{7,6},{8,9},{9,8},{10,11... | collective-permute-start | bytes 1572872 | tf_op jit(solution)/shard_map/ppermute | solution.py:459
  121.3 18.9 %collective-permute-start.9 = (bf16[512,512]{1,0:T(8,128)(2,1)}, bf16[512,512]{1,0:T(8,128)(2,1)}, u32[]{:S(2)}, u32[]{:S(2)}) collective-permute-start(bf16[512,512]{1,0:T(8,128)(2,1)} %collective-permute-done.7.refs_6_), channel_id=1, source_target_pairs={{0,1},{1,0},{2,3},{3,2},{4,5},{5,4},{6,7},{7,6},{8,9},{9,8},{10,11... | collective-permute-start | bytes 1572872 | tf_op jit(solution)/shard_map/ppermute | solution.py:459
  121.4 1.2 copy-start.3
  122.6 1.2 copy-start.6
  123.9 1.2 copy-start.12
  126.0 1.2 copy-start.33
  128.5 11.7 %copy-start.21 = (bf16[512,512]{1,0:T(8,128)(2,1)S(1)}, bf16[512,512]{1,0:T(8,128)(2,1)}, u32[]{:S(2)}) copy-start(bf16[512,512]{1,0:T(8,128)(2,1)} %copy-done.20) | copy-start | bytes 1572868
  128.5 11.7 %copy-start.23 = (bf16[512,512]{1,0:T(8,128)(2,1)S(1)}, bf16[512,512]{1,0:T(8,128)(2,1)}, u32[]{:S(2)}) copy-start(bf16[512,512]{1,0:T(8,128)(2,1)} %copy-done.22) | copy-start | bytes 1572868
  137.5 1.3 copy-start.15
  138.9 1.3 copy-start.17
  140.2 1.2 copy-start.27
  153.6 1.2 copy-start.4
  153.6 1.5 copy-start.7
  153.6 2.2 %copy-start.16 = (f32[512,1024]{1,0:T(8,128)S(1)}, f32[512,1024]{1,0:T(8,128)}, u32[]{:S(2)}) copy-start(f32[512,1024]{1,0:T(8,128)} %copy-done.15) | copy-start | bytes 6291460
  154.1 5.7 %collective-permute-start.15 = (f32[64,768]{1,0:T(8,128)S(1)}, f32[64,768]{1,0:T(8,128)S(1)}, u32[]{:S(2)}, u32[]{:S(2)}) collective-permute-start(f32[64,768]{1,0:T(8,128)S(1)} %get-tuple-element.49), channel_id=1, source_target_pairs={{0,64},{4,68},{8,72},{12,76},{16,80},{20,84},{24,88},{28,92},{32,9... | collective-permute-start | bytes 589832 | tf_op jit(solution)/shard_map/ppermute | solution.py:465
  155.8 1.6 copy-start.18
  (8 other events, 7.4 us)
